TPU v7x, 32 devices: a whole 2x2x4 slice. The times are simulated.
32 devices in a mesh: groups: 2 (over x), clus: 16 (over z, y, core).
Axes of the slice: x: 2, y: 2, z: 4, core: 2. Of those that a mesh axis runs over, the one named last changes fastest.
Arguments:
- tokens: bfloat16 [10240, 4096], P(('groups', 'clus')), parts along dimension 0, may hold values from -6 to 6
- proj_weight: bfloat16 [4096, 1024], replicated, may hold values from -0.09375 to 0.09375
- labels: int32 [10240, 1], P(('groups', 'clus')), parts along dimension 0, may hold values from 0 to 15; in each aligned block of 320 rows (0 to 319, 320 to 639, ...) at most 40 rows name the same one
- valid_rows: int32 [10240], P(('groups', 'clus')), parts along dimension 0, may hold values 0 or 1
Outputs:
- similar: float32 [32, 640, 640], P(('groups', 'clus')), parts along dimension 0
- nearest: float32 [10240], P(('groups', 'clus')), parts along dimension 0
- centre_dist: float32 [10240], P(('groups', 'clus')), parts along dimension 0
There are 2 independent parts, one for each index of `groups`. A program takes and returns all parts, laid end to end along the dimension named above; an argument that names none is the same for every part. Nothing has to cross between parts.
Inputs may be any that keep to these rules, and one draw needn't show every extreme that they name: `labels`: within each device's block of 320 rows no cluster is named by more than 40 rows, and some cluster reaches 40 in some block; every cluster is named somewhere.
All inputs are finite; a program needn't handle non-finite values. No bound on the sum of `valid_rows` on one device may be relied on, other than what follows from the above.
Results may differ from a plain program's by a relative error of at most 0.002.
Values may be sent and summed in bfloat16 or wider, within the bound.
No kernel may reach another device: no remote copies, remote signals or barrier semaphores. Data moves between devices by JAX's collectives and lax.ppermute only.
A program may use at most 64 MiB of HBM per device.

v0:
```python
import jax
import jax.numpy as jnp
from jax import lax
from jax.sharding import PartitionSpec as P


def per_device(tokens, proj_weight, labels, valid_rows):
    row_count = tokens.shape[0]
    embed_width = proj_weight.shape[1]
    owners = lax.axis_size("clus")
    slot_count = 2 * row_count // owners
    embed = jnp.dot(tokens, proj_weight, preferred_element_type=jnp.float32)
    mask_float = valid_rows.astype(jnp.float32)
    scale = lax.rsqrt(jnp.sum(embed * embed, axis=1) + 1e-06)
    unit = (embed * (scale * mask_float)[:, None]).astype(jnp.bfloat16)
    label_flat = labels[:, 0]
    onehot = (label_flat[:, None] == jnp.arange(owners, dtype=jnp.int32)[None, :]).astype(jnp.int32)
    rank_inside = jnp.sum((jnp.cumsum(onehot, axis=0) - 1) * onehot, axis=1)
    slot_index = label_flat * slot_count + rank_inside
    packed = jnp.zeros((owners * slot_count, embed_width), jnp.bfloat16).at[slot_index].set(unit)
    packed = packed.reshape(owners, slot_count, embed_width)
    arrived = lax.all_to_all(packed, "clus", split_axis=0, concat_axis=0, tiled=True)
    width_all = owners * slot_count
    members = arrived.reshape(width_all, embed_width)
    ones_row = jnp.ones((1, width_all), jnp.bfloat16)
    centroid_sum = jnp.dot(ones_row, members, preferred_element_type=jnp.float32)[0]
    centroid_unit = centroid_sum * lax.rsqrt(jnp.sum(centroid_sum * centroid_sum) + 1e-06)
    gram_tile = lax.dot_general(
        members, members, (((1,), (1,)), ((), ())), preferred_element_type=jnp.float32
    )
    itself = jnp.eye(width_all, dtype=jnp.bool_)
    slot_near = jnp.max(jnp.where(itself, 0.0, gram_tile), axis=1)
    slot_dist = 1.0 - jnp.sum(members * centroid_unit[None, :], axis=1)
    returned = (
        lax.all_to_all(
            slot_near.reshape(owners, slot_count), "clus", split_axis=0, concat_axis=0, tiled=True
        ),
        lax.all_to_all(
            slot_dist.reshape(owners, slot_count), "clus", split_axis=0, concat_axis=0, tiled=True
        ),
    )
    nearest = jnp.take(returned[0].reshape(width_all), slot_index) * mask_float
    centre_dist = jnp.take(returned[1].reshape(width_all), slot_index) * mask_float
    return (gram_tile[None], nearest, centre_dist)


def solution(mesh):
    return jax.shard_map(
        per_device,
        mesh=mesh,
        in_specs=(
            P(("groups", "clus"), None),
            P(),
            P(("groups", "clus"), None),
            P(("groups", "clus")),
        ),
        out_specs=(P(("groups", "clus"), None, None), P(("groups", "clus")), P(("groups", "clus"))),
        check_vma=False,
    )
```

profile of v0, /device:TPU:0, one launch (start us, length us, event | category | flops | bytes accessed | tf_op | source)
XLA Modules:
  0.0 85.7 jit_solution(11497426760403779747)
XLA Ops:
  0.6 0.0 copy-start
  0.6 0.9 reduce.1
  1.5 0.9 %reduce-window.6 = s32[16,3,128]{2,0,1:T(8,128)S(1)} reduce-window(s32[16,3,128]{2,0,1:T(8,128)S(1)} %copy_bitcast_fusion, s32[]{:T(128)} %constant.8.clone.1), window={size=1x1x128 pad=0_0x0_0x127_0}, to_apply=%region_0.0 | reduce-window | flops 780288 | bytes 49156 | tf_op jit(solution)/shard_map/reduce-window
  2.4 0.2 slice_reduce_fusion
  2.6 0.1 bitcast_bitcast_fusion
  2.8 0.7 fusion.5
  3.5 0.0 copy-done
  3.5 0.0 copy-start.1
  3.5 7.3 %multiply_reduce_fusion.1 = (f32[320]{0:T(512)S(1)}, f32[320,1024]{1,0:T(8,128)}) fusion(bf16[320,4096]{1,0:T(8,128)(2,1)S(1)} %copy-done, bf16[4096,1024]{1,0:T(8,128)(2,1)} %param.7), kind=kOutput, calls=%fused_computation.7 | convolution fusion | flops 2685009664 | bytes 12322048 | tf_op jit(solution)/shard_map/dot_general | solution.py:12
  10.8 0.0 copy-done.1
  10.8 3.9 %scatter_custom_fusion = bf16[640,1024]{1,0:T(8,128)(2,1)} fusion(s32[320]{0:T(512)S(1)} %fusion.5, f32[320,1024]{1,0:T(8,128)} %get-tuple-element.19, f32[320]{0:T(512)S(1)} %convert_multiply_fusion, bf16[]{:T(256)} %constant.19.clone.1), kind=kCustom, calls=%fused_computation.8 | custom fusion | flops 655360 | bytes 2623490 | tf_op jit(solution)/shard_map/scatter | solution.py:20
  14.7 7.4 %all-to-all-start = ((bf16[16,40,1024]{2,1,0:T(8,128)(2,1)}), bf16[16,40,1024]{2,1,0:T(8,128)(2,1)}, u32[]{:S(2)}, u32[]{:S(2)}) async-start(bf16[16,40,1024]{2,1,0:T(8,128)(2,1)} %bitcast.25), calls=%async_computation | async-start | bytes 2621440 | tf_op jit(solution)/shard_map/all_to_all | solution.py:22
  22.1 27.4 %all-to-all-done = bf16[16,40,1024]{2,1,0:T(8,128)(2,1)} async-done(((bf16[16,40,1024]{2,1,0:T(8,128)(2,1)}), bf16[16,40,1024]{2,1,0:T(8,128)(2,1)}, u32[]{:S(2)}, u32[]{:S(2)}) %all-to-all-start) | async-done | bytes 1310752 | tf_op jit(solution)/shard_map/all_to_all | solution.py:22
  49.6 1.6 %fusion.6 = f32[1,1024]{1,0:T(1,128)S(1)} fusion(bf16[640,1024]{1,0:T(8,128)(2,1)} %bitcast.2), kind=kOutput, calls=%fused_computation.32 | convolution fusion | flops 1310720 | bytes 1314816 | tf_op jit(solution)/shard_map/dot_general | solution.py:26
  51.2 0.6 multiply_reduce_fusion.2
  52.5 1.6 %multiply_reduce_fusion = f32[16,40]{1,0:T(8,128)S(1)} fusion(bf16[16,40,1024]{2,1,0:T(8,128)(2,1)} %all-to-all-done, f32[1024]{0:T(1024)S(1)} %broadcast_multiply_fusion), kind=kLoop, calls=%fused_computation.3 | loop fusion | flops 1965440 | bytes 1317376 | tf_op jit(solution)/shard_map/reduce_sum | solution.py:33
  54.1 0.6 broadcast_subtract_fusion
  54.7 8.0 %all-to-all-start.2 = ((f32[16,1,40]{2,1,0:T(1,128)}), f32[16,1,40]{2,1,0:T(1,128)S(1)}, u32[]{:S(2)}, u32[]{:S(2)}) async-start(f32[16,1,40]{2,1,0:T(1,128)} %bitcast.6), calls=%async_computation.2 | async-start | bytes 16384 | tf_op jit(solution)/shard_map/all_to_all | solution.py:38
  62.7 4.1 %select_reduce_fusion = (f32[640]{0:T(1024)S(1)}, f32[640,640]{0,1:T(8,128)}) fusion(bf16[640,1024]{1,0:T(8,128)(2,1)} %bitcast.2), kind=kOutput, calls=%fused_computation.4 | convolution fusion | flops 840088960 | bytes 2951680 | tf_op jit(solution)/shard_map/dot_general | solution.py:28
  66.9 0.7 all_to_all.14
  67.6 2.7 %copy.17 = f32[1,640,640]{2,1,0:T(8,128)} copy(f32[1,640,640]{1,2,0:T(8,128)} %bitcast.26) | data formatting | bytes 3276800
  70.3 0.0 all-to-all-done.2
  70.3 6.0 %all-to-all-start.1 = ((f32[16,1,40]{2,1,0:T(1,128)}), f32[16,1,40]{2,1,0:T(1,128)S(1)}, u32[]{:S(2)}, u32[]{:S(2)}) async-start(f32[16,1,40]{2,1,0:T(1,128)} %all_to_all.14), calls=%async_computation.1 | async-start | bytes 16384 | tf_op jit(solution)/shard_map/all_to_all | solution.py:35
  76.3 0.5 broadcast.64
  76.8 0.7 reduce.13
  77.5 0.1 reshape.71
  77.6 1.7 %gather_fusion.1 = f32[320]{0:T(512)S(1)} fusion(f32[640]{0:T(1024)S(1)} %reshape.71, s32[1024]{0:T(1024)S(1)} %pad_clamp_fusion), kind=kCustom, calls=%fused_computation.1.clone | custom fusion | bytes 3840 | tf_op jit(solution)/shard_map/jit(_take)/gather | solution.py:43
  79.3 0.6 select_multiply_fusion
  79.9 2.8 %all-to-all-done.1 = f32[16,1,40]{2,1,0:T(1,128)S(1)} async-done(((f32[16,1,40]{2,1,0:T(1,128)}), f32[16,1,40]{2,1,0:T(1,128)S(1)}, u32[]{:S(2)}, u32[]{:S(2)}) %all-to-all-start.1) | async-done | bytes 2592 | tf_op jit(solution)/shard_map/all_to_all | solution.py:35
  82.7 0.7 reduce.12
  83.4 0.1 reshape.70
  83.5 1.7 %gather_fusion = f32[320]{0:T(512)S(1)} fusion(f32[640]{0:T(1024)S(1)} %reshape.70, s32[1024]{0:T(1024)S(1)} %pad_clamp_fusion), kind=kCustom, calls=%fused_computation.clone | custom fusion | bytes 3840 | tf_op jit(solution)/shard_map/jit(_take)/gather | solution.py:42
  85.2 0.6 select_multiply_fusion.1
  (8 shorter events, 0.1 us)
Async XLA Ops:
  0.6 2.8 %copy-start = (bf16[320,4096]{1,0:T(8,128)(2,1)S(1)}, bf16[320,4096]{1,0:T(8,128)(2,1)}, u32[]{:S(2)}) copy-start(bf16[320,4096]{1,0:T(8,128)(2,1)} %param.6) | copy-start | bytes 7864324
  3.5 7.3 %copy-start.1 = (s32[320]{0:T(512)S(1)}, s32[320]{0:T(512)}, u32[]{:S(2)}) copy-start(s32[320]{0:T(512)} %param.9) | copy-start | bytes 3844
  14.7 34.9 %all-to-all-start = ((bf16[16,40,1024]{2,1,0:T(8,128)(2,1)}), bf16[16,40,1024]{2,1,0:T(8,128)(2,1)}, u32[]{:S(2)}, u32[]{:S(2)}) async-start(bf16[16,40,1024]{2,1,0:T(8,128)(2,1)} %bitcast.25), calls=%async_computation | async-start | bytes 2621440 | tf_op jit(solution)/shard_map/all_to_all | solution.py:22
  54.7 15.6 %all-to-all-start.2 = ((f32[16,1,40]{2,1,0:T(1,128)}), f32[16,1,40]{2,1,0:T(1,128)S(1)}, u32[]{:S(2)}, u32[]{:S(2)}) async-start(f32[16,1,40]{2,1,0:T(1,128)} %bitcast.6), calls=%async_computation.2 | async-start | bytes 16384 | tf_op jit(solution)/shard_map/all_to_all | solution.py:38
  70.3 12.4 %all-to-all-start.1 = ((f32[16,1,40]{2,1,0:T(1,128)}), f32[16,1,40]{2,1,0:T(1,128)S(1)}, u32[]{:S(2)}, u32[]{:S(2)}) async-start(f32[16,1,40]{2,1,0:T(1,128)} %all_to_all.14), calls=%async_computation.1 | async-start | bytes 16384 | tf_op jit(solution)/shard_map/all_to_all | solution.py:35
where the time goes:
time: 86.3 us; the launch traced here: 85.7 us
  waiting for transfers between devices  30.3 us (35%)
  starting transfers between devices  21.4 us (25%)
  matrix products  13 us (15%)
  other arithmetic  11.8 us (14%)
  local copies, waits for them, and re-layouts  7.68 us (9%)
  between operations  1.45 us (2%)
    all_to_all x1, waiting for transfers between devices, per_device(): lax.all_to_all(packed, 'clus', split_axis=0, concat_axis=0, tiled=True)  27.4 us
    all_to_all x1, starting transfers between devices, per_device(): lax.all_to_all(slot_dist.reshape(owners, slot_count), 'clus', split_axis=...  8.01 us
    all_to_all x1, starting transfers between devices, per_device(): lax.all_to_all(packed, 'clus', split_axis=0, concat_axis=0, tiled=True)  7.43 us
    dot_general x1, matrix products, per_device(): embed = jnp.dot(tokens, proj_weight, preferred_element_type=jnp.float32)  7.31 us
    all_to_all x1, starting transfers between devices, per_device(): lax.all_to_all(slot_near.reshape(owners, slot_count), 'clus', split_axis=...  6.01 us
    dot_general x1, matrix products, per_device(): lax.dot_general(members, members, (((1,), (1,)), ((), ())), preferred_ele...  4.13 us
    scatter x1, other arithmetic, per_device(): jnp.zeros((owners * slot_count, embed_width), jnp.bfloat16).at[slot_index]  3.86 us
    all_to_all x1, waiting for transfers between devices, per_device(): lax.all_to_all(slot_near.reshape(owners, slot_count), 'clus', split_axis=...  2.84 us
  transfers between devices with their start and end apart: 3, of which 2 were waited for; matrix products, arithmetic and copies ran while one was open for 12% of the time, Pallas kernels for 0%

commit v1 on v0

v1 whole, which is shorter than its diff:
```python
import functools

import jax
import jax.numpy as jnp
from jax import lax
from jax.experimental import pallas as pl
from jax.experimental.pallas import tpu as pltpu
from jax.sharding import PartitionSpec as P

F32 = jnp.float32
BF16 = jnp.bfloat16
VMEM_BYTES = 48 * 1024 * 1024


def split3(x):
    hi = x.astype(BF16)
    rest = x - hi.astype(F32)
    mid = rest.astype(BF16)
    low = (rest - mid.astype(F32)).astype(BF16)
    return hi, mid, low


def embed_kernel(slot_count, steps, tokens_ref, weight_ref, label_ref, valid_ref, packed_ref, rank_ref, total, place):
    step = pl.program_id(0)
    rows = total.shape[0]
    width_all = place.shape[0]
    part = jnp.dot(tokens_ref[...], weight_ref[...], preferred_element_type=F32)

    @pl.when(step == 0)
    def _():
        total[...] = part
        label_row = label_ref[...].astype(F32)
        below = lax.broadcasted_iota(jnp.int32, (rows, rows), 0)
        across = lax.broadcasted_iota(jnp.int32, (rows, rows), 1)
        label_col = jnp.sum(jnp.where(below == across, label_row, 0.0), axis=1, keepdims=True)
        earlier = (label_col == label_row) & (below < across)
        rank = jnp.sum(jnp.where(earlier, 1.0, 0.0), axis=0, keepdims=True).astype(jnp.int32)
        rank_ref[...] = rank
        slot = label_ref[...] * slot_count + rank
        slot = jnp.where(valid_ref[...] > 0, slot, -1)
        slots = lax.broadcasted_iota(jnp.int32, (width_all, rows), 0)
        place[...] = jnp.where(slots == slot, 1.0, 0.0).astype(BF16)

    @pl.when(step > 0)
    def _():
        total[...] += part

    @pl.when(step == steps - 1)
    def _():
        embed = total[...]
        scale = lax.rsqrt(jnp.sum(embed * embed, axis=1, keepdims=True) + 1e-06)
        unit = (embed * scale).astype(BF16)
        packed_ref[...] = jnp.dot(place[...], unit, preferred_element_type=F32).astype(BF16)


def embed_and_pack(tokens, weight, label_row, valid_row, owners, slot_count):
    rows, depth = tokens.shape
    width = weight.shape[1]
    steps = 8 if depth % 1024 == 0 else 1
    block = depth // steps
    width_all = owners * slot_count
    return pl.pallas_call(
        functools.partial(embed_kernel, slot_count, steps),
        grid=(steps,),
        in_specs=[
            pl.BlockSpec((rows, block), lambda k: (0, k)),
            pl.BlockSpec((block, width), lambda k: (k, 0)),
            pl.BlockSpec((1, rows), lambda k: (0, 0)),
            pl.BlockSpec((1, rows), lambda k: (0, 0)),
        ],
        out_specs=(
            pl.BlockSpec((width_all, width), lambda k: (0, 0)),
            pl.BlockSpec((1, rows), lambda k: (0, 0)),
        ),
        out_shape=(
            jax.ShapeDtypeStruct((width_all, width), BF16),
            jax.ShapeDtypeStruct((1, rows), jnp.int32),
        ),
        scratch_shapes=[pltpu.VMEM((rows, width), F32), pltpu.VMEM((width_all, rows), BF16)],
        compiler_params=pltpu.CompilerParams(vmem_limit_bytes=VMEM_BYTES),
        cost_estimate=pl.CostEstimate(
            flops=2 * rows * depth * width, bytes_accessed=2 * depth * width + 2 * rows * depth, transcendentals=0
        ),
    )(tokens, weight, label_row, valid_row)


def score_kernel(slot_count, half, members_ref, message_ref, near_col, sum_col):
    width_all = members_ref.shape[0]
    owners, lanes = message_ref.shape
    block = 128
    for b in range(width_all // block):
        gram = lax.dot_general(
            members_ref[b * block:(b + 1) * block, :], members_ref[...], (((1,), (1,)), ((), ())), preferred_element_type=F32
        )
        own = lax.broadcasted_iota(jnp.int32, (block, width_all), 0) + b * block
        other = lax.broadcasted_iota(jnp.int32, (block, width_all), 1)
        near_col[b * block:(b + 1) * block, :] = jnp.max(jnp.where(own == other, 0.0, gram), axis=1, keepdims=True)
        sum_col[b * block:(b + 1) * block, :] = jnp.sum(gram, axis=1, keepdims=True)
    square = jnp.maximum(jnp.sum(sum_col[...], axis=0, keepdims=True), 0.0)
    dist = 1.0 - sum_col[...] * lax.rsqrt(square + 1e-06)
    slot = lax.broadcasted_iota(jnp.int32, (width_all, lanes), 0)
    within = slot - (slot // slot_count) * slot_count
    lane = lax.broadcasted_iota(jnp.int32, (width_all, lanes), 1)
    spread = jnp.where(lane == within, near_col[...], jnp.where(lane == within + half, dist, 0.0))
    source = lax.broadcasted_iota(jnp.int32, (owners, width_all), 0) * slot_count
    member = lax.broadcasted_iota(jnp.int32, (owners, width_all), 1)
    chosen = jnp.where((member >= source) & (member < source + slot_count), 1.0, 0.0).astype(BF16)
    out = jnp.zeros((owners, lanes), F32)
    for piece in split3(spread):
        out += jnp.dot(chosen, piece, preferred_element_type=F32)
    message_ref[...] = out


def scores(members, owners, slot_count, half):
    width_all = members.shape[0]
    return pl.pallas_call(
        functools.partial(score_kernel, slot_count, half),
        out_shape=jax.ShapeDtypeStruct((owners, 2 * half), F32),
        scratch_shapes=[pltpu.VMEM((width_all, 1), F32)] * 2,
        compiler_params=pltpu.CompilerParams(vmem_limit_bytes=VMEM_BYTES),
    )(members)


def gram_kernel(members_ref, gram_ref):
    width_all = members_ref.shape[0]
    block = 128
    here = pl.program_id(0) * block
    gram_ref[0] = lax.dot_general(
        members_ref[pl.ds(pl.multiple_of(here, block), block), :],
        members_ref[...],
        (((1,), (1,)), ((), ())),
        preferred_element_type=F32,
    )


def gram(members):
    width_all, width = members.shape
    block = 128
    return pl.pallas_call(
        gram_kernel,
        grid=(width_all // block,),
        in_specs=[pl.BlockSpec((width_all, width), lambda b: (0, 0))],
        out_specs=pl.BlockSpec((1, block, width_all), lambda b: (0, b, 0)),
        out_shape=jax.ShapeDtypeStruct((1, width_all, width_all), F32),
        compiler_params=pltpu.CompilerParams(vmem_limit_bytes=VMEM_BYTES),
        cost_estimate=pl.CostEstimate(
            flops=2 * width_all * width_all * width,
            bytes_accessed=2 * width_all * width + 4 * width_all * width_all,
            transcendentals=0,
        ),
    )(members)


def fetch_kernel(half, message_ref, label_ref, rank_ref, valid_ref, near_ref, dist_ref):
    owners, lanes = message_ref.shape
    rows = label_ref.shape[1]
    owner = lax.broadcasted_iota(jnp.int32, (owners, rows), 0)
    chosen = jnp.where(owner == label_ref[...], 1.0, 0.0).astype(BF16)
    mine = jnp.zeros((lanes, rows), F32)
    for piece in split3(message_ref[...]):
        mine += lax.dot_general(piece, chosen, (((0,), (0,)), ((), ())), preferred_element_type=F32)
    lane = lax.broadcasted_iota(jnp.int32, (lanes, rows), 0)
    rank = rank_ref[...]
    valid = valid_ref[...].astype(F32)
    near_ref[...] = jnp.sum(jnp.where(lane == rank, mine, 0.0), axis=0, keepdims=True) * valid
    dist_ref[...] = jnp.sum(jnp.where(lane == rank + half, mine, 0.0), axis=0, keepdims=True) * valid


def fetch(message, label_row, rank_row, valid_row, half):
    rows = label_row.shape[1]
    return pl.pallas_call(
        functools.partial(fetch_kernel, half),
        out_shape=(jax.ShapeDtypeStruct((1, rows), F32),) * 2,
    )(message, label_row, rank_row, valid_row)


def per_device(tokens, proj_weight, labels, valid_rows):
    row_count = tokens.shape[0]
    owners = lax.axis_size("clus")
    slot_count = 2 * row_count // owners
    width_all = owners * slot_count
    half = -(-slot_count // 64) * 64
    label_row = labels.reshape(1, row_count)
    valid_row = valid_rows.reshape(1, row_count)
    packed, rank_row = embed_and_pack(tokens, proj_weight, label_row, valid_row, owners, slot_count)
    arrived = lax.all_to_all(
        packed.reshape(owners, slot_count, -1), "clus", split_axis=0, concat_axis=0, tiled=True
    )
    members = arrived.reshape(width_all, -1)
    message = scores(members, owners, slot_count, half)
    returned = lax.all_to_all(message, "clus", split_axis=0, concat_axis=0, tiled=True)
    similar = gram(members)
    nearest, centre_dist = fetch(returned, label_row, rank_row, valid_row, half)
    return (similar, nearest.reshape(row_count), centre_dist.reshape(row_count))


def solution(mesh):
    return jax.shard_map(
        per_device,
        mesh=mesh,
        in_specs=(
            P(("groups", "clus"), None),
            P(),
            P(("groups", "clus"), None),
            P(("groups", "clus")),
        ),
        out_specs=(P(("groups", "clus"), None, None), P(("groups", "clus")), P(("groups", "clus"))),
        check_vma=False,
    )
```

time: 86.3 us -> 71.3 us (0.83)
  blocking collectives: 0 us -> 38.7 us
  waiting for transfers between devices: 30.3 us -> 2.62 us
  Pallas kernels: 0 us -> 18.6 us
  starting transfers between devices: 21.4 us -> 3.98 us
  matrix products: 13 us -> 0 us
  other arithmetic: 11.8 us -> 2.54 us
  local copies, waits for them, and re-layouts: 7.68 us -> 3.71 us
    all_to_all x0 -> x1, blocking collectives: none -> 38.7 us  [per_device(): lax.all_to_all(packed.reshape(owners, slot_count, -1), 'clus', split_axis...]
    all_to_all x3 -> x1, waiting for transfers between devices: 30.3 us -> 2.62 us  [per_device(): lax.all_to_all(message, 'clus', split_axis=0, concat_axis=0, tiled=True)]
    pallas_call x0 -> x4, Pallas kernels: none -> 18.6 us  [the longest x1 9.77 us: embed_and_pack(): pl.pallas_call(functools.partial(embed_kernel, slot_count, steps), grid=(...]
    all_to_all x3 -> x1, starting transfers between devices: 21.4 us -> 3.98 us  [per_device(): lax.all_to_all(message, 'clus', split_axis=0, concat_axis=0, tiled=True)]
    dot_general x3 -> x0, matrix products: 13 us -> none  [the longest x1 7.31 us: per_device(): embed = jnp.dot(tokens, proj_weight, preferred_element_type=jnp.float32)]
    scatter x1 -> x0, other arithmetic: 3.86 us -> none  [per_device(): jnp.zeros((owners * slot_count, embed_width), jnp.bfloat16).at[slot_index]]
    gather x2 -> x0, local copies, waits for them, and re-layouts: 3.37 us -> none  [the longest x1 1.69 us: per_device(): jnp.take(returned[1].reshape(width_all), slot_index) * mask_float]
    pallas_call x0 -> x2, other arithmetic: none -> 2.54 us  [fetch(): pl.pallas_call(functools.partial(fetch_kernel, half), out_shape=(jax.Shap...]
  transfers between devices with their start and end apart: 3 -> 1, of which waited for: 2 -> 1; matrix products, arithmetic and copies ran while one was open for 12% -> 0% of each run, Pallas kernels for 0% -> 5%
where the time goes in v1:
time: 71.3 us; the launch traced here: 70.8 us
  blocking collectives  38.7 us (54%)
  Pallas kernels  18.6 us (26%)
  starting transfers between devices  3.98 us (6%)
  local copies, waits for them, and re-layouts  3.71 us (5%)
  waiting for transfers between devices  2.62 us (4%)
  other arithmetic  2.54 us (4%)
    all_to_all x1, blocking collectives, per_device(): lax.all_to_all(packed.reshape(owners, slot_count, -1), 'clus', split_axis...  38.7 us
    pallas_call x1, Pallas kernels, embed_and_pack(): pl.pallas_call(functools.partial(embed_kernel, slot_count, steps), grid=(...  9.77 us
    all_to_all x1, starting transfers between devices, per_device(): lax.all_to_all(message, 'clus', split_axis=0, concat_axis=0, tiled=True)  3.98 us
    pallas_call x1, Pallas kernels, gram(): pl.pallas_call(gram_kernel, grid=(width_all // block,), in_specs=[pl.Bloc...  3.79 us
    pallas_call x1, Pallas kernels, scores(): pl.pallas_call(functools.partial(score_kernel, slot_count, half), out_sha...  3.38 us
    unnamed x10, local copies, waits for them, and re-layouts  3.02 us
    all_to_all x1, waiting for transfers between devices, per_device(): lax.all_to_all(message, 'clus', split_axis=0, concat_axis=0, tiled=True)  2.62 us
    pallas_call x2, other arithmetic, fetch(): pl.pallas_call(functools.partial(fetch_kernel, half), out_shape=(jax.Shap...  2.54 us
  transfers between devices with their start and end apart: 1, of which 1 were waited for; matrix products, arithmetic and copies ran while one was open for 0% of the time, Pallas kernels for 5%

profile of v1, /device:TPU:0, one launch (start us, length us, event | category | flops | bytes accessed | tf_op | source)
XLA Modules:
  0.0 70.8 jit_solution(8858884629729848113)
XLA Ops:
  0.6 0.7 reshape.27.valid_ref
  1.3 0.0 copy-start.1
  1.3 0.0 copy-start
  1.3 1.7 %copy-done = bf16[320,4096]{1,0:T(8,128)(2,1)S(1)} copy-done((bf16[320,4096]{1,0:T(8,128)(2,1)S(1)}, bf16[320,4096]{1,0:T(8,128)(2,1)}, u32[]{:S(2)}) %copy-start) | copy-done | bytes 2621464
  3.1 0.0 copy-start.2
  3.1 0.7 copy-done.2
  3.7 9.8 %shard_map.67 = (bf16[640,1024]{1,0:T(8,128)(2,1)S(1)}, s32[1,320]{1,0:T(1,128)S(1)}) custom-call(bf16[320,4096]{1,0:T(8,128)(2,1)S(1)} %copy-done, bf16[4096,1024]{1,0:T(8,128)(2,1)} %weight_ref.1, s32[1,320]{1,0:T(1,128)S(1)} %bitcast.11, s32[1,320]{1,0:T(1,128)S(1)} %reshape.27.valid_ref), custom_call_target="tpu_custom_call" | custom-call | flops 2684354560 | bytes 11010048 | tf_op jit(solution)/shard_map/pallas_call | solution.py:62
  13.5 0.0 copy-done.1
  13.5 0.0 copy-start.3
  13.5 38.7 %all_to_all.16 = bf16[16,40,1024]{2,1,0:T(8,128)(2,1)S(1)} all-to-all(bf16[16,40,1024]{2,1,0:T(8,128)(2,1)S(1)} %bitcast.9), channel_id=1, replica_groups=mesh['groups'=2,'clus'=16] {'clus'}, dimensions={0} | all-to-all | bytes 2621440 | tf_op jit(solution)/shard_map/all_to_all | solution.py:186
  52.2 3.4 %shard_map.69 = f32[16,128]{1,0:T(8,128)} custom-call(bf16[640,1024]{1,0:T(8,128)(2,1)S(1)} %bitcast.7), custom_call_target="tpu_custom_call" | custom-call | tf_op jit(solution)/shard_map/pallas_call | solution.py:116
  55.6 0.0 copy-done.3
  55.6 4.0 %all-to-all-start.1 = ((f32[16,1,128]{2,1,0:T(1,128)}), f32[16,1,128]{2,1,0:T(1,128)S(1)}, u32[]{:S(2)}, u32[]{:S(2)}) async-start(f32[16,1,128]{2,1,0:T(1,128)} %bitcast.4), calls=%async_computation.1 | async-start | bytes 16384 | tf_op jit(solution)/shard_map/all_to_all | solution.py:191
  59.6 3.8 %shard_map.68 = f32[1,640,640]{2,1,0:T(8,128)} custom-call(bf16[640,1024]{1,0:T(8,128)(2,1)S(1)} %bitcast.8), custom_call_target="tpu_custom_call" | custom-call | flops 838860800 | bytes 2949120 | tf_op jit(solution)/shard_map/pallas_call | solution.py:139
  63.4 2.6 %all-to-all-done.1 = f32[16,1,128]{2,1,0:T(1,128)S(1)} async-done(((f32[16,1,128]{2,1,0:T(1,128)}), f32[16,1,128]{2,1,0:T(1,128)S(1)}, u32[]{:S(2)}, u32[]{:S(2)}) %all-to-all-start.1) | async-done | bytes 8224 | tf_op jit(solution)/shard_map/all_to_all | solution.py:191
  66.0 0.0 copy-start.4
  66.0 0.6 copy-done.4
  66.6 1.6 %shard_map.70 = (f32[1,320]{1,0:T(1,128)}, f32[1,320]{1,0:T(1,128)}) custom-call(f32[16,128]{1,0:T(8,128)} %bitcast.12, s32[1,320]{1,0:T(1,128)} %bitcast.10, s32[1,320]{1,0:T(1,128)} %copy-done.3, s32[1,320]{1,0:T(1,128)} %copy-done.1), custom_call_target="tpu_custom_call" | custom-call | tf_op jit(solution)/shard_map/pallas_call | solution.py:171
  68.3 1.3 %reduce = f32[320]{0:T(512)} reduce(f32[1,320]{1,0:T(1,128)} %get-tuple-element.9, f32[]{:T(128)} %constant), dimensions={0}, to_apply=%get-tuple-element.9.reduce_sub_computation | reduce | bytes 2564 | tf_op jit(solution)/shard_map/pallas_call | solution.py:171
  69.5 1.3 %reduce.1 = f32[320]{0:T(512)} reduce(f32[1,320]{1,0:T(1,128)} %get-tuple-element.10, f32[]{:T(128)} %constant), dimensions={0}, to_apply=%get-tuple-element.10.reduce_sub_computation | reduce | bytes 2564 | tf_op jit(solution)/shard_map/pallas_call | solution.py:171
Async XLA Ops:
  1.3 12.2 %copy-start.1 = (s32[1,320]{1,0:T(1,128)}, s32[1,320]{1,0:T(1,128)S(1)}, u32[]{:S(2)}) copy-start(s32[1,320]{1,0:T(1,128)S(1)} %reshape.27.valid_ref) | copy-start | bytes 3844
  1.3 1.7 %copy-start = (bf16[320,4096]{1,0:T(8,128)(2,1)S(1)}, bf16[320,4096]{1,0:T(8,128)(2,1)}, u32[]{:S(2)}) copy-start(bf16[320,4096]{1,0:T(8,128)(2,1)} %tokens_ref.1) | copy-start | bytes 7864324
  3.1 0.7 copy-start.2
  13.5 42.1 %copy-start.3 = (s32[1,320]{1,0:T(1,128)}, s32[1,320]{1,0:T(1,128)S(1)}, u32[]{:S(2)}) copy-start(s32[1,320]{1,0:T(1,128)S(1)} %get-tuple-element.8.rank_ref) | copy-start | bytes 3844
  55.6 10.4 %all-to-all-start.1 = ((f32[16,1,128]{2,1,0:T(1,128)}), f32[16,1,128]{2,1,0:T(1,128)S(1)}, u32[]{:S(2)}, u32[]{:S(2)}) async-start(f32[16,1,128]{2,1,0:T(1,128)} %bitcast.4), calls=%async_computation.1 | async-start | bytes 16384 | tf_op jit(solution)/shard_map/all_to_all | solution.py:191
  66.0 0.6 copy-start.4

commit v2 on v1

v2 whole, which is shorter than its diff:
```python
import functools

import jax
import jax.numpy as jnp
from jax import lax
from jax.experimental import pallas as pl
from jax.experimental.pallas import tpu as pltpu
from jax.sharding import PartitionSpec as P

F32 = jnp.float32
BF16 = jnp.bfloat16
VMEM_BYTES = 48 * 1024 * 1024
EMBED_VMEM_BYTES = 60 * 1024 * 1024


def split3(x):
    hi = x.astype(BF16)
    rest = x - hi.astype(F32)
    mid = rest.astype(BF16)
    low = (rest - mid.astype(F32)).astype(BF16)
    return hi, mid, low


def place_rows(label_row, valid_row, slot_count, width_all):
    rows = label_row.shape[1]
    label = label_row.astype(F32)
    below = lax.broadcasted_iota(jnp.int32, (rows, rows), 0)
    across = lax.broadcasted_iota(jnp.int32, (rows, rows), 1)
    label_col = jnp.sum(jnp.where(below == across, label, 0.0), axis=1, keepdims=True)
    earlier = (label_col == label) & (below < across)
    rank = jnp.sum(jnp.where(earlier, 1.0, 0.0), axis=0, keepdims=True).astype(jnp.int32)
    slot = jnp.where(valid_row > 0, label_row * slot_count + rank, -1)
    slots = lax.broadcasted_iota(jnp.int32, (width_all, rows), 0)
    return rank, jnp.where(slots == slot, 1.0, 0.0).astype(BF16)


def embed_kernel(
    slot_count, tokens_hbm, weight_hbm, label_hbm, valid_hbm, packed_ref, rank_ref,
    tokens, weight, total, place, label_ref, valid_ref, token_sem, weight_sem, small_sem,
):
    steps = token_sem.shape[0]
    block = tokens.shape[1] // steps
    small = (
        pltpu.make_async_copy(label_hbm, label_ref, small_sem.at[0]),
        pltpu.make_async_copy(valid_hbm, valid_ref, small_sem.at[1]),
    )
    for copy in small:
        copy.start()
    copies = []
    for k in range(steps):
        part = slice(k * block, (k + 1) * block)
        pair = (
            pltpu.make_async_copy(tokens_hbm.at[:, part], tokens.at[:, part], token_sem.at[k]),
            pltpu.make_async_copy(weight_hbm.at[part, :], weight.at[part, :], weight_sem.at[k]),
        )
        for copy in pair:
            copy.start()
        copies.append(pair)
    for copy in small:
        copy.wait()
    rank, chosen = place_rows(label_ref[...], valid_ref[...].reshape(label_ref.shape), slot_count, place.shape[0])
    rank_ref[...] = rank
    place[...] = chosen
    for k, pair in enumerate(copies):
        for copy in pair:
            copy.wait()
        part = slice(k * block, (k + 1) * block)
        product = jnp.dot(tokens[:, part], weight[part, :], preferred_element_type=F32)
        if k == 0:
            total[...] = product
        else:
            total[...] += product
    embed = total[...]
    scale = lax.rsqrt(jnp.sum(embed * embed, axis=1, keepdims=True) + 1e-06)
    unit = (embed * scale).astype(BF16)
    packed_ref[...] = jnp.dot(place[...], unit, preferred_element_type=F32).astype(BF16)


def embed_and_pack(tokens, weight, label_row, valid, owners, slot_count):
    rows, depth = tokens.shape
    width = weight.shape[1]
    steps = 8 if depth % 1024 == 0 else 1
    width_all = owners * slot_count
    return pl.pallas_call(
        functools.partial(embed_kernel, slot_count),
        in_specs=[pl.BlockSpec(memory_space=pltpu.HBM)] * 4,
        out_shape=(
            jax.ShapeDtypeStruct((width_all, width), BF16),
            jax.ShapeDtypeStruct((1, rows), jnp.int32),
        ),
        scratch_shapes=[
            pltpu.VMEM((rows, depth), BF16),
            pltpu.VMEM((depth, width), BF16),
            pltpu.VMEM((rows, width), F32),
            pltpu.VMEM((width_all, rows), BF16),
            pltpu.VMEM((1, rows), jnp.int32),
            pltpu.VMEM((rows,), jnp.int32),
            pltpu.SemaphoreType.DMA((steps,)),
            pltpu.SemaphoreType.DMA((steps,)),
            pltpu.SemaphoreType.DMA((2,)),
        ],
        compiler_params=pltpu.CompilerParams(vmem_limit_bytes=EMBED_VMEM_BYTES),
        cost_estimate=pl.CostEstimate(
            flops=2 * rows * depth * width, bytes_accessed=2 * depth * width + 2 * rows * depth, transcendentals=0
        ),
    )(tokens, weight, label_row, valid)


def score_kernel(slot_count, half, members_ref, message_ref, similar_hbm, gram, sem):
    width_all = members_ref.shape[0]
    owners, lanes = message_ref.shape
    block = width_all // 2
    copies = []
    nears, sums = [], []
    for b in range(2):
        part = slice(b * block, (b + 1) * block)
        gram[part, :] = lax.dot_general(
            members_ref[part, :], members_ref[...], (((1,), (1,)), ((), ())), preferred_element_type=F32
        )
        copy = pltpu.make_async_copy(gram.at[part, :], similar_hbm.at[0, part, :], sem.at[b])
        copy.start()
        copies.append(copy)
        tile = gram[part, :]
        own = lax.broadcasted_iota(jnp.int32, (block, width_all), 0) + b * block
        other = lax.broadcasted_iota(jnp.int32, (block, width_all), 1)
        nears.append(jnp.max(jnp.where(own == other, 0.0, tile), axis=1, keepdims=True))
        sums.append(jnp.sum(tile, axis=1, keepdims=True))
    near = jnp.concatenate(nears, axis=0)
    sums = jnp.concatenate(sums, axis=0)
    square = jnp.maximum(jnp.sum(sums, axis=0, keepdims=True), 0.0)
    dist = 1.0 - sums * lax.rsqrt(square + 1e-06)
    slot = lax.broadcasted_iota(jnp.int32, (width_all, lanes), 0)
    within = slot - (slot // slot_count) * slot_count
    lane = lax.broadcasted_iota(jnp.int32, (width_all, lanes), 1)
    spread = jnp.where(lane == within, near, jnp.where(lane == within + half, dist, 0.0))
    source = lax.broadcasted_iota(jnp.int32, (owners, width_all), 0) * slot_count
    member = lax.broadcasted_iota(jnp.int32, (owners, width_all), 1)
    chosen = jnp.where((member >= source) & (member < source + slot_count), 1.0, 0.0).astype(BF16)
    out = jnp.zeros((owners, lanes), F32)
    for piece in split3(spread):
        out += jnp.dot(chosen, piece, preferred_element_type=F32)
    message_ref[...] = out
    for copy in copies:
        copy.wait()


def scores(members, owners, slot_count, half):
    width_all, width = members.shape
    return pl.pallas_call(
        functools.partial(score_kernel, slot_count, half),
        out_specs=(pl.BlockSpec(memory_space=pltpu.VMEM), pl.BlockSpec(memory_space=pltpu.HBM)),
        out_shape=(
            jax.ShapeDtypeStruct((owners, 2 * half), F32),
            jax.ShapeDtypeStruct((1, width_all, width_all), F32),
        ),
        scratch_shapes=[pltpu.VMEM((width_all, width_all), F32), pltpu.SemaphoreType.DMA((2,))],
        compiler_params=pltpu.CompilerParams(vmem_limit_bytes=VMEM_BYTES),
    )(members)


def fetch_kernel(half, message_ref, label_ref, rank_ref, valid_ref, near_ref, dist_ref):
    owners, lanes = message_ref.shape
    rows = label_ref.shape[1]
    owner = lax.broadcasted_iota(jnp.int32, (owners, rows), 0)
    chosen = jnp.where(owner == label_ref[...], 1.0, 0.0).astype(BF16)
    mine = jnp.zeros((lanes, rows), F32)
    for piece in split3(message_ref[...]):
        mine += lax.dot_general(piece, chosen, (((0,), (0,)), ((), ())), preferred_element_type=F32)
    lane = lax.broadcasted_iota(jnp.int32, (lanes, rows), 0)
    rank = rank_ref[...]
    valid = valid_ref[...].astype(F32)
    near_ref[...] = jnp.sum(jnp.where(lane == rank, mine, 0.0), axis=0) * valid
    dist_ref[...] = jnp.sum(jnp.where(lane == rank + half, mine, 0.0), axis=0) * valid


def fetch(message, label_row, rank_row, valid, half):
    rows = label_row.shape[1]
    return pl.pallas_call(
        functools.partial(fetch_kernel, half),
        out_shape=(jax.ShapeDtypeStruct((rows,), F32),) * 2,
    )(message, label_row, rank_row, valid)


def per_device(tokens, proj_weight, labels, valid_rows):
    row_count = tokens.shape[0]
    owners = lax.axis_size("clus")
    slot_count = 2 * row_count // owners
    width_all = owners * slot_count
    half = -(-slot_count // 64) * 64
    label_row = labels.reshape(1, row_count)
    packed, rank_row = embed_and_pack(tokens, proj_weight, label_row, valid_rows, owners, slot_count)
    arrived = lax.all_to_all(
        packed.reshape(owners, slot_count, -1), "clus", split_axis=0, concat_axis=0, tiled=True
    )
    members = arrived.reshape(width_all, -1)
    message, similar = scores(members, owners, slot_count, half)
    returned = lax.all_to_all(message, "clus", split_axis=0, concat_axis=0, tiled=True)
    nearest, centre_dist = fetch(returned, label_row, rank_row, valid_rows, half)
    return (similar, nearest, centre_dist)


def solution(mesh):
    return jax.shard_map(
        per_device,
        mesh=mesh,
        in_specs=(
            P(("groups", "clus"), None),
            P(),
            P(("groups", "clus"), None),
            P(("groups", "clus")),
        ),
        out_specs=(P(("groups", "clus"), None, None), P(("groups", "clus")), P(("groups", "clus"))),
        check_vma=False,
    )
```

time: 71.3 us -> 63.2 us (0.89)
  blocking collectives: 38.7 us -> 49.2 us
  Pallas kernels: 18.6 us -> 13.1 us
  starting transfers between devices: 3.98 us -> 0 us
  local copies, waits for them, and re-layouts: 3.71 us -> 0 us
  waiting for transfers between devices: 2.62 us -> 0 us
  other arithmetic: 2.54 us -> 0 us
    all_to_all x0 -> x1, blocking collectives: none -> 10.3 us  [per_device(): lax.all_to_all(message, 'clus', split_axis=0, concat_axis=0, tiled=True)]
    pallas_call x3 -> x2, Pallas kernels: 16.9 us -> 11.5 us  [the longest x1 9.24 us: embed_and_pack(): pl.pallas_call(functools.partial(embed_kernel, slot_count), in_specs=[pl....]
    all_to_all x1 -> x0, starting transfers between devices: 3.98 us -> none  [per_device(): lax.all_to_all(message, 'clus', split_axis=0, concat_axis=0, tiled=True)]
    unnamed x10 -> x0, local copies, waits for them, and re-layouts: 3.02 us -> none
    all_to_all x1 -> x0, waiting for transfers between devices: 2.62 us -> none  [per_device(): lax.all_to_all(message, 'clus', split_axis=0, concat_axis=0, tiled=True)]
    pallas_call x2 -> x0, other arithmetic: 2.54 us -> none  [fetch(): pl.pallas_call(functools.partial(fetch_kernel, half), out_shape=(jax.Shap...]
  transfers between devices with their start and end apart: 1 -> 0, of which waited for: 1 -> 0; matrix products, arithmetic and copies ran while one was open for 0% -> 0% of each run, Pallas kernels for 5% -> 0%
where the time goes in v2:
time: 63.2 us; the launch traced here: 62.9 us
  blocking collectives  49.2 us (78%)
  Pallas kernels  13.1 us (21%)
  between operations  0.65 us (1%)
    all_to_all x1, blocking collectives, per_device(): lax.all_to_all(packed.reshape(owners, slot_count, -1), 'clus', split_axis...  38.9 us
    all_to_all x1, blocking collectives, per_device(): lax.all_to_all(message, 'clus', split_axis=0, concat_axis=0, tiled=True)  10.3 us
    pallas_call x1, Pallas kernels, embed_and_pack(): pl.pallas_call(functools.partial(embed_kernel, slot_count), in_specs=[pl....  9.24 us
    pallas_call x1, Pallas kernels, scores(): pl.pallas_call(functools.partial(score_kernel, slot_count, half), out_spe...  2.24 us
    pallas_call x1, Pallas kernels, fetch(): pl.pallas_call(functools.partial(fetch_kernel, half), out_shape=(jax.Shap...  1.59 us

profile of v2, /device:TPU:0, one launch (start us, length us, event | category | flops | bytes accessed | tf_op | source)
XLA Modules:
  0.0 62.9 jit_solution(18404340297919650102)
XLA Ops:
  0.6 9.2 %shard_map.67 = (bf16[640,1024]{1,0:T(8,128)(2,1)}, s32[1,320]{1,0:T(1,128)}) custom-call(bf16[320,4096]{1,0:T(8,128)(2,1)} %tokens_hbm.1, bf16[4096,1024]{1,0:T(8,128)(2,1)} %weight_hbm.1, s32[1,320]{1,0:T(1,128)} %bitcast.11, s32[320]{0:T(512)} %valid_ref.1), custom_call_target="tpu_custom_call" | custom-call | flops 2684354560 | bytes 11010048 | tf_op jit(solution)/shard_map/pallas_call | solution.py:84
  9.9 38.9 %all_to_all.16 = bf16[16,40,1024]{2,1,0:T(8,128)(2,1)S(1)} all-to-all(bf16[16,40,1024]{2,1,0:T(8,128)(2,1)} %bitcast.9), channel_id=1, replica_groups=mesh['groups'=2,'clus'=16] {'clus'}, dimensions={0} | all-to-all | bytes 2621440 | tf_op jit(solution)/shard_map/all_to_all | solution.py:192
  48.8 2.2 %shard_map.68 = (f32[16,128]{1,0:T(8,128)S(1)}, f32[1,640,640]{2,1,0:T(8,128)}) custom-call(bf16[640,1024]{1,0:T(8,128)(2,1)S(1)} %bitcast.7), custom_call_target="tpu_custom_call" | custom-call | tf_op jit(solution)/shard_map/pallas_call | solution.py:149
  51.0 10.3 %all_to_all.17 = f32[16,1,128]{2,1,0:T(1,128)} all-to-all(f32[16,1,128]{2,1,0:T(1,128)S(1)} %bitcast.8), channel_id=1, replica_groups=mesh['groups'=2,'clus'=16] {'clus'}, dimensions={0} | all-to-all | bytes 16384 | tf_op jit(solution)/shard_map/all_to_all | solution.py:197
  61.3 1.6 %shard_map.69 = (f32[320]{0:T(512)}, f32[320]{0:T(512)}) custom-call(f32[16,128]{1,0:T(8,128)} %bitcast.10, s32[1,320]{1,0:T(1,128)} %bitcast.12, s32[1,320]{1,0:T(1,128)} %get-tuple-element.12.rank_ref, s32[320]{0:T(512)} %valid_ref.1), custom_call_target="tpu_custom_call" | custom-call | tf_op jit(solution)/shard_map/pallas_call | solution.py:178

commit v3 on v2

--- a/solution.py
+++ b/solution.py
@@ -10,7 +10,10 @@
 F32 = jnp.float32
 BF16 = jnp.bfloat16
 VMEM_BYTES = 48 * 1024 * 1024
-EMBED_VMEM_BYTES = 60 * 1024 * 1024
+EMBED_VMEM_BYTES = 55 * 1024 * 1024
+LATE_VMEM_BYTES = 55 * 1024 * 1024
+EARLY = 3
+ORDER_FLOPS = 2 * 10**9
 
 
 def split3(x):
@@ -21,25 +24,29 @@
     return hi, mid, low
 
 
-def place_rows(label_row, valid_row, slot_count, width_all):
+def rank_rows(label_row):
     rows = label_row.shape[1]
     label = label_row.astype(F32)
     below = lax.broadcasted_iota(jnp.int32, (rows, rows), 0)
     across = lax.broadcasted_iota(jnp.int32, (rows, rows), 1)
     label_col = jnp.sum(jnp.where(below == across, label, 0.0), axis=1, keepdims=True)
     earlier = (label_col == label) & (below < across)
-    rank = jnp.sum(jnp.where(earlier, 1.0, 0.0), axis=0, keepdims=True).astype(jnp.int32)
-    slot = jnp.where(valid_row > 0, label_row * slot_count + rank, -1)
-    slots = lax.broadcasted_iota(jnp.int32, (width_all, rows), 0)
-    return rank, jnp.where(slots == slot, 1.0, 0.0).astype(BF16)
-
-
-def embed_kernel(
-    slot_count, tokens_hbm, weight_hbm, label_hbm, valid_hbm, packed_ref, rank_ref,
-    tokens, weight, total, place, label_ref, valid_ref, token_sem, weight_sem, small_sem,
+    return jnp.sum(jnp.where(earlier, 1.0, 0.0), axis=0, keepdims=True).astype(jnp.int32)
+
+
+def place_rows(slot_row, valid_row, width_all):
+    slots = lax.broadcasted_iota(jnp.int32, (width_all, slot_row.shape[1]), 0)
+    slot = jnp.where(valid_row > 0, slot_row, -1)
+    return jnp.where(slots == slot, 1.0, 0.0).astype(BF16)
+
+
+def early_kernel(
+    slot_count, tokens_hbm, weight_hbm, label_hbm, valid_hbm, keep_ref, send_ref, rank_ref, tokens,
+    weight, total, place, label_ref, valid_ref, token_sem, weight_sem, small_sem,
 ):
     steps = token_sem.shape[0]
     block = tokens.shape[1] // steps
+    early = weight.shape[1]
     small = (
         pltpu.make_async_copy(label_hbm, label_ref, small_sem.at[0]),
         pltpu.make_async_copy(valid_hbm, valid_ref, small_sem.at[1]),
@@ -51,16 +58,17 @@
         part = slice(k * block, (k + 1) * block)
         pair = (
             pltpu.make_async_copy(tokens_hbm.at[:, part], tokens.at[:, part], token_sem.at[k]),
-            pltpu.make_async_copy(weight_hbm.at[part, :], weight.at[part, :], weight_sem.at[k]),
+            pltpu.make_async_copy(weight_hbm.at[part, 0:early], weight.at[part, :], weight_sem.at[k]),
         )
         for copy in pair:
             copy.start()
         copies.append(pair)
     for copy in small:
         copy.wait()
-    rank, chosen = place_rows(label_ref[...], valid_ref[...].reshape(label_ref.shape), slot_count, place.shape[0])
+    rank = rank_rows(label_ref[...])
     rank_ref[...] = rank
-    place[...] = chosen
+    relative = (label_ref[...] ^ lax.axis_index("clus")) * slot_count + rank
+    place[...] = place_rows(relative, valid_ref[...].reshape(label_ref.shape), place.shape[0])
     for k, pair in enumerate(copies):
         for copy in pair:
             copy.wait()
@@ -70,28 +78,29 @@
             total[...] = product
         else:
             total[...] += product
-    embed = total[...]
-    scale = lax.rsqrt(jnp.sum(embed * embed, axis=1, keepdims=True) + 1e-06)
-    unit = (embed * scale).astype(BF16)
-    packed_ref[...] = jnp.dot(place[...], unit, preferred_element_type=F32).astype(BF16)
-
-
-def embed_and_pack(tokens, weight, label_row, valid, owners, slot_count):
+    embed = total[...].astype(BF16)
+    near = keep_ref.shape[0]
+    send_ref[...] = jnp.dot(place[near:, :], embed, preferred_element_type=F32).astype(BF16)
+    keep_ref[...] = jnp.dot(place[:near, :], embed, preferred_element_type=F32).astype(BF16)
+
+
+def embed_early(tokens, weight, label_row, valid, owners, slot_count, early):
     rows, depth = tokens.shape
-    width = weight.shape[1]
-    steps = 8 if depth % 1024 == 0 else 1
+    steps = 4 if depth % 1024 == 0 else 1
     width_all = owners * slot_count
     return pl.pallas_call(
-        functools.partial(embed_kernel, slot_count),
+        functools.partial(early_kernel, slot_count),
         in_specs=[pl.BlockSpec(memory_space=pltpu.HBM)] * 4,
+        out_specs=(pl.BlockSpec(memory_space=pltpu.VMEM),) * 4,
         out_shape=(
-            jax.ShapeDtypeStruct((width_all, width), BF16),
+            jax.ShapeDtypeStruct((width_all // 2, early), BF16),
+            jax.ShapeDtypeStruct((width_all // 2, early), BF16),
             jax.ShapeDtypeStruct((1, rows), jnp.int32),
+            jax.ShapeDtypeStruct((rows, depth), BF16),
         ),
         scratch_shapes=[
-            pltpu.VMEM((rows, depth), BF16),
-            pltpu.VMEM((depth, width), BF16),
-            pltpu.VMEM((rows, width), F32),
+            pltpu.VMEM((depth, early), BF16),
+            pltpu.VMEM((rows, early), F32),
             pltpu.VMEM((width_all, rows), BF16),
             pltpu.VMEM((1, rows), jnp.int32),
             pltpu.VMEM((rows,), jnp.int32),
@@ -101,26 +110,140 @@
         ],
         compiler_params=pltpu.CompilerParams(vmem_limit_bytes=EMBED_VMEM_BYTES),
         cost_estimate=pl.CostEstimate(
-            flops=2 * rows * depth * width, bytes_accessed=2 * depth * width + 2 * rows * depth, transcendentals=0
+            flops=2 * rows * depth * early, bytes_accessed=2 * depth * early + 2 * rows * depth, transcendentals=0
         ),
     )(tokens, weight, label_row, valid)
 
 
-def score_kernel(slot_count, half, members_ref, message_ref, similar_hbm, gram, sem):
-    width_all = members_ref.shape[0]
+def late_kernel(
+    slot_count, tokens, weight_hbm, label_hbm, valid_hbm, rank_ref, packed_ref,
+    weight, total, place, label_ref, valid_ref, weight_sem, small_sem,
+):
+    steps = weight_sem.shape[0]
+    block = tokens.shape[1] // steps
+    late = weight.shape[1]
+    early = weight_hbm.shape[1] - late
+    small = (
+        pltpu.make_async_copy(label_hbm, label_ref, small_sem.at[0]),
+        pltpu.make_async_copy(valid_hbm, valid_ref, small_sem.at[1]),
+    )
+    for copy in small:
+        copy.start()
+    copies = []
+    for k in range(steps):
+        part = slice(k * block, (k + 1) * block)
+        copy = pltpu.make_async_copy(weight_hbm.at[part, early:early + late], weight.at[part, :], weight_sem.at[k])
+        copy.start()
+        copies.append(copy)
+    for copy in small:
+        copy.wait()
+    slot = label_ref[...] * slot_count + rank_ref[...]
+    place[...] = place_rows(slot, valid_ref[...].reshape(label_ref.shape), place.shape[0])
+    for k, copy in enumerate(copies):
+        copy.wait()
+        part = slice(k * block, (k + 1) * block)
+        product = jnp.dot(tokens[:, part], weight[part, :], preferred_element_type=F32)
+        if k == 0:
+            total[...] = product
+        else:
+            total[...] += product
+    packed_ref[...] = jnp.dot(place[...], total[...].astype(BF16), preferred_element_type=F32).astype(BF16)
+
+
+def embed_late(tokens, weight, label_row, valid, rank_row, owners, slot_count, early):
+    rows, depth = tokens.shape
+    late = weight.shape[1] - early
+    steps = 8 if depth % 1024 == 0 else 1
+    width_all = owners * slot_count
+    return pl.pallas_call(
+        functools.partial(late_kernel, slot_count),
+        in_specs=[pl.BlockSpec(memory_space=pltpu.VMEM)]
+        + [pl.BlockSpec(memory_space=pltpu.HBM)] * 3
+        + [pl.BlockSpec(memory_space=pltpu.VMEM)],
+        out_shape=jax.ShapeDtypeStruct((width_all, late), BF16),
+        scratch_shapes=[
+            pltpu.VMEM((depth, late), BF16),
+            pltpu.VMEM((rows, late), F32),
+            pltpu.VMEM((width_all, rows), BF16),
+            pltpu.VMEM((1, rows), jnp.int32),
+            pltpu.VMEM((rows,), jnp.int32),
+            pltpu.SemaphoreType.DMA((steps,)),
+            pltpu.SemaphoreType.DMA((2,)),
+        ],
+        compiler_params=pltpu.CompilerParams(vmem_limit_bytes=LATE_VMEM_BYTES),
+        cost_estimate=pl.CostEstimate(
+            flops=2 * rows * depth * late, bytes_accessed=2 * depth * late, transcendentals=0
+        ),
+    )(tokens, weight, label_row, valid, rank_row)
+
+
+def spread_early(keep, send, owners, slot_count):
+    early = keep.shape[1]
+    held = keep.reshape(1, owners // 2, slot_count, early)
+    leaving = send.reshape(1, owners // 2, slot_count, early)
+    bit = owners // 2
+    while bit:
+        arrived = lax.ppermute(leaving, "clus", [(i, i ^ bit) for i in range(owners)])
+        both = jnp.concatenate([held, arrived], axis=0)
+        bit //= 2
+        held, leaving = both[:, :bit], both[:, bit:]
+    return both.reshape(owners * slot_count, early)
+
+
+def order_kernel(slot_count, relative_ref, members_ref):
+    width_all = relative_ref.shape[0]
+    owners = width_all // slot_count
+    me = lax.axis_index("clus")
+    member = lax.broadcasted_iota(jnp.int32, (width_all, 1), 0)
+    source = member // slot_count
+    distance = source ^ me
+    index = jnp.zeros_like(distance)
+    low, high = 1, owners // 2
+    while high:
+        index += jnp.where((distance & low) > 0, high, 0)
+        low, high = low * 2, high // 2
+    wanted = index * slot_count + member - source * slot_count
+    held = lax.broadcasted_iota(jnp.int32, (width_all, width_all), 1)
+    chosen = jnp.where(held == wanted, 1.0, 0.0).astype(BF16)
+    members_ref[...] = jnp.dot(chosen, relative_ref[...], preferred_element_type=F32).astype(BF16)
+
+
+def order_early(relative, slot_count):
+    return pl.pallas_call(
+        functools.partial(order_kernel, slot_count),
+        out_shape=jax.ShapeDtypeStruct(relative.shape, BF16),
+        compiler_params=pltpu.CompilerParams(vmem_limit_bytes=VMEM_BYTES),
+        cost_estimate=pl.CostEstimate(flops=ORDER_FLOPS, bytes_accessed=4 * relative.size, transcendentals=0),
+    )(relative)
+
+
+def score_kernel(slot_count, half, early_ref, late_ref, message_ref, similar_hbm, gram, sem):
+    width_all = early_ref.shape[0]
     owners, lanes = message_ref.shape
     block = width_all // 2
+    transposed = (((1,), (1,)), ((), ()))
+    cols, rows = [], []
+    for b in range(2):
+        part = slice(b * block, (b + 1) * block)
+        tile = lax.dot_general(early_ref[part, :], early_ref[...], transposed, preferred_element_type=F32)
+        tile += lax.dot_general(late_ref[part, :], late_ref[...], transposed, preferred_element_type=F32)
+        gram[part, :] = tile
+        own = lax.broadcasted_iota(jnp.int32, (block, width_all), 0) + b * block
+        other = lax.broadcasted_iota(jnp.int32, (block, width_all), 1)
+        itself = jnp.where(own == other, tile, 0.0)
+        cols.append(jnp.sum(itself, axis=1, keepdims=True))
+        rows.append(jnp.sum(itself, axis=0, keepdims=True))
+    scale_row = lax.rsqrt(rows[0] + rows[1] + 1e-06)
     copies = []
     nears, sums = [], []
     for b in range(2):
         part = slice(b * block, (b + 1) * block)
-        gram[part, :] = lax.dot_general(
-            members_ref[part, :], members_ref[...], (((1,), (1,)), ((), ())), preferred_element_type=F32
-        )
+        scale_col = lax.rsqrt(cols[b] + 1e-06)
+        tile = gram[part, :] * scale_col * scale_row
+        gram[part, :] = tile
         copy = pltpu.make_async_copy(gram.at[part, :], similar_hbm.at[0, part, :], sem.at[b])
         copy.start()
         copies.append(copy)
-        tile = gram[part, :]
         own = lax.broadcasted_iota(jnp.int32, (block, width_all), 0) + b * block
         other = lax.broadcasted_iota(jnp.int32, (block, width_all), 1)
         nears.append(jnp.max(jnp.where(own == other, 0.0, tile), axis=1, keepdims=True))
@@ -144,8 +267,8 @@
         copy.wait()
 
 
-def scores(members, owners, slot_count, half):
-    width_all, width = members.shape
+def scores(early, late, owners, slot_count, half):
+    width_all = early.shape[0]
     return pl.pallas_call(
         functools.partial(score_kernel, slot_count, half),
         out_specs=(pl.BlockSpec(memory_space=pltpu.VMEM), pl.BlockSpec(memory_space=pltpu.HBM)),
@@ -155,7 +278,7 @@
         ),
         scratch_shapes=[pltpu.VMEM((width_all, width_all), F32), pltpu.SemaphoreType.DMA((2,))],
         compiler_params=pltpu.CompilerParams(vmem_limit_bytes=VMEM_BYTES),
-    )(members)
+    )(early, late)
 
 
 def fetch_kernel(half, message_ref, label_ref, rank_ref, valid_ref, near_ref, dist_ref):
@@ -187,13 +310,17 @@
     slot_count = 2 * row_count // owners
     width_all = owners * slot_count
     half = -(-slot_count // 64) * 64
+    early = EARLY * proj_weight.shape[1] // 8
     label_row = labels.reshape(1, row_count)
-    packed, rank_row = embed_and_pack(tokens, proj_weight, label_row, valid_rows, owners, slot_count)
+    keep, send, rank_row, held_tokens = embed_early(
+        tokens, proj_weight, label_row, valid_rows, owners, slot_count, early
+    )
+    packed = embed_late(held_tokens, proj_weight, label_row, valid_rows, rank_row, owners, slot_count, early)
     arrived = lax.all_to_all(
         packed.reshape(owners, slot_count, -1), "clus", split_axis=0, concat_axis=0, tiled=True
     )
-    members = arrived.reshape(width_all, -1)
-    message, similar = scores(members, owners, slot_count, half)
+    early_members = order_early(spread_early(keep, send, owners, slot_count), slot_count)
+    message, similar = scores(early_members, arrived.reshape(width_all, -1), owners, slot_count, half)
     returned = lax.all_to_all(message, "clus", split_axis=0, concat_axis=0, tiled=True)
     nearest, centre_dist = fetch(returned, label_row, rank_row, valid_rows, half)
     return (similar, nearest, centre_dist)

time: 63.2 us -> 70.4 us (1.11)
  blocking collectives: 49.2 us -> 10.9 us
  waiting for transfers between devices: 0 us -> 27 us
  starting transfers between devices: 0 us -> 11.6 us
  Pallas kernels: 13.1 us -> 19.5 us
    all_to_all x1 -> x0, blocking collectives: 38.9 us -> none  [per_device(): lax.all_to_all(packed.reshape(owners, slot_count, -1), 'clus', split_axis...]
    ppermute x0 -> x4, waiting for transfers between devices: none -> 27 us  [spread_early(): lax.ppermute(leaving, 'clus', [(i, i ^ bit) for i in range(owners)])]
    ppermute x0 -> x4, starting transfers between devices: none -> 7.69 us  [spread_early(): lax.ppermute(leaving, 'clus', [(i, i ^ bit) for i in range(owners)])]
    pallas_call x1 -> x3, Pallas kernels: 9.24 us -> 15.2 us  [the longest x1 9.11 us: embed_late(): pl.pallas_call(functools.partial(late_kernel, slot_count), in_specs=[pl.B...]
    all_to_all x0 -> x1, starting transfers between devices: none -> 3.92 us  [per_device(): lax.all_to_all(packed.reshape(owners, slot_count, -1), 'clus', split_axis...]
  transfers between devices with their start and end apart: 0 -> 5, of which waited for: 0 -> 3; matrix products, arithmetic and copies ran while one was open for 0% -> 0% of each run, Pallas kernels for 0% -> 14%
where the time goes in v3:
time: 70.4 us; the launch traced here: 70 us
  waiting for transfers between devices  27 us (38%)
  Pallas kernels  19.5 us (28%)
  starting transfers between devices  11.6 us (16%)
  blocking collectives  10.9 us (15%)
  between operations  0.72 us (1%)
    ppermute x4, waiting for transfers between devices, spread_early(): lax.ppermute(leaving, 'clus', [(i, i ^ bit) for i in range(owners)])  27 us
    all_to_all x1, blocking collectives, per_device(): lax.all_to_all(message, 'clus', split_axis=0, concat_axis=0, tiled=True)  10.9 us
    pallas_call x1, Pallas kernels, embed_late(): pl.pallas_call(functools.partial(late_kernel, slot_count), in_specs=[pl.B...  9.11 us
    ppermute x4, starting transfers between devices, spread_early(): lax.ppermute(leaving, 'clus', [(i, i ^ bit) for i in range(owners)])  7.69 us
    pallas_call x1, Pallas kernels, embed_early(): pl.pallas_call(functools.partial(early_kernel, slot_count), in_specs=[pl....  5.34 us
    all_to_all x1, starting transfers between devices, per_device(): lax.all_to_all(packed.reshape(owners, slot_count, -1), 'clus', split_axis...  3.92 us
    pallas_call x1, Pallas kernels, scores(): pl.pallas_call(functools.partial(score_kernel, slot_count, half), out_spe...  2.7 us
    pallas_call x1, Pallas kernels, fetch(): pl.pallas_call(functools.partial(fetch_kernel, half), out_shape=(jax.Shap...  1.59 us
  transfers between devices with their start and end apart: 5, of which 3 were waited for; matrix products, arithmetic and copies ran while one was open for 0% of the time, Pallas kernels for 14%

profile of v3, /device:TPU:0, one launch (start us, length us, event | category | flops | bytes accessed | tf_op | source)
XLA Modules:
  0.0 70.0 jit_solution(17303895985836218553)
XLA Ops:
  0.6 5.3 %shard_map.67 = (bf16[320,384]{1,0:T(8,128)(2,1)}, bf16[320,384]{1,0:T(8,128)(2,1)}, s32[1,320]{1,0:T(1,128)}, bf16[320,4096]{1,0:T(8,128)(2,1)}) custom-call(bf16[320,4096]{1,0:T(8,128)(2,1)} %tokens_hbm.1, bf16[4096,1024]{1,0:T(8,128)(2,1)} %weight_hbm.3, s32[1,320]{1,0:T(1,128)} %bitcast.20, s32[320]{0:T(512)} %valid_ref.1), custom_call_target="tpu_custom_call" | custom-call | flops 1006632960 | bytes 5767168 | tf_op jit(solution)/shard_map/pallas_call | solution.py:91
  6.0 4.1 %collective-permute-start = (bf16[1,8,40,384]{3,2,0,1:T(8,128)(2,1)}, bf16[1,8,40,384]{3,2,0,1:T(8,128)(2,1)S(1)}, u32[]{:S(2)}, u32[]{:S(2)}) collective-permute-start(bf16[1,8,40,384]{3,2,0,1:T(8,128)(2,1)} %bitcast.23), channel_id=1, source_target_pairs={{0,8},{1,9},{2,10},{3,11},{4,12},{5,13},{6,14},{7,15},{8,0},{9,1},... | collective-permute-start | bytes 737288 | tf_op jit(solution)/shard_map/ppermute | solution.py:186
  10.1 0.0 copy-start
  10.1 9.1 %shard_map.69 = bf16[640,640]{1,0:T(8,128)(2,1)} custom-call(bf16[320,4096]{1,0:T(8,128)(2,1)} %get-tuple-element.13.tokens, bf16[4096,1024]{1,0:T(8,128)(2,1)} %weight_hbm.3, s32[1,320]{1,0:T(1,128)} %bitcast.21, s32[320]{0:T(512)} %valid_ref.1, s32[1,320]{1,0:T(1,128)} %get-tuple-element.14.rank_ref), custom_call_target="tpu_custom_call" | custom-call | flops 1677721600 | bytes 5242880 | tf_op jit(solution)/shard_map/pallas_call | solution.py:158
  19.2 3.9 %all-to-all-start = ((bf16[16,40,640]{2,1,0:T(8,128)(2,1)}), bf16[16,40,640]{2,1,0:T(8,128)(2,1)S(1)}, u32[]{:S(2)}, u32[]{:S(2)}) async-start(bf16[16,40,640]{2,1,0:T(8,128)(2,1)} %bitcast.17), calls=%async_computation | async-start | bytes 1638400 | tf_op jit(solution)/shard_map/all_to_all | solution.py:319
  23.1 0.0 collective-permute-done
  23.1 0.0 copy-done
  23.1 0.1 fusion.2
  23.2 2.0 %collective-permute-start.1 = (bf16[2,4,40,384]{3,2,0,1:T(8,128)(2,1)S(1)}, bf16[2,4,40,384]{3,2,0,1:T(8,128)(2,1)S(1)}, u32[]{:S(2)}, u32[]{:S(2)}) collective-permute-start(bf16[2,4,40,384]{3,2,0,1:T(8,128)(2,1)S(1)} %get-tuple-element.24), channel_id=1, source_target_pairs={{0,4},{1,5},{2,6},{3,7},{4,0},{5,1},{6,2},{7,3},{8,12},{9,13},{10,... | collective-permute-start | bytes 737288 | tf_op jit(solution)/shard_map/ppermute | solution.py:186
  25.2 19.5 %collective-permute-done.1 = bf16[2,4,40,384]{3,2,0,1:T(8,128)(2,1)S(1)} collective-permute-done((bf16[2,4,40,384]{3,2,0,1:T(8,128)(2,1)S(1)}, bf16[2,4,40,384]{3,2,0,1:T(8,128)(2,1)S(1)}, u32[]{:S(2)}, u32[]{:S(2)}) %collective-permute-start.1) | collective-permute-done | bytes 245792 | tf_op jit(solution)/shard_map/ppermute | solution.py:186
  44.7 0.1 fusion.1
  44.8 1.5 %collective-permute-start.2 = (bf16[4,2,40,384]{3,2,0,1:T(8,128)(2,1)S(1)}, bf16[4,2,40,384]{3,2,0,1:T(8,128)(2,1)S(1)}, u32[]{:S(2)}, u32[]{:S(2)}) collective-permute-start(bf16[4,2,40,384]{3,2,0,1:T(8,128)(2,1)S(1)} %get-tuple-element.22), channel_id=1, source_target_pairs={{0,2},{1,3},{2,0},{3,1},{4,6},{5,7},{6,4},{7,5},{8,10},{9,11},{10,... | collective-permute-start | bytes 737288 | tf_op jit(solution)/shard_map/ppermute | solution.py:186
  46.3 6.0 %collective-permute-done.2 = bf16[4,2,40,384]{3,2,0,1:T(8,128)(2,1)S(1)} collective-permute-done((bf16[4,2,40,384]{3,2,0,1:T(8,128)(2,1)S(1)}, bf16[4,2,40,384]{3,2,0,1:T(8,128)(2,1)S(1)}, u32[]{:S(2)}, u32[]{:S(2)}) %collective-permute-start.2) | collective-permute-done | bytes 245792 | tf_op jit(solution)/shard_map/ppermute | solution.py:186
  52.3 0.1 fusion
  52.4 0.1 collective-permute-start.3
  52.5 1.5 %collective-permute-done.3 = bf16[8,1,40,384]{3,2,0,1:T(8,128)(2,1)S(1)} collective-permute-done((bf16[8,1,40,384]{3,2,0,1:T(8,128)(2,1)S(1)}, bf16[8,1,40,384]{3,2,0,1:T(8,128)(2,1)S(1)}, u32[]{:S(2)}, u32[]{:S(2)}) %collective-permute-start.3) | collective-permute-done | bytes 245792 | tf_op jit(solution)/shard_map/ppermute | solution.py:186
  54.0 0.1 pad_maximum_fusion
  54.0 0.8 %shard_map.68.early_ref = bf16[640,384]{1,0:T(8,128)(2,1)S(1)} custom-call(bf16[640,384]{1,0:T(8,128)(2,1)S(1)} %bitcast.15), custom_call_target="tpu_custom_call" | custom-call | flops 2000000000 | bytes 983040 | tf_op jit(solution)/shard_map/pallas_call | solution.py:212
  54.8 0.0 all-to-all-done
  54.8 2.7 %shard_map.70 = (f32[16,128]{1,0:T(8,128)S(1)}, f32[1,640,640]{2,1,0:T(8,128)}) custom-call(bf16[640,384]{1,0:T(8,128)(2,1)S(1)} %shard_map.68.early_ref, bf16[640,640]{1,0:T(8,128)(2,1)S(1)} %bitcast.14), custom_call_target="tpu_custom_call" | custom-call | tf_op jit(solution)/shard_map/pallas_call | solution.py:272
  57.5 10.9 %all_to_all.16 = f32[16,1,128]{2,1,0:T(1,128)} all-to-all(f32[16,1,128]{2,1,0:T(1,128)S(1)} %bitcast.16), channel_id=1, replica_groups=mesh['groups'=2,'clus'=16] {'clus'}, dimensions={0} | all-to-all | bytes 16384 | tf_op jit(solution)/shard_map/all_to_all | solution.py:324
  68.4 1.6 %shard_map.71 = (f32[320]{0:T(512)}, f32[320]{0:T(512)}) custom-call(f32[16,128]{1,0:T(8,128)} %bitcast.19, s32[1,320]{1,0:T(1,128)} %bitcast.22, s32[1,320]{1,0:T(1,128)} %get-tuple-element.14.rank_ref, s32[320]{0:T(512)} %valid_ref.1), custom_call_target="tpu_custom_call" | custom-call | tf_op jit(solution)/shard_map/pallas_call | solution.py:301
Async XLA Ops:
  6.0 17.2 %collective-permute-start = (bf16[1,8,40,384]{3,2,0,1:T(8,128)(2,1)}, bf16[1,8,40,384]{3,2,0,1:T(8,128)(2,1)S(1)}, u32[]{:S(2)}, u32[]{:S(2)}) collective-permute-start(bf16[1,8,40,384]{3,2,0,1:T(8,128)(2,1)} %bitcast.23), channel_id=1, source_target_pairs={{0,8},{1,9},{2,10},{3,11},{4,12},{5,13},{6,14},{7,15},{8,0},{9,1},... | collective-permute-start | bytes 737288 | tf_op jit(solution)/shard_map/ppermute | solution.py:186
  10.1 13.1 %copy-start = (bf16[320,384]{1,0:T(8,128)(2,1)S(1)}, bf16[320,384]{1,0:T(8,128)(2,1)}, u32[]{:S(2)}) copy-start(bf16[320,384]{1,0:T(8,128)(2,1)} %get-tuple-element.11) | copy-start | bytes 737284
  19.2 35.6 %all-to-all-start = ((bf16[16,40,640]{2,1,0:T(8,128)(2,1)}), bf16[16,40,640]{2,1,0:T(8,128)(2,1)S(1)}, u32[]{:S(2)}, u32[]{:S(2)}) async-start(bf16[16,40,640]{2,1,0:T(8,128)(2,1)} %bitcast.17), calls=%async_computation | async-start | bytes 1638400 | tf_op jit(solution)/shard_map/all_to_all | solution.py:319
  23.2 21.5 %collective-permute-start.1 = (bf16[2,4,40,384]{3,2,0,1:T(8,128)(2,1)S(1)}, bf16[2,4,40,384]{3,2,0,1:T(8,128)(2,1)S(1)}, u32[]{:S(2)}, u32[]{:S(2)}) collective-permute-start(bf16[2,4,40,384]{3,2,0,1:T(8,128)(2,1)S(1)} %get-tuple-element.24), channel_id=1, source_target_pairs={{0,4},{1,5},{2,6},{3,7},{4,0},{5,1},{6,2},{7,3},{8,12},{9,13},{10,... | collective-permute-start | bytes 737288 | tf_op jit(solution)/shard_map/ppermute | solution.py:186
  44.8 7.6 %collective-permute-start.2 = (bf16[4,2,40,384]{3,2,0,1:T(8,128)(2,1)S(1)}, bf16[4,2,40,384]{3,2,0,1:T(8,128)(2,1)S(1)}, u32[]{:S(2)}, u32[]{:S(2)}) collective-permute-start(bf16[4,2,40,384]{3,2,0,1:T(8,128)(2,1)S(1)} %get-tuple-element.22), channel_id=1, source_target_pairs={{0,2},{1,3},{2,0},{3,1},{4,6},{5,7},{6,4},{7,5},{8,10},{9,11},{10,... | collective-permute-start | bytes 737288 | tf_op jit(solution)/shard_map/ppermute | solution.py:186
  52.4 1.6 %collective-permute-start.3 = (bf16[8,1,40,384]{3,2,0,1:T(8,128)(2,1)S(1)}, bf16[8,1,40,384]{3,2,0,1:T(8,128)(2,1)S(1)}, u32[]{:S(2)}, u32[]{:S(2)}) collective-permute-start(bf16[8,1,40,384]{3,2,0,1:T(8,128)(2,1)S(1)} %get-tuple-element.20), channel_id=1, source_target_pairs={{0,1},{1,0},{2,3},{3,2},{4,5},{5,4},{6,7},{7,6},{8,9},{9,8},{10,11... | collective-permute-start | bytes 737288 | tf_op jit(solution)/shard_map/ppermute | solution.py:186

commit v4 on v2

--- a/solution.py
+++ b/solution.py
@@ -11,6 +11,8 @@
 BF16 = jnp.bfloat16
 VMEM_BYTES = 48 * 1024 * 1024
 EMBED_VMEM_BYTES = 60 * 1024 * 1024
+EARLY = 1
+ORDER_FLOPS = 15000000000
 
 
 def split3(x):
@@ -21,25 +23,38 @@
     return hi, mid, low
 
 
-def place_rows(label_row, valid_row, slot_count, width_all):
+def rank_rows(label_row):
     rows = label_row.shape[1]
     label = label_row.astype(F32)
     below = lax.broadcasted_iota(jnp.int32, (rows, rows), 0)
     across = lax.broadcasted_iota(jnp.int32, (rows, rows), 1)
     label_col = jnp.sum(jnp.where(below == across, label, 0.0), axis=1, keepdims=True)
     earlier = (label_col == label) & (below < across)
-    rank = jnp.sum(jnp.where(earlier, 1.0, 0.0), axis=0, keepdims=True).astype(jnp.int32)
-    slot = jnp.where(valid_row > 0, label_row * slot_count + rank, -1)
-    slots = lax.broadcasted_iota(jnp.int32, (width_all, rows), 0)
-    return rank, jnp.where(slots == slot, 1.0, 0.0).astype(BF16)
+    return jnp.sum(jnp.where(earlier, 1.0, 0.0), axis=0, keepdims=True).astype(jnp.int32)
+
+
+def place_rows(slot_row, valid_row, width_all):
+    slots = lax.broadcasted_iota(jnp.int32, (width_all, slot_row.shape[1]), 0)
+    slot = jnp.where(valid_row > 0, slot_row, -1)
+    return jnp.where(slots == slot, 1.0, 0.0).astype(BF16)
+
+
+def exchange_bits(owners):
+    bits = []
+    bit = owners // 2
+    while bit:
+        bits.append(bit)
+        bit //= 2
+    return bits[:1] + bits[2:] + bits[1:2]
 
 
 def embed_kernel(
-    slot_count, tokens_hbm, weight_hbm, label_hbm, valid_hbm, packed_ref, rank_ref,
-    tokens, weight, total, place, label_ref, valid_ref, token_sem, weight_sem, small_sem,
+    slot_count, bits, tokens_hbm, weight_hbm, label_hbm, valid_hbm, keep_ref, send_ref, packed_ref, rank_ref,
+    tokens, weight, total, place, apart, label_ref, valid_ref, token_sem, weight_sem, small_sem,
 ):
     steps = token_sem.shape[0]
     block = tokens.shape[1] // steps
+    early = keep_ref.shape[1]
     small = (
         pltpu.make_async_copy(label_hbm, label_ref, small_sem.at[0]),
         pltpu.make_async_copy(valid_hbm, valid_ref, small_sem.at[1]),
@@ -49,21 +64,30 @@
     copies = []
     for k in range(steps):
         part = slice(k * block, (k + 1) * block)
-        pair = (
+        copies.append((
             pltpu.make_async_copy(tokens_hbm.at[:, part], tokens.at[:, part], token_sem.at[k]),
             pltpu.make_async_copy(weight_hbm.at[part, :], weight.at[part, :], weight_sem.at[k]),
-        )
+        ))
+    for pair in copies[:2]:
         for copy in pair:
             copy.start()
-        copies.append(pair)
     for copy in small:
         copy.wait()
-    rank, chosen = place_rows(label_ref[...], valid_ref[...].reshape(label_ref.shape), slot_count, place.shape[0])
+    label = label_ref[...]
+    valid = valid_ref[...].reshape(label.shape)
+    rank = rank_rows(label)
     rank_ref[...] = rank
-    place[...] = chosen
+    place[...] = place_rows(label * slot_count + rank, valid, place.shape[0])
+    distance = label ^ lax.axis_index("clus")
+    position = jnp.zeros_like(label)
+    for k, bit in enumerate(bits):
+        position += jnp.where((distance & bit) > 0, 1 << (len(bits) - 1 - k), 0)
+    apart[...] = place_rows(position * slot_count + rank, valid, place.shape[0])
     for k, pair in enumerate(copies):
         for copy in pair:
             copy.wait()
+        for copy in (copies[k + 2] if k + 2 < steps else ()):
+            copy.start()
         part = slice(k * block, (k + 1) * block)
         product = jnp.dot(tokens[:, part], weight[part, :], preferred_element_type=F32)
         if k == 0:
@@ -72,26 +96,33 @@
             total[...] += product
     embed = total[...]
     scale = lax.rsqrt(jnp.sum(embed * embed, axis=1, keepdims=True) + 1e-06)
-    unit = (embed * scale).astype(BF16)
+    near = keep_ref.shape[0]
+    unit = (total[:, :early] * scale).astype(BF16)
+    send_ref[...] = jnp.dot(apart[near:, :], unit, preferred_element_type=F32).astype(BF16)
+    keep_ref[...] = jnp.dot(apart[:near, :], unit, preferred_element_type=F32).astype(BF16)
+    unit = (total[:, early:] * scale).astype(BF16)
     packed_ref[...] = jnp.dot(place[...], unit, preferred_element_type=F32).astype(BF16)
 
 
-def embed_and_pack(tokens, weight, label_row, valid, owners, slot_count):
+def embed_and_pack(tokens, weight, label_row, valid, owners, slot_count, early):
     rows, depth = tokens.shape
     width = weight.shape[1]
-    steps = 8 if depth % 1024 == 0 else 1
+    steps = 4 if depth % 512 == 0 else 1
     width_all = owners * slot_count
     return pl.pallas_call(
-        functools.partial(embed_kernel, slot_count),
+        functools.partial(embed_kernel, slot_count, exchange_bits(owners)),
         in_specs=[pl.BlockSpec(memory_space=pltpu.HBM)] * 4,
         out_shape=(
-            jax.ShapeDtypeStruct((width_all, width), BF16),
+            jax.ShapeDtypeStruct((width_all // 2, early), BF16),
+            jax.ShapeDtypeStruct((width_all // 2, early), BF16),
+            jax.ShapeDtypeStruct((width_all, width - early), BF16),
             jax.ShapeDtypeStruct((1, rows), jnp.int32),
         ),
         scratch_shapes=[
             pltpu.VMEM((rows, depth), BF16),
             pltpu.VMEM((depth, width), BF16),
             pltpu.VMEM((rows, width), F32),
+            pltpu.VMEM((width_all, rows), BF16),
             pltpu.VMEM((width_all, rows), BF16),
             pltpu.VMEM((1, rows), jnp.int32),
             pltpu.VMEM((rows,), jnp.int32),
@@ -106,21 +137,57 @@
     )(tokens, weight, label_row, valid)
 
 
-def score_kernel(slot_count, half, members_ref, message_ref, similar_hbm, gram, sem):
-    width_all = members_ref.shape[0]
+def spread_early(keep, send, owners, slot_count):
+    early = keep.shape[1]
+    left = owners // 2
+    held = keep.reshape(1, left, slot_count, early)
+    leaving = send.reshape(1, left, slot_count, early)
+    for bit in exchange_bits(owners):
+        arrived = lax.ppermute(leaving, "clus", [(i, i ^ bit) for i in range(owners)])
+        both = jnp.concatenate([held, arrived], axis=0)
+        left //= 2
+        held, leaving = both[:, :left], both[:, left:]
+    return both.reshape(owners * slot_count, early)
+
+
+def order_kernel(slot_count, bits, relative_ref, members_ref):
+    width_all = relative_ref.shape[0]
+    member = lax.broadcasted_iota(jnp.int32, (width_all, 1), 0)
+    source = member // slot_count
+    distance = source ^ lax.axis_index("clus")
+    index = jnp.zeros_like(distance)
+    for k, bit in enumerate(bits):
+        index += jnp.where((distance & bit) > 0, 1 << k, 0)
+    wanted = index * slot_count + member - source * slot_count
+    held = lax.broadcasted_iota(jnp.int32, (width_all, width_all), 1)
+    chosen = jnp.where(held == wanted, 1.0, 0.0).astype(BF16)
+    members_ref[...] = jnp.dot(chosen, relative_ref[...], preferred_element_type=F32).astype(BF16)
+
+
+def order_early(relative, owners, slot_count):
+    return pl.pallas_call(
+        functools.partial(order_kernel, slot_count, exchange_bits(owners)),
+        out_shape=jax.ShapeDtypeStruct(relative.shape, BF16),
+        compiler_params=pltpu.CompilerParams(vmem_limit_bytes=VMEM_BYTES),
+        cost_estimate=pl.CostEstimate(flops=ORDER_FLOPS, bytes_accessed=4 * relative.size, transcendentals=0),
+    )(relative)
+
+
+def score_kernel(slot_count, half, early_ref, late_ref, message_ref, similar_hbm, gram, sem):
+    width_all = early_ref.shape[0]
+    transposed = (((1,), (1,)), ((), ()))
     owners, lanes = message_ref.shape
     block = width_all // 2
     copies = []
     nears, sums = [], []
     for b in range(2):
         part = slice(b * block, (b + 1) * block)
-        gram[part, :] = lax.dot_general(
-            members_ref[part, :], members_ref[...], (((1,), (1,)), ((), ())), preferred_element_type=F32
-        )
+        tile = lax.dot_general(early_ref[part, :], early_ref[...], transposed, preferred_element_type=F32)
+        tile += lax.dot_general(late_ref[part, :], late_ref[...], transposed, preferred_element_type=F32)
+        gram[part, :] = tile
         copy = pltpu.make_async_copy(gram.at[part, :], similar_hbm.at[0, part, :], sem.at[b])
         copy.start()
         copies.append(copy)
-        tile = gram[part, :]
         own = lax.broadcasted_iota(jnp.int32, (block, width_all), 0) + b * block
         other = lax.broadcasted_iota(jnp.int32, (block, width_all), 1)
         nears.append(jnp.max(jnp.where(own == other, 0.0, tile), axis=1, keepdims=True))
@@ -144,8 +211,8 @@
         copy.wait()
 
 
-def scores(members, owners, slot_count, half):
-    width_all, width = members.shape
+def scores(early, late, owners, slot_count, half):
+    width_all = early.shape[0]
     return pl.pallas_call(
         functools.partial(score_kernel, slot_count, half),
         out_specs=(pl.BlockSpec(memory_space=pltpu.VMEM), pl.BlockSpec(memory_space=pltpu.HBM)),
@@ -155,7 +222,7 @@
         ),
         scratch_shapes=[pltpu.VMEM((width_all, width_all), F32), pltpu.SemaphoreType.DMA((2,))],
         compiler_params=pltpu.CompilerParams(vmem_limit_bytes=VMEM_BYTES),
-    )(members)
+    )(early, late)
 
 
 def fetch_kernel(half, message_ref, label_ref, rank_ref, valid_ref, near_ref, dist_ref):
@@ -187,13 +254,16 @@
     slot_count = 2 * row_count // owners
     width_all = owners * slot_count
     half = -(-slot_count // 64) * 64
+    early = EARLY * proj_weight.shape[1] // 8
     label_row = labels.reshape(1, row_count)
-    packed, rank_row = embed_and_pack(tokens, proj_weight, label_row, valid_rows, owners, slot_count)
+    keep, send, packed, rank_row = embed_and_pack(
+        tokens, proj_weight, label_row, valid_rows, owners, slot_count, early
+    )
     arrived = lax.all_to_all(
         packed.reshape(owners, slot_count, -1), "clus", split_axis=0, concat_axis=0, tiled=True
     )
-    members = arrived.reshape(width_all, -1)
-    message, similar = scores(members, owners, slot_count, half)
+    early_members = order_early(spread_early(keep, send, owners, slot_count), owners, slot_count)
+    message, similar = scores(early_members, arrived.reshape(width_all, -1), owners, slot_count, half)
     returned = lax.all_to_all(message, "clus", split_axis=0, concat_axis=0, tiled=True)
     nearest, centre_dist = fetch(returned, label_row, rank_row, valid_rows, half)
     return (similar, nearest, centre_dist)

time: 63.2 us -> 58.9 us (0.932)
  blocking collectives: 49.2 us -> 13.2 us
  waiting for transfers between devices: 0 us -> 22.4 us
  starting transfers between devices: 0 us -> 9.92 us
  Pallas kernels: 13.1 us -> 12.3 us
    all_to_all x1 -> x0, blocking collectives: 38.9 us -> none  [per_device(): lax.all_to_all(packed.reshape(owners, slot_count, -1), 'clus', split_axis...]
    ppermute x0 -> x4, waiting for transfers between devices: none -> 19.5 us  [spread_early(): lax.ppermute(leaving, 'clus', [(i, i ^ bit) for i in range(owners)])]
    ppermute x0 -> x4, starting transfers between devices: none -> 6.01 us  [spread_early(): lax.ppermute(leaving, 'clus', [(i, i ^ bit) for i in range(owners)])]
    all_to_all x0 -> x1, starting transfers between devices: none -> 3.91 us  [per_device(): lax.all_to_all(packed.reshape(owners, slot_count, -1), 'clus', split_axis...]
    all_to_all x1, blocking collectives: 10.3 us -> 13.2 us  [per_device(): lax.all_to_all(message, 'clus', split_axis=0, concat_axis=0, tiled=True)]
    all_to_all x0 -> x1, waiting for transfers between devices: none -> 2.89 us  [per_device(): lax.all_to_all(packed.reshape(owners, slot_count, -1), 'clus', split_axis...]
    pallas_call x1 -> x2, Pallas kernels: 9.24 us -> 8.28 us  [the longest x1 7.74 us: embed_and_pack(): pl.pallas_call(functools.partial(embed_kernel, slot_count, exchange_bits(...]
  transfers between devices with their start and end apart: 0 -> 5, of which waited for: 0 -> 5; matrix products, arithmetic and copies ran while one was open for 0% -> 0% of each run, Pallas kernels for 0% -> 1%
where the time goes in v4:
time: 58.9 us; the launch traced here: 58.6 us
  waiting for transfers between devices  22.4 us (38%)
  blocking collectives  13.2 us (22%)
  Pallas kernels  12.3 us (21%)
  starting transfers between devices  9.92 us (17%)
  between operations  0.7 us (1%)
    ppermute x4, waiting for transfers between devices, spread_early(): lax.ppermute(leaving, 'clus', [(i, i ^ bit) for i in range(owners)])  19.5 us
    all_to_all x1, blocking collectives, per_device(): lax.all_to_all(message, 'clus', split_axis=0, concat_axis=0, tiled=True)  13.2 us
    pallas_call x1, Pallas kernels, embed_and_pack(): pl.pallas_call(functools.partial(embed_kernel, slot_count, exchange_bits(...  7.74 us
    ppermute x4, starting transfers between devices, spread_early(): lax.ppermute(leaving, 'clus', [(i, i ^ bit) for i in range(owners)])  6.01 us
    all_to_all x1, starting transfers between devices, per_device(): lax.all_to_all(packed.reshape(owners, slot_count, -1), 'clus', split_axis...  3.91 us
    all_to_all x1, waiting for transfers between devices, per_device(): lax.all_to_all(packed.reshape(owners, slot_count, -1), 'clus', split_axis...  2.89 us
    pallas_call x1, Pallas kernels, scores(): pl.pallas_call(functools.partial(score_kernel, slot_count, half), out_spe...  2.4 us
    pallas_call x1, Pallas kernels, fetch(): pl.pallas_call(functools.partial(fetch_kernel, half), out_shape=(jax.Shap...  1.59 us
  transfers between devices with their start and end apart: 5, of which 5 were waited for; matrix products, arithmetic and copies ran while one was open for 0% of the time, Pallas kernels for 1%

profile of v4, /device:TPU:0, one launch (start us, length us, event | category | flops | bytes accessed | tf_op | source)
XLA Modules:
  0.0 58.6 jit_solution(16224374280380070112)
XLA Ops:
  0.6 7.7 %shard_map.67 = (bf16[320,128]{1,0:T(8,128)(2,1)}, bf16[320,128]{1,0:T(8,128)(2,1)}, bf16[640,896]{1,0:T(8,128)(2,1)}, s32[1,320]{1,0:T(1,128)}) custom-call(bf16[320,4096]{1,0:T(8,128)(2,1)} %tokens_hbm.1, bf16[4096,1024]{1,0:T(8,128)(2,1)} %weight_hbm.1, s32[1,320]{1,0:T(1,128)} %bitcast.20, s32[320]{0:T(512)} %valid_ref.1), custom_call_target="tpu_custom_call" | custom-call | flops 2684354560 | bytes 11010048 | tf_op jit(solution)/shard_map/pallas_call | solution.py:112
  8.4 0.0 copy-start
  8.4 4.1 %collective-permute-start = (bf16[1,8,40,128]{3,2,0,1:T(8,128)(2,1)}, bf16[1,8,40,128]{3,2,0,1:T(8,128)(2,1)S(1)}, u32[]{:S(2)}, u32[]{:S(2)}) collective-permute-start(bf16[1,8,40,128]{3,2,0,1:T(8,128)(2,1)} %bitcast.22), channel_id=1, source_target_pairs={{0,8},{1,9},{2,10},{3,11},{4,12},{5,13},{6,14},{7,15},{8,0},{9,1},... | collective-permute-start | bytes 245768 | tf_op jit(solution)/shard_map/ppermute | solution.py:146
  12.5 3.9 %all-to-all-start = ((bf16[16,40,896]{2,1,0:T(8,128)(2,1)}), bf16[16,40,896]{2,1,0:T(8,128)(2,1)S(1)}, u32[]{:S(2)}, u32[]{:S(2)}) async-start(bf16[16,40,896]{2,1,0:T(8,128)(2,1)} %bitcast.17), calls=%async_computation | async-start | bytes 2293760 | tf_op jit(solution)/shard_map/all_to_all | solution.py:262
  16.4 0.5 collective-permute-done
  16.9 0.0 copy-done
  16.9 1.8 %collective-permute-start.1 = (bf16[2,4,40,128]{3,2,0,1:T(8,128)(2,1)S(1)}, bf16[2,4,40,128]{3,2,0,1:T(8,128)(2,1)S(1)}, u32[]{:S(2)}, u32[]{:S(2)}) collective-permute-start(bf16[2,4,40,128]{3,2,0,1:T(8,128)(2,1)S(1)} %get-tuple-element.24), channel_id=1, source_target_pairs={{0,2},{1,3},{2,0},{3,1},{4,6},{5,7},{6,4},{7,5},{8,10},{9,11},{10,... | collective-permute-start | bytes 245768 | tf_op jit(solution)/shard_map/ppermute | solution.py:146
  18.7 9.8 %collective-permute-done.1 = bf16[2,4,40,128]{3,2,0,1:T(8,128)(2,1)S(1)} collective-permute-done((bf16[2,4,40,128]{3,2,0,1:T(8,128)(2,1)S(1)}, bf16[2,4,40,128]{3,2,0,1:T(8,128)(2,1)S(1)}, u32[]{:S(2)}, u32[]{:S(2)}) %collective-permute-start.1) | collective-permute-done | bytes 81952 | tf_op jit(solution)/shard_map/ppermute | solution.py:146
  28.5 0.1 collective-permute-start.2
  28.6 1.3 %collective-permute-done.2 = bf16[4,2,40,128]{3,2,0,1:T(8,128)(2,1)S(1)} collective-permute-done((bf16[4,2,40,128]{3,2,0,1:T(8,128)(2,1)S(1)}, bf16[4,2,40,128]{3,2,0,1:T(8,128)(2,1)S(1)}, u32[]{:S(2)}, u32[]{:S(2)}) %collective-permute-start.2) | collective-permute-done | bytes 81952 | tf_op jit(solution)/shard_map/ppermute | solution.py:146
  29.9 0.1 collective-permute-start.3
  29.9 7.9 %collective-permute-done.3 = bf16[8,1,40,128]{3,2,0,1:T(8,128)(2,1)S(1)} collective-permute-done((bf16[8,1,40,128]{3,2,0,1:T(8,128)(2,1)S(1)}, bf16[8,1,40,128]{3,2,0,1:T(8,128)(2,1)S(1)}, u32[]{:S(2)}, u32[]{:S(2)}) %collective-permute-start.3) | collective-permute-done | bytes 81952 | tf_op jit(solution)/shard_map/ppermute | solution.py:146
  37.9 0.5 shard_map.68.early_ref
  38.4 2.9 %all-to-all-done = bf16[16,40,896]{2,1,0:T(8,128)(2,1)S(1)} async-done(((bf16[16,40,896]{2,1,0:T(8,128)(2,1)}), bf16[16,40,896]{2,1,0:T(8,128)(2,1)S(1)}, u32[]{:S(2)}, u32[]{:S(2)}) %all-to-all-start) | async-done | bytes 1146912 | tf_op jit(solution)/shard_map/all_to_all | solution.py:262
  41.3 2.4 %shard_map.69 = (f32[16,128]{1,0:T(8,128)S(1)}, f32[1,640,640]{2,1,0:T(8,128)}) custom-call(bf16[640,128]{1,0:T(8,128)(2,1)S(1)} %shard_map.68.early_ref, bf16[640,896]{1,0:T(8,128)(2,1)S(1)} %bitcast.14), custom_call_target="tpu_custom_call" | custom-call | tf_op jit(solution)/shard_map/pallas_call | solution.py:216
  43.7 13.2 %all_to_all.16 = f32[16,1,128]{2,1,0:T(1,128)} all-to-all(f32[16,1,128]{2,1,0:T(1,128)S(1)} %bitcast.16), channel_id=1, replica_groups=mesh['groups'=2,'clus'=16] {'clus'}, dimensions={0} | all-to-all | bytes 16384 | tf_op jit(solution)/shard_map/all_to_all | solution.py:267
  57.0 1.6 %shard_map.70 = (f32[320]{0:T(512)}, f32[320]{0:T(512)}) custom-call(f32[16,128]{1,0:T(8,128)} %bitcast.19, s32[1,320]{1,0:T(1,128)} %bitcast.21, s32[1,320]{1,0:T(1,128)} %get-tuple-element.16.rank_ref, s32[320]{0:T(512)} %valid_ref.1), custom_call_target="tpu_custom_call" | custom-call | tf_op jit(solution)/shard_map/pallas_call | solution.py:245
  (4 shorter events, 0.1 us)
Async XLA Ops:
  8.4 8.5 %copy-start = (bf16[320,128]{1,0:T(8,128)(2,1)S(1)}, bf16[320,128]{1,0:T(8,128)(2,1)}, u32[]{:S(2)}) copy-start(bf16[320,128]{1,0:T(8,128)(2,1)} %get-tuple-element.11) | copy-start | bytes 245764
  8.4 8.5 %collective-permute-start = (bf16[1,8,40,128]{3,2,0,1:T(8,128)(2,1)}, bf16[1,8,40,128]{3,2,0,1:T(8,128)(2,1)S(1)}, u32[]{:S(2)}, u32[]{:S(2)}) collective-permute-start(bf16[1,8,40,128]{3,2,0,1:T(8,128)(2,1)} %bitcast.22), channel_id=1, source_target_pairs={{0,8},{1,9},{2,10},{3,11},{4,12},{5,13},{6,14},{7,15},{8,0},{9,1},... | collective-permute-start | bytes 245768 | tf_op jit(solution)/shard_map/ppermute | solution.py:146
  12.5 28.8 %all-to-all-start = ((bf16[16,40,896]{2,1,0:T(8,128)(2,1)}), bf16[16,40,896]{2,1,0:T(8,128)(2,1)S(1)}, u32[]{:S(2)}, u32[]{:S(2)}) async-start(bf16[16,40,896]{2,1,0:T(8,128)(2,1)} %bitcast.17), calls=%async_computation | async-start | bytes 2293760 | tf_op jit(solution)/shard_map/all_to_all | solution.py:262
  16.9 11.6 %collective-permute-start.1 = (bf16[2,4,40,128]{3,2,0,1:T(8,128)(2,1)S(1)}, bf16[2,4,40,128]{3,2,0,1:T(8,128)(2,1)S(1)}, u32[]{:S(2)}, u32[]{:S(2)}) collective-permute-start(bf16[2,4,40,128]{3,2,0,1:T(8,128)(2,1)S(1)} %get-tuple-element.24), channel_id=1, source_target_pairs={{0,2},{1,3},{2,0},{3,1},{4,6},{5,7},{6,4},{7,5},{8,10},{9,11},{10,... | collective-permute-start | bytes 245768 | tf_op jit(solution)/shard_map/ppermute | solution.py:146
  28.5 1.3 %collective-permute-start.2 = (bf16[4,2,40,128]{3,2,0,1:T(8,128)(2,1)S(1)}, bf16[4,2,40,128]{3,2,0,1:T(8,128)(2,1)S(1)}, u32[]{:S(2)}, u32[]{:S(2)}) collective-permute-start(bf16[4,2,40,128]{3,2,0,1:T(8,128)(2,1)S(1)} %get-tuple-element.22), channel_id=1, source_target_pairs={{0,1},{1,0},{2,3},{3,2},{4,5},{5,4},{6,7},{7,6},{8,9},{9,8},{10,11... | collective-permute-start | bytes 245768 | tf_op jit(solution)/shard_map/ppermute | solution.py:146
  29.9 8.0 %collective-permute-start.3 = (bf16[8,1,40,128]{3,2,0,1:T(8,128)(2,1)S(1)}, bf16[8,1,40,128]{3,2,0,1:T(8,128)(2,1)S(1)}, u32[]{:S(2)}, u32[]{:S(2)}) collective-permute-start(bf16[8,1,40,128]{3,2,0,1:T(8,128)(2,1)S(1)} %get-tuple-element.20), channel_id=1, source_target_pairs={{0,4},{1,5},{2,6},{3,7},{4,0},{5,1},{6,2},{7,3},{8,12},{9,13},{10,... | collective-permute-start | bytes 245768 | tf_op jit(solution)/shard_map/ppermute | solution.py:146

commit v5 on v4

--- a/solution.py
+++ b/solution.py
@@ -11,8 +11,9 @@
 BF16 = jnp.bfloat16
 VMEM_BYTES = 48 * 1024 * 1024
 EMBED_VMEM_BYTES = 60 * 1024 * 1024
-EARLY = 1
-ORDER_FLOPS = 15000000000
+FETCH_VMEM_BYTES = 8 * 1024 * 1024
+EARLY = 2
+ORDER_FLOPS = 13 * 10**9
 
 
 def split3(x):
@@ -40,12 +41,12 @@
 
 
 def exchange_bits(owners):
-    bits = []
-    bit = owners // 2
-    while bit:
-        bits.append(bit)
-        bit //= 2
-    return bits[:1] + bits[2:] + bits[1:2]
+    middle = []
+    bit = 1
+    while bit < owners // 8:
+        middle.append(bit)
+        bit *= 2
+    return [owners // 2] + middle + [owners // 8, owners // 4]
 
 
 def embed_kernel(
@@ -139,15 +140,20 @@
 
 def spread_early(keep, send, owners, slot_count):
     early = keep.shape[1]
+    *bits, low, high = exchange_bits(owners)
     left = owners // 2
     held = keep.reshape(1, left, slot_count, early)
     leaving = send.reshape(1, left, slot_count, early)
-    for bit in exchange_bits(owners):
+    for bit in bits:
         arrived = lax.ppermute(leaving, "clus", [(i, i ^ bit) for i in range(owners)])
         both = jnp.concatenate([held, arrived], axis=0)
         left //= 2
         held, leaving = both[:, :left], both[:, left:]
-    return both.reshape(owners * slot_count, early)
+    blocks = [both[:, k] for k in range(4)]
+    parts = [blocks[0]]
+    for block, mask in ((blocks[2], low), (blocks[1], high), (blocks[3], low | high)):
+        parts.append(lax.ppermute(block, "clus", [(i, i ^ mask) for i in range(owners)]))
+    return jnp.concatenate(parts, axis=0).reshape(owners * slot_count, early)
 
 
 def order_kernel(slot_count, bits, relative_ref, members_ref):
@@ -190,22 +196,23 @@
         copies.append(copy)
         own = lax.broadcasted_iota(jnp.int32, (block, width_all), 0) + b * block
         other = lax.broadcasted_iota(jnp.int32, (block, width_all), 1)
-        nears.append(jnp.max(jnp.where(own == other, 0.0, tile), axis=1, keepdims=True))
-        sums.append(jnp.sum(tile, axis=1, keepdims=True))
-    near = jnp.concatenate(nears, axis=0)
-    sums = jnp.concatenate(sums, axis=0)
-    square = jnp.maximum(jnp.sum(sums, axis=0, keepdims=True), 0.0)
-    dist = 1.0 - sums * lax.rsqrt(square + 1e-06)
+        nears.append(jnp.max(jnp.where(own == other, 0.0, tile), axis=0, keepdims=True))
+        sums.append(jnp.sum(tile, axis=0, keepdims=True))
+    near = jnp.maximum(nears[0], nears[1])
+    total = sums[0] + sums[1]
+    square = jnp.maximum(jnp.sum(total, axis=1, keepdims=True), 0.0)
+    dist = 1.0 - total * lax.rsqrt(square + 1e-06)
     slot = lax.broadcasted_iota(jnp.int32, (width_all, lanes), 0)
     within = slot - (slot // slot_count) * slot_count
     lane = lax.broadcasted_iota(jnp.int32, (width_all, lanes), 1)
-    spread = jnp.where(lane == within, near, jnp.where(lane == within + half, dist, 0.0))
     source = lax.broadcasted_iota(jnp.int32, (owners, width_all), 0) * slot_count
     member = lax.broadcasted_iota(jnp.int32, (owners, width_all), 1)
-    chosen = jnp.where((member >= source) & (member < source + slot_count), 1.0, 0.0).astype(BF16)
+    mine = (member >= source) & (member < source + slot_count)
     out = jnp.zeros((owners, lanes), F32)
-    for piece in split3(spread):
-        out += jnp.dot(chosen, piece, preferred_element_type=F32)
+    for values, start in ((near, 0), (dist, half)):
+        chosen = jnp.where(lane == within + start, 1.0, 0.0).astype(BF16)
+        for piece in split3(jnp.where(mine, values, 0.0)):
+            out += jnp.dot(piece, chosen, preferred_element_type=F32)
     message_ref[...] = out
     for copy in copies:
         copy.wait()
@@ -245,6 +252,7 @@
     return pl.pallas_call(
         functools.partial(fetch_kernel, half),
         out_shape=(jax.ShapeDtypeStruct((rows,), F32),) * 2,
+        compiler_params=pltpu.CompilerParams(vmem_limit_bytes=FETCH_VMEM_BYTES),
     )(message, label_row, rank_row, valid)
 
 

time: 58.9 us -> 57.4 us (0.975)
  waiting for transfers between devices: 22.4 us -> 14.6 us
  starting transfers between devices: 9.92 us -> 15.8 us
  Pallas kernels: 12.3 us -> 11.2 us
  other arithmetic: 0.07 us -> 1.03 us
  blocking collectives: 13.2 us -> 13.8 us
    ppermute x4 -> x2, waiting for transfers between devices: 19.5 us -> 5.47 us  [spread_early(): lax.ppermute(leaving, 'clus', [(i, i ^ bit) for i in range(owners)])]
    ppermute x0 -> x3, waiting for transfers between devices: none -> 9.1 us  [spread_early(): lax.ppermute(block, 'clus', [(i, i ^ mask) for i in range(owners)])]
    ppermute x0 -> x3, starting transfers between devices: none -> 7.66 us  [spread_early(): lax.ppermute(block, 'clus', [(i, i ^ mask) for i in range(owners)])]
    all_to_all x1, waiting for transfers between devices: 2.89 us -> 0.01 us  [per_device(): lax.all_to_all(packed.reshape(owners, slot_count, -1), 'clus', split_axis...]
    ppermute x4 -> x2, starting transfers between devices: 6.01 us -> 4.18 us  [spread_early(): lax.ppermute(leaving, 'clus', [(i, i ^ bit) for i in range(owners)])]
    concatenate x4 -> x1, other arithmetic: 0.07 us -> 0.96 us  [spread_early(): both = jnp.concatenate([held, arrived], axis=0)]
    pallas_call x1, Pallas kernels: 1.59 us -> 0.87 us  [fetch(): pl.pallas_call(functools.partial(fetch_kernel, half), out_shape=(jax.Shap...]
    all_to_all x1, blocking collectives: 13.2 us -> 13.8 us  [per_device(): lax.all_to_all(message, 'clus', split_axis=0, concat_axis=0, tiled=True)]
  transfers between devices with their start and end apart: 5 -> 6, of which waited for: 5 -> 4; matrix products, arithmetic and copies ran while one was open for 0% -> 2% of each run, Pallas kernels for 1% -> 1%
where the time goes in v5:
time: 57.4 us; the launch traced here: 57.1 us
  starting transfers between devices  15.8 us (28%)
  waiting for transfers between devices  14.6 us (25%)
  blocking collectives  13.8 us (24%)
  Pallas kernels  11.2 us (20%)
  other arithmetic  1.03 us (2%)
  between operations  0.72 us (1%)
    all_to_all x1, blocking collectives, per_device(): lax.all_to_all(message, 'clus', split_axis=0, concat_axis=0, tiled=True)  13.8 us
    ppermute x3, waiting for transfers between devices, spread_early(): lax.ppermute(block, 'clus', [(i, i ^ mask) for i in range(owners)])  9.1 us
    ppermute x3, starting transfers between devices, spread_early(): lax.ppermute(block, 'clus', [(i, i ^ mask) for i in range(owners)])  7.66 us
    pallas_call x1, Pallas kernels, embed_and_pack(): pl.pallas_call(functools.partial(embed_kernel, slot_count, exchange_bits(...  7.54 us
    ppermute x2, waiting for transfers between devices, spread_early(): lax.ppermute(leaving, 'clus', [(i, i ^ bit) for i in range(owners)])  5.47 us
    ppermute x2, starting transfers between devices, spread_early(): lax.ppermute(leaving, 'clus', [(i, i ^ bit) for i in range(owners)])  4.18 us
    all_to_all x1, starting transfers between devices, per_device(): lax.all_to_all(packed.reshape(owners, slot_count, -1), 'clus', split_axis...  3.91 us
    pallas_call x1, Pallas kernels, scores(): pl.pallas_call(functools.partial(score_kernel, slot_count, half), out_spe...  2.19 us
  transfers between devices with their start and end apart: 6, of which 4 were waited for; matrix products, arithmetic and copies ran while one was open for 2% of the time, Pallas kernels for 1%

profile of v5, /device:TPU:0, one launch (start us, length us, event | category | flops | bytes accessed | tf_op | source)
XLA Modules:
  0.0 57.1 jit_solution(14728946445339993319)
XLA Ops:
  0.6 7.5 %shard_map.67 = (bf16[320,256]{1,0:T(8,128)(2,1)}, bf16[320,256]{1,0:T(8,128)(2,1)}, bf16[640,768]{1,0:T(8,128)(2,1)}, s32[1,320]{1,0:T(1,128)}) custom-call(bf16[320,4096]{1,0:T(8,128)(2,1)} %tokens_hbm.1, bf16[4096,1024]{1,0:T(8,128)(2,1)} %weight_hbm.1, s32[1,320]{1,0:T(1,128)} %bitcast.26, s32[320]{0:T(512)} %valid_ref.1), custom_call_target="tpu_custom_call" | custom-call | flops 2684354560 | bytes 11010048 | tf_op jit(solution)/shard_map/pallas_call | solution.py:113
  8.2 4.1 %collective-permute-start = (bf16[1,8,40,256]{3,2,0,1:T(8,128)(2,1)}, bf16[1,8,40,256]{3,2,0,1:T(8,128)(2,1)S(1)}, u32[]{:S(2)}, u32[]{:S(2)}) collective-permute-start(bf16[1,8,40,256]{3,2,0,1:T(8,128)(2,1)} %bitcast.30), channel_id=1, source_target_pairs={{0,8},{1,9},{2,10},{3,11},{4,12},{5,13},{6,14},{7,15},{8,0},{9,1},... | collective-permute-start | bytes 491528 | tf_op jit(solution)/shard_map/ppermute | solution.py:148
  12.3 3.9 %all-to-all-start = ((bf16[16,40,768]{2,1,0:T(8,128)(2,1)}), bf16[16,40,768]{2,1,0:T(8,128)(2,1)S(1)}, u32[]{:S(2)}, u32[]{:S(2)}) async-start(bf16[16,40,768]{2,1,0:T(8,128)(2,1)} %bitcast.28), calls=%async_computation | async-start | bytes 1966080 | tf_op jit(solution)/shard_map/all_to_all | solution.py:270
  16.2 4.1 %collective-permute-done = bf16[1,8,40,256]{3,2,0,1:T(8,128)(2,1)S(1)} collective-permute-done((bf16[1,8,40,256]{3,2,0,1:T(8,128)(2,1)}, bf16[1,8,40,256]{3,2,0,1:T(8,128)(2,1)S(1)}, u32[]{:S(2)}, u32[]{:S(2)}) %collective-permute-start) | collective-permute-done | bytes 163872 | tf_op jit(solution)/shard_map/ppermute | solution.py:148
  20.3 1.0 %fusion = (bf16[2,4,40,256]{3,2,0,1:T(8,128)(2,1)S(1)}, bf16[2,4,40,256]{3,2,0,1:T(8,128)(2,1)S(1)}) fusion(bf16[1,8,40,256]{3,2,0,1:T(8,128)(2,1)} %bitcast.29, bf16[1,8,40,256]{3,2,0,1:T(8,128)(2,1)S(1)} %collective-permute-done), kind=kLoop, calls=%fused_computation.9 | loop fusion | flops 163840 | bytes 655360 | tf_op jit(solution)/shard_map/concatenate | solution.py:149
  21.3 0.1 collective-permute-start.1
  21.3 1.4 %collective-permute-done.1 = bf16[2,4,40,256]{3,2,0,1:T(8,128)(2,1)S(1)} collective-permute-done((bf16[2,4,40,256]{3,2,0,1:T(8,128)(2,1)S(1)}, bf16[2,4,40,256]{3,2,0,1:T(8,128)(2,1)S(1)}, u32[]{:S(2)}, u32[]{:S(2)}) %collective-permute-start.1) | collective-permute-done | bytes 163872 | tf_op jit(solution)/shard_map/ppermute | solution.py:148
  22.8 1.6 %collective-permute-start.2 = (bf16[4,40,256]{2,1,0:T(8,128)(2,1)S(1)}, bf16[4,40,256]{2,1,0:T(8,128)(2,1)S(1)}, u32[]{:S(2)}, u32[]{:S(2)}) collective-permute-start(bf16[4,40,256]{2,1,0:T(8,128)(2,1)S(1)} %get-tuple-element.20), channel_id=1, source_target_pairs={{0,2},{1,3},{2,0},{3,1},{4,6},{5,7},{6,4},{7,5},{8,10},{9,11},{10,... | collective-permute-start | bytes 245768 | tf_op jit(solution)/shard_map/ppermute | solution.py:155
  24.4 5.5 %collective-permute-start.4 = (bf16[4,40,256]{2,1,0:T(8,128)(2,1)S(1)}, bf16[4,40,256]{2,1,0:T(8,128)(2,1)S(1)}, u32[]{:S(2)}, u32[]{:S(2)}) collective-permute-start(bf16[4,40,256]{2,1,0:T(8,128)(2,1)S(1)} %get-tuple-element.21), channel_id=1, source_target_pairs={{0,6},{1,7},{2,4},{3,5},{4,2},{5,3},{6,0},{7,1},{8,14},{9,15},{10,... | collective-permute-start | bytes 245768 | tf_op jit(solution)/shard_map/ppermute | solution.py:155
  29.9 0.5 collective-permute-start.3
  30.4 0.0 collective-permute-done.2
  30.4 5.0 %collective-permute-done.4 = bf16[4,40,256]{2,1,0:T(8,128)(2,1)S(1)} collective-permute-done((bf16[4,40,256]{2,1,0:T(8,128)(2,1)S(1)}, bf16[4,40,256]{2,1,0:T(8,128)(2,1)S(1)}, u32[]{:S(2)}, u32[]{:S(2)}) %collective-permute-start.4) | collective-permute-done | bytes 81952 | tf_op jit(solution)/shard_map/ppermute | solution.py:155
  35.4 4.1 %collective-permute-done.3 = bf16[4,40,256]{2,1,0:T(8,128)(2,1)S(1)} collective-permute-done((bf16[4,40,256]{2,1,0:T(8,128)(2,1)S(1)}, bf16[4,40,256]{2,1,0:T(8,128)(2,1)S(1)}, u32[]{:S(2)}, u32[]{:S(2)}) %collective-permute-start.3) | collective-permute-done | bytes 81952 | tf_op jit(solution)/shard_map/ppermute | solution.py:155
  39.6 0.0 copy-start
  39.6 0.0 copy-start.1
  39.6 0.0 copy-start.2
  39.6 0.6 shard_map.68.early_ref
  40.2 0.0 all-to-all-done
  40.2 2.2 %shard_map.69 = (f32[16,128]{1,0:T(8,128)S(1)}, f32[1,640,640]{2,1,0:T(8,128)}) custom-call(bf16[640,256]{1,0:T(8,128)(2,1)S(1)} %shard_map.68.early_ref, bf16[640,768]{1,0:T(8,128)(2,1)S(1)} %bitcast.22), custom_call_target="tpu_custom_call" | custom-call | tf_op jit(solution)/shard_map/pallas_call | solution.py:223
  42.4 13.8 %all_to_all.16 = f32[16,1,128]{2,1,0:T(1,128)S(1)} all-to-all(f32[16,1,128]{2,1,0:T(1,128)S(1)} %bitcast.25), channel_id=1, replica_groups=mesh['groups'=2,'clus'=16] {'clus'}, dimensions={0} | all-to-all | bytes 16384 | tf_op jit(solution)/shard_map/all_to_all | solution.py:275
  56.2 0.0 copy-done
  56.2 0.0 copy-done.1
  56.2 0.0 copy-done.2
  56.2 0.9 %shard_map.70 = (f32[320]{0:T(512)}, f32[320]{0:T(512)}) custom-call(f32[16,128]{1,0:T(8,128)S(1)} %bitcast.24, s32[1,320]{1,0:T(1,128)S(1)} %bitcast.27, s32[1,320]{1,0:T(1,128)S(1)} %copy-done.2, s32[320]{0:T(512)S(1)} %copy-done), custom_call_target="tpu_custom_call" | custom-call | tf_op jit(solution)/shard_map/pallas_call | solution.py:252
  (2 shorter events, 0.1 us)
Async XLA Ops:
  8.2 12.1 %collective-permute-start = (bf16[1,8,40,256]{3,2,0,1:T(8,128)(2,1)}, bf16[1,8,40,256]{3,2,0,1:T(8,128)(2,1)S(1)}, u32[]{:S(2)}, u32[]{:S(2)}) collective-permute-start(bf16[1,8,40,256]{3,2,0,1:T(8,128)(2,1)} %bitcast.30), channel_id=1, source_target_pairs={{0,8},{1,9},{2,10},{3,11},{4,12},{5,13},{6,14},{7,15},{8,0},{9,1},... | collective-permute-start | bytes 491528 | tf_op jit(solution)/shard_map/ppermute | solution.py:148
  12.3 27.9 %all-to-all-start = ((bf16[16,40,768]{2,1,0:T(8,128)(2,1)}), bf16[16,40,768]{2,1,0:T(8,128)(2,1)S(1)}, u32[]{:S(2)}, u32[]{:S(2)}) async-start(bf16[16,40,768]{2,1,0:T(8,128)(2,1)} %bitcast.28), calls=%async_computation | async-start | bytes 1966080 | tf_op jit(solution)/shard_map/all_to_all | solution.py:270
  21.3 1.5 %collective-permute-start.1 = (bf16[2,4,40,256]{3,2,0,1:T(8,128)(2,1)S(1)}, bf16[2,4,40,256]{3,2,0,1:T(8,128)(2,1)S(1)}, u32[]{:S(2)}, u32[]{:S(2)}) collective-permute-start(bf16[2,4,40,256]{3,2,0,1:T(8,128)(2,1)S(1)} %get-tuple-element.24), channel_id=1, source_target_pairs={{0,1},{1,0},{2,3},{3,2},{4,5},{5,4},{6,7},{7,6},{8,9},{9,8},{10,11... | collective-permute-start | bytes 491528 | tf_op jit(solution)/shard_map/ppermute | solution.py:148
  22.8 7.7 %collective-permute-start.2 = (bf16[4,40,256]{2,1,0:T(8,128)(2,1)S(1)}, bf16[4,40,256]{2,1,0:T(8,128)(2,1)S(1)}, u32[]{:S(2)}, u32[]{:S(2)}) collective-permute-start(bf16[4,40,256]{2,1,0:T(8,128)(2,1)S(1)} %get-tuple-element.20), channel_id=1, source_target_pairs={{0,2},{1,3},{2,0},{3,1},{4,6},{5,7},{6,4},{7,5},{8,10},{9,11},{10,... | collective-permute-start | bytes 245768 | tf_op jit(solution)/shard_map/ppermute | solution.py:155
  24.4 11.0 %collective-permute-start.4 = (bf16[4,40,256]{2,1,0:T(8,128)(2,1)S(1)}, bf16[4,40,256]{2,1,0:T(8,128)(2,1)S(1)}, u32[]{:S(2)}, u32[]{:S(2)}) collective-permute-start(bf16[4,40,256]{2,1,0:T(8,128)(2,1)S(1)} %get-tuple-element.21), channel_id=1, source_target_pairs={{0,6},{1,7},{2,4},{3,5},{4,2},{5,3},{6,0},{7,1},{8,14},{9,15},{10,... | collective-permute-start | bytes 245768 | tf_op jit(solution)/shard_map/ppermute | solution.py:155
  29.9 9.6 %collective-permute-start.3 = (bf16[4,40,256]{2,1,0:T(8,128)(2,1)S(1)}, bf16[4,40,256]{2,1,0:T(8,128)(2,1)S(1)}, u32[]{:S(2)}, u32[]{:S(2)}) collective-permute-start(bf16[4,40,256]{2,1,0:T(8,128)(2,1)S(1)} %get-tuple-element.22), channel_id=1, source_target_pairs={{0,4},{1,5},{2,6},{3,7},{4,0},{5,1},{6,2},{7,3},{8,12},{9,13},{10,... | collective-permute-start | bytes 245768 | tf_op jit(solution)/shard_map/ppermute | solution.py:155
  39.6 16.6 %copy-start = (s32[320]{0:T(512)S(1)}, s32[320]{0:T(512)}, u32[]{:S(2)}) copy-start(s32[320]{0:T(512)} %valid_ref.1) | copy-start | bytes 3844
  39.6 16.6 %copy-start.1 = (s32[320,1]{0,1:T(1,128)S(1)}, s32[320,1]{0,1:T(1,128)}, u32[]{:S(2)}) copy-start(s32[320,1]{0,1:T(1,128)} %param.6) | copy-start | bytes 3844
  39.6 16.6 %copy-start.2 = (s32[1,320]{1,0:T(1,128)S(1)}, s32[1,320]{1,0:T(1,128)}, u32[]{:S(2)}) copy-start(s32[1,320]{1,0:T(1,128)} %get-tuple-element.16.rank_ref) | copy-start | bytes 3844

commit v6 on v5

--- a/solution.py
+++ b/solution.py
@@ -10,7 +10,8 @@
 F32 = jnp.float32
 BF16 = jnp.bfloat16
 VMEM_BYTES = 48 * 1024 * 1024
-EMBED_VMEM_BYTES = 60 * 1024 * 1024
+EMBED_VMEM_BYTES = 40 * 1024 * 1024
+PACK_VMEM_BYTES = 16 * 1024 * 1024
 FETCH_VMEM_BYTES = 8 * 1024 * 1024
 EARLY = 2
 ORDER_FLOPS = 13 * 10**9
@@ -50,8 +51,8 @@
 
 
 def embed_kernel(
-    slot_count, bits, tokens_hbm, weight_hbm, label_hbm, valid_hbm, keep_ref, send_ref, packed_ref, rank_ref,
-    tokens, weight, total, place, apart, label_ref, valid_ref, token_sem, weight_sem, small_sem,
+    slot_count, bits, tokens_hbm, weight_hbm, label_hbm, valid_hbm, keep_ref, send_ref, place, late_ref, rank_ref,
+    tokens, weight, total, apart, label_ref, valid_ref, token_sem, weight_sem, small_sem,
 ):
     steps = token_sem.shape[0]
     block = tokens.shape[1] // steps
@@ -101,8 +102,7 @@
     unit = (total[:, :early] * scale).astype(BF16)
     send_ref[...] = jnp.dot(apart[near:, :], unit, preferred_element_type=F32).astype(BF16)
     keep_ref[...] = jnp.dot(apart[:near, :], unit, preferred_element_type=F32).astype(BF16)
-    unit = (total[:, early:] * scale).astype(BF16)
-    packed_ref[...] = jnp.dot(place[...], unit, preferred_element_type=F32).astype(BF16)
+    late_ref[...] = (total[:, early:] * scale).astype(BF16)
 
 
 def embed_and_pack(tokens, weight, label_row, valid, owners, slot_count, early):
@@ -116,14 +116,14 @@
         out_shape=(
             jax.ShapeDtypeStruct((width_all // 2, early), BF16),
             jax.ShapeDtypeStruct((width_all // 2, early), BF16),
-            jax.ShapeDtypeStruct((width_all, width - early), BF16),
+            jax.ShapeDtypeStruct((width_all, rows), BF16),
+            jax.ShapeDtypeStruct((rows, width - early), BF16),
             jax.ShapeDtypeStruct((1, rows), jnp.int32),
         ),
         scratch_shapes=[
             pltpu.VMEM((rows, depth), BF16),
             pltpu.VMEM((depth, width), BF16),
             pltpu.VMEM((rows, width), F32),
-            pltpu.VMEM((width_all, rows), BF16),
             pltpu.VMEM((width_all, rows), BF16),
             pltpu.VMEM((1, rows), jnp.int32),
             pltpu.VMEM((rows,), jnp.int32),
@@ -135,7 +135,24 @@
         cost_estimate=pl.CostEstimate(
             flops=2 * rows * depth * width, bytes_accessed=2 * depth * width + 2 * rows * depth, transcendentals=0
         ),
-    )(tokens, weight, label_row, valid)
+    )(*(pltpu.with_memory_space_constraint(x, pltpu.HBM) for x in (tokens, weight, label_row, valid)))
+
+
+def pack_kernel(place_ref, unit_ref, packed_ref):
+    packed_ref[...] = jnp.dot(place_ref[...], unit_ref[...], preferred_element_type=F32).astype(BF16)
+
+
+def pack(place, unit):
+    width_all, rows = place.shape
+    late = unit.shape[1]
+    return pl.pallas_call(
+        pack_kernel,
+        out_shape=jax.ShapeDtypeStruct((width_all, late), BF16),
+        compiler_params=pltpu.CompilerParams(vmem_limit_bytes=PACK_VMEM_BYTES),
+        cost_estimate=pl.CostEstimate(
+            flops=2 * width_all * rows * late, bytes_accessed=2 * width_all * late, transcendentals=0
+        ),
+    )(place, unit)
 
 
 def spread_early(keep, send, owners, slot_count):
@@ -264,11 +281,11 @@
     half = -(-slot_count // 64) * 64
     early = EARLY * proj_weight.shape[1] // 8
     label_row = labels.reshape(1, row_count)
-    keep, send, packed, rank_row = embed_and_pack(
+    keep, send, place, unit, rank_row = embed_and_pack(
         tokens, proj_weight, label_row, valid_rows, owners, slot_count, early
     )
     arrived = lax.all_to_all(
-        packed.reshape(owners, slot_count, -1), "clus", split_axis=0, concat_axis=0, tiled=True
+        pack(place, unit).reshape(owners, slot_count, -1), "clus", split_axis=0, concat_axis=0, tiled=True
     )
     early_members = order_early(spread_early(keep, send, owners, slot_count), owners, slot_count)
     message, similar = scores(early_members, arrived.reshape(width_all, -1), owners, slot_count, half)

time: 57.4 us -> 54.7 us (0.953)
  starting transfers between devices: 15.8 us -> 11.6 us
  waiting for transfers between devices: 14.6 us -> 17.9 us
  blocking collectives: 13.8 us -> 12.7 us
  other arithmetic: 1.03 us -> 0.11 us
    ppermute x3, waiting for transfers between devices: 9.1 us -> 13.6 us  [spread_early(): lax.ppermute(block, 'clus', [(i, i ^ mask) for i in range(owners)])]
    ppermute x3, starting transfers between devices: 7.66 us -> 3.55 us  [spread_early(): lax.ppermute(block, 'clus', [(i, i ^ mask) for i in range(owners)])]
    ppermute x2, waiting for transfers between devices: 5.47 us -> 3.56 us  [spread_early(): lax.ppermute(leaving, 'clus', [(i, i ^ bit) for i in range(owners)])]
    pallas_call x0 -> x1, Pallas kernels: none -> 1.61 us  [pack(): pl.pallas_call(pack_kernel, out_shape=jax.ShapeDtypeStruct((width_all, la...]
    pallas_call x1, Pallas kernels: 7.54 us -> 6.09 us  [embed_and_pack(): pl.pallas_call(functools.partial(embed_kernel, slot_count, exchange_bits(...]
    all_to_all x1, blocking collectives: 13.8 us -> 12.7 us  [per_device(): lax.all_to_all(message, 'clus', split_axis=0, concat_axis=0, tiled=True)]
    concatenate x1, other arithmetic: 0.96 us -> 0.03 us  [spread_early(): both = jnp.concatenate([held, arrived], axis=0)]
    all_to_all x1, waiting for transfers between devices: 0.01 us -> 0.73 us  [per_device(): lax.all_to_all(pack(place, unit).reshape(owners, slot_count, -1), 'clus',...]
  transfers between devices with their start and end apart: 6 -> 6, of which waited for: 4 -> 6; matrix products, arithmetic and copies ran while one was open for 2% -> 0% of each run, Pallas kernels for 1% -> 4%
where the time goes in v6:
time: 54.7 us; the launch traced here: 54.4 us
  waiting for transfers between devices  17.9 us (33%)
  blocking collectives  12.7 us (23%)
  starting transfers between devices  11.6 us (21%)
  Pallas kernels  11.3 us (21%)
  between operations  0.7 us (1%)
    ppermute x3, waiting for transfers between devices, spread_early(): lax.ppermute(block, 'clus', [(i, i ^ mask) for i in range(owners)])  13.6 us
    all_to_all x1, blocking collectives, per_device(): lax.all_to_all(message, 'clus', split_axis=0, concat_axis=0, tiled=True)  12.7 us
    pallas_call x1, Pallas kernels, embed_and_pack(): pl.pallas_call(functools.partial(embed_kernel, slot_count, exchange_bits(...  6.09 us
    ppermute x2, starting transfers between devices, spread_early(): lax.ppermute(leaving, 'clus', [(i, i ^ bit) for i in range(owners)])  4.17 us
    all_to_all x1, starting transfers between devices, per_device(): lax.all_to_all(pack(place, unit).reshape(owners, slot_count, -1), 'clus',...  3.91 us
    ppermute x2, waiting for transfers between devices, spread_early(): lax.ppermute(leaving, 'clus', [(i, i ^ bit) for i in range(owners)])  3.56 us
    ppermute x3, starting transfers between devices, spread_early(): lax.ppermute(block, 'clus', [(i, i ^ mask) for i in range(owners)])  3.55 us
    pallas_call x1, Pallas kernels, scores(): pl.pallas_call(functools.partial(score_kernel, slot_count, half), out_spe...  2.17 us
  transfers between devices with their start and end apart: 6, of which 6 were waited for; matrix products, arithmetic and copies ran while one was open for 0% of the time, Pallas kernels for 4%

profile of v6, /device:TPU:0, one launch (start us, length us, event | category | flops | bytes accessed | tf_op | source)
XLA Modules:
  0.0 54.4 jit_solution(6014293472060411948)
XLA Ops:
  0.6 6.1 %shard_map.67 = (bf16[320,256]{1,0:T(8,128)(2,1)S(1)}, bf16[320,256]{1,0:T(8,128)(2,1)S(1)}, bf16[640,320]{1,0:T(8,128)(2,1)S(1)}, bf16[320,768]{1,0:T(8,128)(2,1)S(1)}, s32[1,320]{1,0:T(1,128)S(1)}) custom-call(bf16[320,4096]{1,0:T(8,128)(2,1)} %tokens_hbm.1, bf16[4096,1024]{1,0:T(8,128)(2,1)} %weight_hbm.1, s32[1,320]{1,0:T(1,128)} %bitcast.27, s32[320]{0:T(512)} %valid_ref.1), custom_call_target="tpu_custom_call" | custom-call | flops 2684354560 | bytes 11010048 | tf_op jit(solution)/shard_map/pallas_call | solution.py:113
  6.7 4.1 %collective-permute-start = (bf16[1,8,40,256]{3,2,0,1:T(8,128)(2,1)S(1)}, bf16[1,8,40,256]{3,2,0,1:T(8,128)(2,1)S(1)}, u32[]{:S(2)}, u32[]{:S(2)}) collective-permute-start(bf16[1,8,40,256]{3,2,0,1:T(8,128)(2,1)S(1)} %bitcast.29), channel_id=1, source_target_pairs={{0,8},{1,9},{2,10},{3,11},{4,12},{5,13},{6,14},{7,15},{8,0},{9,1},... | collective-permute-start | bytes 491528 | tf_op jit(solution)/shard_map/ppermute | solution.py:165
  10.8 1.6 %shard_map.69 = bf16[640,768]{1,0:T(8,128)(2,1)} custom-call(bf16[640,320]{1,0:T(8,128)(2,1)S(1)} %get-tuple-element.14.place_ref, bf16[320,768]{1,0:T(8,128)(2,1)S(1)} %get-tuple-element.15.unit_ref), custom_call_target="tpu_custom_call" | custom-call | flops 314572800 | bytes 983040 | tf_op jit(solution)/shard_map/pallas_call | solution.py:148
  12.4 3.9 %all-to-all-start = ((bf16[16,40,768]{2,1,0:T(8,128)(2,1)}), bf16[16,40,768]{2,1,0:T(8,128)(2,1)S(1)}, u32[]{:S(2)}, u32[]{:S(2)}) async-start(bf16[16,40,768]{2,1,0:T(8,128)(2,1)} %bitcast.10), calls=%async_computation | async-start | bytes 1966080 | tf_op jit(solution)/shard_map/all_to_all | solution.py:287
  16.4 2.2 %collective-permute-done = bf16[1,8,40,256]{3,2,0,1:T(8,128)(2,1)S(1)} collective-permute-done((bf16[1,8,40,256]{3,2,0,1:T(8,128)(2,1)S(1)}, bf16[1,8,40,256]{3,2,0,1:T(8,128)(2,1)S(1)}, u32[]{:S(2)}, u32[]{:S(2)}) %collective-permute-start) | collective-permute-done | bytes 163872 | tf_op jit(solution)/shard_map/ppermute | solution.py:165
  18.6 0.1 collective-permute-start.1
  18.7 1.4 %collective-permute-done.1 = bf16[2,4,40,256]{3,2,0,1:T(8,128)(2,1)S(1)} collective-permute-done((bf16[2,4,40,256]{3,2,0,1:T(8,128)(2,1)S(1)}, bf16[2,4,40,256]{3,2,0,1:T(8,128)(2,1)S(1)}, u32[]{:S(2)}, u32[]{:S(2)}) %collective-permute-start.1) | collective-permute-done | bytes 163872 | tf_op jit(solution)/shard_map/ppermute | solution.py:165
  20.1 1.6 %collective-permute-start.2 = (bf16[4,40,256]{2,1,0:T(8,128)(2,1)S(1)}, bf16[4,40,256]{2,1,0:T(8,128)(2,1)S(1)}, u32[]{:S(2)}, u32[]{:S(2)}) collective-permute-start(bf16[4,40,256]{2,1,0:T(8,128)(2,1)S(1)} %get-tuple-element.22), channel_id=1, source_target_pairs={{0,2},{1,3},{2,0},{3,1},{4,6},{5,7},{6,4},{7,5},{8,10},{9,11},{10,... | collective-permute-start | bytes 245768 | tf_op jit(solution)/shard_map/ppermute | solution.py:172
  21.7 0.7 %collective-permute-start.4 = (bf16[4,40,256]{2,1,0:T(8,128)(2,1)S(1)}, bf16[4,40,256]{2,1,0:T(8,128)(2,1)S(1)}, u32[]{:S(2)}, u32[]{:S(2)}) collective-permute-start(bf16[4,40,256]{2,1,0:T(8,128)(2,1)S(1)} %get-tuple-element.23), channel_id=1, source_target_pairs={{0,6},{1,7},{2,4},{3,5},{4,2},{5,3},{6,0},{7,1},{8,14},{9,15},{10,... | collective-permute-start | bytes 245768 | tf_op jit(solution)/shard_map/ppermute | solution.py:172
  22.4 1.2 %collective-permute-start.3 = (bf16[4,40,256]{2,1,0:T(8,128)(2,1)S(1)}, bf16[4,40,256]{2,1,0:T(8,128)(2,1)S(1)}, u32[]{:S(2)}, u32[]{:S(2)}) collective-permute-start(bf16[4,40,256]{2,1,0:T(8,128)(2,1)S(1)} %get-tuple-element.24), channel_id=1, source_target_pairs={{0,4},{1,5},{2,6},{3,7},{4,0},{5,1},{6,2},{7,3},{8,12},{9,13},{10,... | collective-permute-start | bytes 245768 | tf_op jit(solution)/shard_map/ppermute | solution.py:172
  23.6 3.8 %collective-permute-done.2 = bf16[4,40,256]{2,1,0:T(8,128)(2,1)S(1)} collective-permute-done((bf16[4,40,256]{2,1,0:T(8,128)(2,1)S(1)}, bf16[4,40,256]{2,1,0:T(8,128)(2,1)S(1)}, u32[]{:S(2)}, u32[]{:S(2)}) %collective-permute-start.2) | collective-permute-done | bytes 81952 | tf_op jit(solution)/shard_map/ppermute | solution.py:172
  27.5 8.2 %collective-permute-done.4 = bf16[4,40,256]{2,1,0:T(8,128)(2,1)S(1)} collective-permute-done((bf16[4,40,256]{2,1,0:T(8,128)(2,1)S(1)}, bf16[4,40,256]{2,1,0:T(8,128)(2,1)S(1)}, u32[]{:S(2)}, u32[]{:S(2)}) %collective-permute-start.4) | collective-permute-done | bytes 81952 | tf_op jit(solution)/shard_map/ppermute | solution.py:172
  35.7 1.6 %collective-permute-done.3 = bf16[4,40,256]{2,1,0:T(8,128)(2,1)S(1)} collective-permute-done((bf16[4,40,256]{2,1,0:T(8,128)(2,1)S(1)}, bf16[4,40,256]{2,1,0:T(8,128)(2,1)S(1)}, u32[]{:S(2)}, u32[]{:S(2)}) %collective-permute-start.3) | collective-permute-done | bytes 81952 | tf_op jit(solution)/shard_map/ppermute | solution.py:172
  37.3 0.0 copy-start
  37.3 0.0 copy-start.1
  37.3 0.6 %shard_map.68.early_ref = bf16[640,256]{1,0:T(8,128)(2,1)S(1)} custom-call(bf16[640,256]{1,0:T(8,128)(2,1)S(1)} %bitcast.23), custom_call_target="tpu_custom_call" | custom-call | flops 12999999488 | bytes 655360 | tf_op jit(solution)/shard_map/pallas_call | solution.py:191
  37.9 0.7 %all-to-all-done = bf16[16,40,768]{2,1,0:T(8,128)(2,1)S(1)} async-done(((bf16[16,40,768]{2,1,0:T(8,128)(2,1)}), bf16[16,40,768]{2,1,0:T(8,128)(2,1)S(1)}, u32[]{:S(2)}, u32[]{:S(2)}) %all-to-all-start) | async-done | bytes 983072 | tf_op jit(solution)/shard_map/all_to_all | solution.py:287
  38.6 2.2 %shard_map.70 = (f32[16,128]{1,0:T(8,128)S(1)}, f32[1,640,640]{2,1,0:T(8,128)}) custom-call(bf16[640,256]{1,0:T(8,128)(2,1)S(1)} %shard_map.68.early_ref, bf16[640,768]{1,0:T(8,128)(2,1)S(1)} %bitcast.22), custom_call_target="tpu_custom_call" | custom-call | tf_op jit(solution)/shard_map/pallas_call | solution.py:240
  40.8 12.7 %all_to_all.16 = f32[16,1,128]{2,1,0:T(1,128)S(1)} all-to-all(f32[16,1,128]{2,1,0:T(1,128)S(1)} %bitcast.26), channel_id=1, replica_groups=mesh['groups'=2,'clus'=16] {'clus'}, dimensions={0} | all-to-all | bytes 16384 | tf_op jit(solution)/shard_map/all_to_all | solution.py:292
  53.5 0.0 copy-done
  53.5 0.0 copy-done.1
  53.5 0.9 %shard_map.71 = (f32[320]{0:T(512)}, f32[320]{0:T(512)}) custom-call(f32[16,128]{1,0:T(8,128)S(1)} %bitcast.25, s32[1,320]{1,0:T(1,128)S(1)} %bitcast.28, s32[1,320]{1,0:T(1,128)S(1)} %get-tuple-element.18.rank_ref, s32[320]{0:T(512)S(1)} %copy-done), custom_call_target="tpu_custom_call" | custom-call | tf_op jit(solution)/shard_map/pallas_call | solution.py:269
  (3 shorter events, 0.1 us)
Async XLA Ops:
  6.7 11.8 %collective-permute-start = (bf16[1,8,40,256]{3,2,0,1:T(8,128)(2,1)S(1)}, bf16[1,8,40,256]{3,2,0,1:T(8,128)(2,1)S(1)}, u32[]{:S(2)}, u32[]{:S(2)}) collective-permute-start(bf16[1,8,40,256]{3,2,0,1:T(8,128)(2,1)S(1)} %bitcast.29), channel_id=1, source_target_pairs={{0,8},{1,9},{2,10},{3,11},{4,12},{5,13},{6,14},{7,15},{8,0},{9,1},... | collective-permute-start | bytes 491528 | tf_op jit(solution)/shard_map/ppermute | solution.py:165
  12.4 26.2 %all-to-all-start = ((bf16[16,40,768]{2,1,0:T(8,128)(2,1)}), bf16[16,40,768]{2,1,0:T(8,128)(2,1)S(1)}, u32[]{:S(2)}, u32[]{:S(2)}) async-start(bf16[16,40,768]{2,1,0:T(8,128)(2,1)} %bitcast.10), calls=%async_computation | async-start | bytes 1966080 | tf_op jit(solution)/shard_map/all_to_all | solution.py:287
  18.6 1.5 %collective-permute-start.1 = (bf16[2,4,40,256]{3,2,0,1:T(8,128)(2,1)S(1)}, bf16[2,4,40,256]{3,2,0,1:T(8,128)(2,1)S(1)}, u32[]{:S(2)}, u32[]{:S(2)}) collective-permute-start(bf16[2,4,40,256]{3,2,0,1:T(8,128)(2,1)S(1)} %get-tuple-element.26), channel_id=1, source_target_pairs={{0,1},{1,0},{2,3},{3,2},{4,5},{5,4},{6,7},{7,6},{8,9},{9,8},{10,11... | collective-permute-start | bytes 491528 | tf_op jit(solution)/shard_map/ppermute | solution.py:165
  20.1 7.4 %collective-permute-start.2 = (bf16[4,40,256]{2,1,0:T(8,128)(2,1)S(1)}, bf16[4,40,256]{2,1,0:T(8,128)(2,1)S(1)}, u32[]{:S(2)}, u32[]{:S(2)}) collective-permute-start(bf16[4,40,256]{2,1,0:T(8,128)(2,1)S(1)} %get-tuple-element.22), channel_id=1, source_target_pairs={{0,2},{1,3},{2,0},{3,1},{4,6},{5,7},{6,4},{7,5},{8,10},{9,11},{10,... | collective-permute-start | bytes 245768 | tf_op jit(solution)/shard_map/ppermute | solution.py:172
  21.7 14.0 %collective-permute-start.4 = (bf16[4,40,256]{2,1,0:T(8,128)(2,1)S(1)}, bf16[4,40,256]{2,1,0:T(8,128)(2,1)S(1)}, u32[]{:S(2)}, u32[]{:S(2)}) collective-permute-start(bf16[4,40,256]{2,1,0:T(8,128)(2,1)S(1)} %get-tuple-element.23), channel_id=1, source_target_pairs={{0,6},{1,7},{2,4},{3,5},{4,2},{5,3},{6,0},{7,1},{8,14},{9,15},{10,... | collective-permute-start | bytes 245768 | tf_op jit(solution)/shard_map/ppermute | solution.py:172
  22.4 14.8 %collective-permute-start.3 = (bf16[4,40,256]{2,1,0:T(8,128)(2,1)S(1)}, bf16[4,40,256]{2,1,0:T(8,128)(2,1)S(1)}, u32[]{:S(2)}, u32[]{:S(2)}) collective-permute-start(bf16[4,40,256]{2,1,0:T(8,128)(2,1)S(1)} %get-tuple-element.24), channel_id=1, source_target_pairs={{0,4},{1,5},{2,6},{3,7},{4,0},{5,1},{6,2},{7,3},{8,12},{9,13},{10,... | collective-permute-start | bytes 245768 | tf_op jit(solution)/shard_map/ppermute | solution.py:172
  37.3 16.2 %copy-start = (s32[320]{0:T(512)S(1)}, s32[320]{0:T(512)}, u32[]{:S(2)}) copy-start(s32[320]{0:T(512)} %valid_ref.1) | copy-start | bytes 3844
  37.3 16.2 %copy-start.1 = (s32[320,1]{0,1:T(1,128)S(1)}, s32[320,1]{0,1:T(1,128)}, u32[]{:S(2)}) copy-start(s32[320,1]{0,1:T(1,128)} %param.6) | copy-start | bytes 3844

commit v7 on v6

--- a/solution.py
+++ b/solution.py
@@ -51,7 +51,7 @@
 
 
 def embed_kernel(
-    slot_count, bits, tokens_hbm, weight_hbm, label_hbm, valid_hbm, keep_ref, send_ref, place, late_ref, rank_ref,
+    slot_count, bits, tokens_hbm, weight_hbm, label_hbm, valid_hbm, keep_ref, send_ref, slot_ref, late_ref, rank_ref,
     tokens, weight, total, apart, label_ref, valid_ref, token_sem, weight_sem, small_sem,
 ):
     steps = token_sem.shape[0]
@@ -79,12 +79,12 @@
     valid = valid_ref[...].reshape(label.shape)
     rank = rank_rows(label)
     rank_ref[...] = rank
-    place[...] = place_rows(label * slot_count + rank, valid, place.shape[0])
+    slot_ref[...] = jnp.where(valid > 0, label * slot_count + rank, -1)
     distance = label ^ lax.axis_index("clus")
     position = jnp.zeros_like(label)
     for k, bit in enumerate(bits):
         position += jnp.where((distance & bit) > 0, 1 << (len(bits) - 1 - k), 0)
-    apart[...] = place_rows(position * slot_count + rank, valid, place.shape[0])
+    apart[...] = place_rows(position * slot_count + rank, valid, apart.shape[0])
     for k, pair in enumerate(copies):
         for copy in pair:
             copy.wait()
@@ -116,7 +116,7 @@
         out_shape=(
             jax.ShapeDtypeStruct((width_all // 2, early), BF16),
             jax.ShapeDtypeStruct((width_all // 2, early), BF16),
-            jax.ShapeDtypeStruct((width_all, rows), BF16),
+            jax.ShapeDtypeStruct((1, rows), jnp.int32),
             jax.ShapeDtypeStruct((rows, width - early), BF16),
             jax.ShapeDtypeStruct((1, rows), jnp.int32),
         ),
@@ -138,13 +138,14 @@
     )(*(pltpu.with_memory_space_constraint(x, pltpu.HBM) for x in (tokens, weight, label_row, valid)))
 
 
-def pack_kernel(place_ref, unit_ref, packed_ref):
-    packed_ref[...] = jnp.dot(place_ref[...], unit_ref[...], preferred_element_type=F32).astype(BF16)
-
-
-def pack(place, unit):
-    width_all, rows = place.shape
-    late = unit.shape[1]
+def pack_kernel(slot_ref, unit_ref, packed_ref):
+    slot = slot_ref[...]
+    place = place_rows(slot, slot + 1, packed_ref.shape[0])
+    packed_ref[...] = jnp.dot(place, unit_ref[...], preferred_element_type=F32).astype(BF16)
+
+
+def pack(slot_row, unit, width_all):
+    rows, late = unit.shape
     return pl.pallas_call(
         pack_kernel,
         out_shape=jax.ShapeDtypeStruct((width_all, late), BF16),
@@ -152,7 +153,7 @@
         cost_estimate=pl.CostEstimate(
             flops=2 * width_all * rows * late, bytes_accessed=2 * width_all * late, transcendentals=0
         ),
-    )(place, unit)
+    )(slot_row, unit)
 
 
 def spread_early(keep, send, owners, slot_count):
@@ -173,7 +174,7 @@
     return jnp.concatenate(parts, axis=0).reshape(owners * slot_count, early)
 
 
-def order_kernel(slot_count, bits, relative_ref, members_ref):
+def order_kernel(slot_count, bits, relative_ref, gram_ref):
     width_all = relative_ref.shape[0]
     member = lax.broadcasted_iota(jnp.int32, (width_all, 1), 0)
     source = member // slot_count
@@ -184,13 +185,14 @@
     wanted = index * slot_count + member - source * slot_count
     held = lax.broadcasted_iota(jnp.int32, (width_all, width_all), 1)
     chosen = jnp.where(held == wanted, 1.0, 0.0).astype(BF16)
-    members_ref[...] = jnp.dot(chosen, relative_ref[...], preferred_element_type=F32).astype(BF16)
+    members = jnp.dot(chosen, relative_ref[...], preferred_element_type=F32).astype(BF16)
+    gram_ref[...] = lax.dot_general(members, members, (((1,), (1,)), ((), ())), preferred_element_type=F32)
 
 
 def order_early(relative, owners, slot_count):
     return pl.pallas_call(
         functools.partial(order_kernel, slot_count, exchange_bits(owners)),
-        out_shape=jax.ShapeDtypeStruct(relative.shape, BF16),
+        out_shape=jax.ShapeDtypeStruct((relative.shape[0],) * 2, F32),
         compiler_params=pltpu.CompilerParams(vmem_limit_bytes=VMEM_BYTES),
         cost_estimate=pl.CostEstimate(flops=ORDER_FLOPS, bytes_accessed=4 * relative.size, transcendentals=0),
     )(relative)
@@ -205,8 +207,8 @@
     nears, sums = [], []
     for b in range(2):
         part = slice(b * block, (b + 1) * block)
-        tile = lax.dot_general(early_ref[part, :], early_ref[...], transposed, preferred_element_type=F32)
-        tile += lax.dot_general(late_ref[part, :], late_ref[...], transposed, preferred_element_type=F32)
+        tile = lax.dot_general(late_ref[part, :], late_ref[...], transposed, preferred_element_type=F32)
+        tile += early_ref[part, :]
         gram[part, :] = tile
         copy = pltpu.make_async_copy(gram.at[part, :], similar_hbm.at[0, part, :], sem.at[b])
         copy.start()
@@ -281,14 +283,14 @@
     half = -(-slot_count // 64) * 64
     early = EARLY * proj_weight.shape[1] // 8
     label_row = labels.reshape(1, row_count)
-    keep, send, place, unit, rank_row = embed_and_pack(
+    keep, send, slot_row, unit, rank_row = embed_and_pack(
         tokens, proj_weight, label_row, valid_rows, owners, slot_count, early
     )
     arrived = lax.all_to_all(
-        pack(place, unit).reshape(owners, slot_count, -1), "clus", split_axis=0, concat_axis=0, tiled=True
+        pack(slot_row, unit, width_all).reshape(owners, slot_count, -1), "clus", split_axis=0, concat_axis=0, tiled=True
     )
-    early_members = order_early(spread_early(keep, send, owners, slot_count), owners, slot_count)
-    message, similar = scores(early_members, arrived.reshape(width_all, -1), owners, slot_count, half)
+    early_gram = order_early(spread_early(keep, send, owners, slot_count), owners, slot_count)
+    message, similar = scores(early_gram, arrived.reshape(width_all, -1), owners, slot_count, half)
     returned = lax.all_to_all(message, "clus", split_axis=0, concat_axis=0, tiled=True)
     nearest, centre_dist = fetch(returned, label_row, rank_row, valid_rows, half)
     return (similar, nearest, centre_dist)

time: 54.7 us -> 54.2 us (level)
  waiting for transfers between devices: 17.9 us -> 17.2 us
    all_to_all x1, waiting for transfers between devices: 0.73 us -> 0.03 us  [per_device(): lax.all_to_all(pack(slot_row, unit, width_all).reshape(owners, slot_count...]
    pallas_call x1, Pallas kernels: 0.56 us -> 1.26 us  [order_early(): pl.pallas_call(functools.partial(order_kernel, slot_count, exchange_bits(...]
  transfers between devices with their start and end apart: 6 -> 6, of which waited for: 6 -> 5; matrix products, arithmetic and copies ran while one was open for 0% -> 0% of each run, Pallas kernels for 4% -> 5%
where the time goes in v7:
time: 54.2 us; the launch traced here: 54 us
  waiting for transfers between devices  17.2 us (32%)
  blocking collectives  12.8 us (24%)
  starting transfers between devices  11.6 us (21%)
  Pallas kernels  11.5 us (21%)
  between operations  0.7 us (1%)
    ppermute x3, waiting for transfers between devices, spread_early(): lax.ppermute(block, 'clus', [(i, i ^ mask) for i in range(owners)])  13.6 us
    all_to_all x1, blocking collectives, per_device(): lax.all_to_all(message, 'clus', split_axis=0, concat_axis=0, tiled=True)  12.8 us
    pallas_call x1, Pallas kernels, embed_and_pack(): pl.pallas_call(functools.partial(embed_kernel, slot_count, exchange_bits(...  5.87 us
    ppermute x2, starting transfers between devices, spread_early(): lax.ppermute(leaving, 'clus', [(i, i ^ bit) for i in range(owners)])  4.17 us
    all_to_all x1, starting transfers between devices, per_device(): lax.all_to_all(pack(slot_row, unit, width_all).reshape(owners, slot_count...  3.91 us
    ppermute x2, waiting for transfers between devices, spread_early(): lax.ppermute(leaving, 'clus', [(i, i ^ bit) for i in range(owners)])  3.56 us
    ppermute x3, starting transfers between devices, spread_early(): lax.ppermute(block, 'clus', [(i, i ^ mask) for i in range(owners)])  3.55 us
    pallas_call x1, Pallas kernels, scores(): pl.pallas_call(functools.partial(score_kernel, slot_count, half), out_spe...  1.92 us
  transfers between devices with their start and end apart: 6, of which 5 were waited for; matrix products, arithmetic and copies ran while one was open for 0% of the time, Pallas kernels for 5%

profile of v7, /device:TPU:0, one launch (start us, length us, event | category | flops | bytes accessed | tf_op | source)
XLA Modules:
  0.0 54.0 jit_solution(9828850457962087103)
XLA Ops:
  0.6 5.9 %shard_map.67 = (bf16[320,256]{1,0:T(8,128)(2,1)S(1)}, bf16[320,256]{1,0:T(8,128)(2,1)S(1)}, s32[1,320]{1,0:T(1,128)S(1)}, bf16[320,768]{1,0:T(8,128)(2,1)S(1)}, s32[1,320]{1,0:T(1,128)S(1)}) custom-call(bf16[320,4096]{1,0:T(8,128)(2,1)} %tokens_hbm.1, bf16[4096,1024]{1,0:T(8,128)(2,1)} %weight_hbm.1, s32[1,320]{1,0:T(1,128)} %bitcast.27, s32[320]{0:T(512)} %valid_ref.1), custom_call_target="tpu_custom_call" | custom-call | flops 2684354560 | bytes 11010048 | tf_op jit(solution)/shard_map/pallas_call | solution.py:113
  6.5 4.1 %collective-permute-start = (bf16[1,8,40,256]{3,2,0,1:T(8,128)(2,1)S(1)}, bf16[1,8,40,256]{3,2,0,1:T(8,128)(2,1)S(1)}, u32[]{:S(2)}, u32[]{:S(2)}) collective-permute-start(bf16[1,8,40,256]{3,2,0,1:T(8,128)(2,1)S(1)} %bitcast.29), channel_id=1, source_target_pairs={{0,8},{1,9},{2,10},{3,11},{4,12},{5,13},{6,14},{7,15},{8,0},{9,1},... | collective-permute-start | bytes 491528 | tf_op jit(solution)/shard_map/ppermute | solution.py:166
  10.6 1.6 %shard_map.69 = bf16[640,768]{1,0:T(8,128)(2,1)} custom-call(s32[1,320]{1,0:T(1,128)S(1)} %get-tuple-element.14.slot_ref, bf16[320,768]{1,0:T(8,128)(2,1)S(1)} %get-tuple-element.15.unit_ref), custom_call_target="tpu_custom_call" | custom-call | flops 314572800 | bytes 983040 | tf_op jit(solution)/shard_map/pallas_call | solution.py:149
  12.2 3.9 %all-to-all-start = ((bf16[16,40,768]{2,1,0:T(8,128)(2,1)}), bf16[16,40,768]{2,1,0:T(8,128)(2,1)S(1)}, u32[]{:S(2)}, u32[]{:S(2)}) async-start(bf16[16,40,768]{2,1,0:T(8,128)(2,1)} %bitcast.10), calls=%async_computation | async-start | bytes 1966080 | tf_op jit(solution)/shard_map/all_to_all | solution.py:289
  16.1 2.2 %collective-permute-done = bf16[1,8,40,256]{3,2,0,1:T(8,128)(2,1)S(1)} collective-permute-done((bf16[1,8,40,256]{3,2,0,1:T(8,128)(2,1)S(1)}, bf16[1,8,40,256]{3,2,0,1:T(8,128)(2,1)S(1)}, u32[]{:S(2)}, u32[]{:S(2)}) %collective-permute-start) | collective-permute-done | bytes 163872 | tf_op jit(solution)/shard_map/ppermute | solution.py:166
  18.4 0.1 collective-permute-start.1
  18.4 1.4 %collective-permute-done.1 = bf16[2,4,40,256]{3,2,0,1:T(8,128)(2,1)S(1)} collective-permute-done((bf16[2,4,40,256]{3,2,0,1:T(8,128)(2,1)S(1)}, bf16[2,4,40,256]{3,2,0,1:T(8,128)(2,1)S(1)}, u32[]{:S(2)}, u32[]{:S(2)}) %collective-permute-start.1) | collective-permute-done | bytes 163872 | tf_op jit(solution)/shard_map/ppermute | solution.py:166
  19.9 1.6 %collective-permute-start.2 = (bf16[4,40,256]{2,1,0:T(8,128)(2,1)S(1)}, bf16[4,40,256]{2,1,0:T(8,128)(2,1)S(1)}, u32[]{:S(2)}, u32[]{:S(2)}) collective-permute-start(bf16[4,40,256]{2,1,0:T(8,128)(2,1)S(1)} %get-tuple-element.22), channel_id=1, source_target_pairs={{0,2},{1,3},{2,0},{3,1},{4,6},{5,7},{6,4},{7,5},{8,10},{9,11},{10,... | collective-permute-start | bytes 245768 | tf_op jit(solution)/shard_map/ppermute | solution.py:173
  21.5 0.7 %collective-permute-start.4 = (bf16[4,40,256]{2,1,0:T(8,128)(2,1)S(1)}, bf16[4,40,256]{2,1,0:T(8,128)(2,1)S(1)}, u32[]{:S(2)}, u32[]{:S(2)}) collective-permute-start(bf16[4,40,256]{2,1,0:T(8,128)(2,1)S(1)} %get-tuple-element.23), channel_id=1, source_target_pairs={{0,6},{1,7},{2,4},{3,5},{4,2},{5,3},{6,0},{7,1},{8,14},{9,15},{10,... | collective-permute-start | bytes 245768 | tf_op jit(solution)/shard_map/ppermute | solution.py:173
  22.2 1.2 %collective-permute-start.3 = (bf16[4,40,256]{2,1,0:T(8,128)(2,1)S(1)}, bf16[4,40,256]{2,1,0:T(8,128)(2,1)S(1)}, u32[]{:S(2)}, u32[]{:S(2)}) collective-permute-start(bf16[4,40,256]{2,1,0:T(8,128)(2,1)S(1)} %get-tuple-element.24), channel_id=1, source_target_pairs={{0,4},{1,5},{2,6},{3,7},{4,0},{5,1},{6,2},{7,3},{8,12},{9,13},{10,... | collective-permute-start | bytes 245768 | tf_op jit(solution)/shard_map/ppermute | solution.py:173
  23.4 3.8 %collective-permute-done.2 = bf16[4,40,256]{2,1,0:T(8,128)(2,1)S(1)} collective-permute-done((bf16[4,40,256]{2,1,0:T(8,128)(2,1)S(1)}, bf16[4,40,256]{2,1,0:T(8,128)(2,1)S(1)}, u32[]{:S(2)}, u32[]{:S(2)}) %collective-permute-start.2) | collective-permute-done | bytes 81952 | tf_op jit(solution)/shard_map/ppermute | solution.py:173
  27.2 8.2 %collective-permute-done.4 = bf16[4,40,256]{2,1,0:T(8,128)(2,1)S(1)} collective-permute-done((bf16[4,40,256]{2,1,0:T(8,128)(2,1)S(1)}, bf16[4,40,256]{2,1,0:T(8,128)(2,1)S(1)}, u32[]{:S(2)}, u32[]{:S(2)}) %collective-permute-start.4) | collective-permute-done | bytes 81952 | tf_op jit(solution)/shard_map/ppermute | solution.py:173
  35.4 1.6 %collective-permute-done.3 = bf16[4,40,256]{2,1,0:T(8,128)(2,1)S(1)} collective-permute-done((bf16[4,40,256]{2,1,0:T(8,128)(2,1)S(1)}, bf16[4,40,256]{2,1,0:T(8,128)(2,1)S(1)}, u32[]{:S(2)}, u32[]{:S(2)}) %collective-permute-start.3) | collective-permute-done | bytes 81952 | tf_op jit(solution)/shard_map/ppermute | solution.py:173
  37.1 1.3 %shard_map.68.early_ref = f32[640,640]{1,0:T(8,128)S(1)} custom-call(bf16[640,256]{1,0:T(8,128)(2,1)S(1)} %bitcast.23), custom_call_target="tpu_custom_call" | custom-call | flops 12999999488 | bytes 655360 | tf_op jit(solution)/shard_map/pallas_call | solution.py:193
  38.3 0.0 copy-start
  38.3 0.0 copy-start.1
  38.4 0.0 all-to-all-done
  38.4 1.9 %shard_map.70 = (f32[16,128]{1,0:T(8,128)S(1)}, f32[1,640,640]{2,1,0:T(8,128)}) custom-call(f32[640,640]{1,0:T(8,128)S(1)} %shard_map.68.early_ref, bf16[640,768]{1,0:T(8,128)(2,1)S(1)} %bitcast.22), custom_call_target="tpu_custom_call" | custom-call | tf_op jit(solution)/shard_map/pallas_call | solution.py:242
  40.3 12.8 %all_to_all.16 = f32[16,1,128]{2,1,0:T(1,128)S(1)} all-to-all(f32[16,1,128]{2,1,0:T(1,128)S(1)} %bitcast.26), channel_id=1, replica_groups=mesh['groups'=2,'clus'=16] {'clus'}, dimensions={0} | all-to-all | bytes 16384 | tf_op jit(solution)/shard_map/all_to_all | solution.py:294
  53.1 0.0 copy-done
  53.1 0.0 copy-done.1
  53.1 0.9 %shard_map.71 = (f32[320]{0:T(512)}, f32[320]{0:T(512)}) custom-call(f32[16,128]{1,0:T(8,128)S(1)} %bitcast.25, s32[1,320]{1,0:T(1,128)S(1)} %bitcast.28, s32[1,320]{1,0:T(1,128)S(1)} %get-tuple-element.18.rank_ref, s32[320]{0:T(512)S(1)} %copy-done), custom_call_target="tpu_custom_call" | custom-call | tf_op jit(solution)/shard_map/pallas_call | solution.py:271
  (3 shorter events, 0.1 us)
Async XLA Ops:
  6.5 11.8 %collective-permute-start = (bf16[1,8,40,256]{3,2,0,1:T(8,128)(2,1)S(1)}, bf16[1,8,40,256]{3,2,0,1:T(8,128)(2,1)S(1)}, u32[]{:S(2)}, u32[]{:S(2)}) collective-permute-start(bf16[1,8,40,256]{3,2,0,1:T(8,128)(2,1)S(1)} %bitcast.29), channel_id=1, source_target_pairs={{0,8},{1,9},{2,10},{3,11},{4,12},{5,13},{6,14},{7,15},{8,0},{9,1},... | collective-permute-start | bytes 491528 | tf_op jit(solution)/shard_map/ppermute | solution.py:166
  12.2 26.2 %all-to-all-start = ((bf16[16,40,768]{2,1,0:T(8,128)(2,1)}), bf16[16,40,768]{2,1,0:T(8,128)(2,1)S(1)}, u32[]{:S(2)}, u32[]{:S(2)}) async-start(bf16[16,40,768]{2,1,0:T(8,128)(2,1)} %bitcast.10), calls=%async_computation | async-start | bytes 1966080 | tf_op jit(solution)/shard_map/all_to_all | solution.py:289
  18.4 1.5 %collective-permute-start.1 = (bf16[2,4,40,256]{3,2,0,1:T(8,128)(2,1)S(1)}, bf16[2,4,40,256]{3,2,0,1:T(8,128)(2,1)S(1)}, u32[]{:S(2)}, u32[]{:S(2)}) collective-permute-start(bf16[2,4,40,256]{3,2,0,1:T(8,128)(2,1)S(1)} %get-tuple-element.26), channel_id=1, source_target_pairs={{0,1},{1,0},{2,3},{3,2},{4,5},{5,4},{6,7},{7,6},{8,9},{9,8},{10,11... | collective-permute-start | bytes 491528 | tf_op jit(solution)/shard_map/ppermute | solution.py:166
  19.9 7.4 %collective-permute-start.2 = (bf16[4,40,256]{2,1,0:T(8,128)(2,1)S(1)}, bf16[4,40,256]{2,1,0:T(8,128)(2,1)S(1)}, u32[]{:S(2)}, u32[]{:S(2)}) collective-permute-start(bf16[4,40,256]{2,1,0:T(8,128)(2,1)S(1)} %get-tuple-element.22), channel_id=1, source_target_pairs={{0,2},{1,3},{2,0},{3,1},{4,6},{5,7},{6,4},{7,5},{8,10},{9,11},{10,... | collective-permute-start | bytes 245768 | tf_op jit(solution)/shard_map/ppermute | solution.py:173
  21.5 14.0 %collective-permute-start.4 = (bf16[4,40,256]{2,1,0:T(8,128)(2,1)S(1)}, bf16[4,40,256]{2,1,0:T(8,128)(2,1)S(1)}, u32[]{:S(2)}, u32[]{:S(2)}) collective-permute-start(bf16[4,40,256]{2,1,0:T(8,128)(2,1)S(1)} %get-tuple-element.23), channel_id=1, source_target_pairs={{0,6},{1,7},{2,4},{3,5},{4,2},{5,3},{6,0},{7,1},{8,14},{9,15},{10,... | collective-permute-start | bytes 245768 | tf_op jit(solution)/shard_map/ppermute | solution.py:173
  22.2 14.8 %collective-permute-start.3 = (bf16[4,40,256]{2,1,0:T(8,128)(2,1)S(1)}, bf16[4,40,256]{2,1,0:T(8,128)(2,1)S(1)}, u32[]{:S(2)}, u32[]{:S(2)}) collective-permute-start(bf16[4,40,256]{2,1,0:T(8,128)(2,1)S(1)} %get-tuple-element.24), channel_id=1, source_target_pairs={{0,4},{1,5},{2,6},{3,7},{4,0},{5,1},{6,2},{7,3},{8,12},{9,13},{10,... | collective-permute-start | bytes 245768 | tf_op jit(solution)/shard_map/ppermute | solution.py:173
  38.3 14.7 %copy-start = (s32[320]{0:T(512)S(1)}, s32[320]{0:T(512)}, u32[]{:S(2)}) copy-start(s32[320]{0:T(512)} %valid_ref.1) | copy-start | bytes 3844
  38.3 14.7 %copy-start.1 = (s32[320,1]{0,1:T(1,128)S(1)}, s32[320,1]{0,1:T(1,128)}, u32[]{:S(2)}) copy-start(s32[320,1]{0,1:T(1,128)} %param.6) | copy-start | bytes 3844

commit v8 on v7

--- a/solution.py
+++ b/solution.py
@@ -13,6 +13,8 @@
 EMBED_VMEM_BYTES = 40 * 1024 * 1024
 PACK_VMEM_BYTES = 16 * 1024 * 1024
 FETCH_VMEM_BYTES = 8 * 1024 * 1024
+PARTS = 32
+EDGES = (0, 8, 18, 26, 32)
 EARLY = 2
 ORDER_FLOPS = 13 * 10**9
 
@@ -55,7 +57,8 @@
     tokens, weight, total, apart, label_ref, valid_ref, token_sem, weight_sem, small_sem,
 ):
     steps = token_sem.shape[0]
-    block = tokens.shape[1] // steps
+    depth = tokens.shape[1]
+    edges = [depth * part // PARTS for part in EDGES] if steps == len(EDGES) - 1 else [0, depth]
     early = keep_ref.shape[1]
     small = (
         pltpu.make_async_copy(label_hbm, label_ref, small_sem.at[0]),
@@ -65,7 +68,7 @@
         copy.start()
     copies = []
     for k in range(steps):
-        part = slice(k * block, (k + 1) * block)
+        part = slice(edges[k], edges[k + 1])
         copies.append((
             pltpu.make_async_copy(tokens_hbm.at[:, part], tokens.at[:, part], token_sem.at[k]),
             pltpu.make_async_copy(weight_hbm.at[part, :], weight.at[part, :], weight_sem.at[k]),
@@ -90,7 +93,7 @@
             copy.wait()
         for copy in (copies[k + 2] if k + 2 < steps else ()):
             copy.start()
-        part = slice(k * block, (k + 1) * block)
+        part = slice(edges[k], edges[k + 1])
         product = jnp.dot(tokens[:, part], weight[part, :], preferred_element_type=F32)
         if k == 0:
             total[...] = product
@@ -108,7 +111,7 @@
 def embed_and_pack(tokens, weight, label_row, valid, owners, slot_count, early):
     rows, depth = tokens.shape
     width = weight.shape[1]
-    steps = 4 if depth % 512 == 0 else 1
+    steps = len(EDGES) - 1 if depth % (128 * PARTS) == 0 else 1
     width_all = owners * slot_count
     return pl.pallas_call(
         functools.partial(embed_kernel, slot_count, exchange_bits(owners)),

time: 54.2 us -> 54 us (level)
  no operation moved by 1% of the time
where the time goes in v8:
time: 54 us; the launch traced here: 53.8 us
  waiting for transfers between devices  17.2 us (32%)
  blocking collectives  12.8 us (24%)
  starting transfers between devices  11.6 us (21%)
  Pallas kernels  11.4 us (21%)
  between operations  0.7 us (1%)
    ppermute x3, waiting for transfers between devices, spread_early(): lax.ppermute(block, 'clus', [(i, i ^ mask) for i in range(owners)])  13.6 us
    all_to_all x1, blocking collectives, per_device(): lax.all_to_all(message, 'clus', split_axis=0, concat_axis=0, tiled=True)  12.8 us
    pallas_call x1, Pallas kernels, embed_and_pack(): pl.pallas_call(functools.partial(embed_kernel, slot_count, exchange_bits(...  5.71 us
    ppermute x2, starting transfers between devices, spread_early(): lax.ppermute(leaving, 'clus', [(i, i ^ bit) for i in range(owners)])  4.17 us
    all_to_all x1, starting transfers between devices, per_device(): lax.all_to_all(pack(slot_row, unit, width_all).reshape(owners, slot_count...  3.91 us
    ppermute x2, waiting for transfers between devices, spread_early(): lax.ppermute(leaving, 'clus', [(i, i ^ bit) for i in range(owners)])  3.56 us
    ppermute x3, starting transfers between devices, spread_early(): lax.ppermute(block, 'clus', [(i, i ^ mask) for i in range(owners)])  3.55 us
    pallas_call x1, Pallas kernels, scores(): pl.pallas_call(functools.partial(score_kernel, slot_count, half), out_spe...  1.93 us
  transfers between devices with their start and end apart: 6, of which 5 were waited for; matrix products, arithmetic and copies ran while one was open for 0% of the time, Pallas kernels for 5%

profile of v8, /device:TPU:0, one launch (start us, length us, event | category | flops | bytes accessed | tf_op | source)
XLA Modules:
  0.0 53.8 jit_solution(13620294473462009576)
XLA Ops:
  0.6 5.7 %shard_map.67 = (bf16[320,256]{1,0:T(8,128)(2,1)S(1)}, bf16[320,256]{1,0:T(8,128)(2,1)S(1)}, s32[1,320]{1,0:T(1,128)S(1)}, bf16[320,768]{1,0:T(8,128)(2,1)S(1)}, s32[1,320]{1,0:T(1,128)S(1)}) custom-call(bf16[320,4096]{1,0:T(8,128)(2,1)} %tokens_hbm.1, bf16[4096,1024]{1,0:T(8,128)(2,1)} %weight_hbm.1, s32[1,320]{1,0:T(1,128)} %bitcast.27, s32[320]{0:T(512)} %valid_ref.1), custom_call_target="tpu_custom_call" | custom-call | flops 2684354560 | bytes 11010048 | tf_op jit(solution)/shard_map/pallas_call | solution.py:116
  6.3 4.1 %collective-permute-start = (bf16[1,8,40,256]{3,2,0,1:T(8,128)(2,1)S(1)}, bf16[1,8,40,256]{3,2,0,1:T(8,128)(2,1)S(1)}, u32[]{:S(2)}, u32[]{:S(2)}) collective-permute-start(bf16[1,8,40,256]{3,2,0,1:T(8,128)(2,1)S(1)} %bitcast.29), channel_id=1, source_target_pairs={{0,8},{1,9},{2,10},{3,11},{4,12},{5,13},{6,14},{7,15},{8,0},{9,1},... | collective-permute-start | bytes 491528 | tf_op jit(solution)/shard_map/ppermute | solution.py:169
  10.5 1.6 %shard_map.69 = bf16[640,768]{1,0:T(8,128)(2,1)} custom-call(s32[1,320]{1,0:T(1,128)S(1)} %get-tuple-element.14.slot_ref, bf16[320,768]{1,0:T(8,128)(2,1)S(1)} %get-tuple-element.15.unit_ref), custom_call_target="tpu_custom_call" | custom-call | flops 314572800 | bytes 983040 | tf_op jit(solution)/shard_map/pallas_call | solution.py:152
  12.1 3.9 %all-to-all-start = ((bf16[16,40,768]{2,1,0:T(8,128)(2,1)}), bf16[16,40,768]{2,1,0:T(8,128)(2,1)S(1)}, u32[]{:S(2)}, u32[]{:S(2)}) async-start(bf16[16,40,768]{2,1,0:T(8,128)(2,1)} %bitcast.10), calls=%async_computation | async-start | bytes 1966080 | tf_op jit(solution)/shard_map/all_to_all | solution.py:292
  16.0 2.2 %collective-permute-done = bf16[1,8,40,256]{3,2,0,1:T(8,128)(2,1)S(1)} collective-permute-done((bf16[1,8,40,256]{3,2,0,1:T(8,128)(2,1)S(1)}, bf16[1,8,40,256]{3,2,0,1:T(8,128)(2,1)S(1)}, u32[]{:S(2)}, u32[]{:S(2)}) %collective-permute-start) | collective-permute-done | bytes 163872 | tf_op jit(solution)/shard_map/ppermute | solution.py:169
  18.2 0.1 collective-permute-start.1
  18.3 1.4 %collective-permute-done.1 = bf16[2,4,40,256]{3,2,0,1:T(8,128)(2,1)S(1)} collective-permute-done((bf16[2,4,40,256]{3,2,0,1:T(8,128)(2,1)S(1)}, bf16[2,4,40,256]{3,2,0,1:T(8,128)(2,1)S(1)}, u32[]{:S(2)}, u32[]{:S(2)}) %collective-permute-start.1) | collective-permute-done | bytes 163872 | tf_op jit(solution)/shard_map/ppermute | solution.py:169
  19.7 1.6 %collective-permute-start.2 = (bf16[4,40,256]{2,1,0:T(8,128)(2,1)S(1)}, bf16[4,40,256]{2,1,0:T(8,128)(2,1)S(1)}, u32[]{:S(2)}, u32[]{:S(2)}) collective-permute-start(bf16[4,40,256]{2,1,0:T(8,128)(2,1)S(1)} %get-tuple-element.22), channel_id=1, source_target_pairs={{0,2},{1,3},{2,0},{3,1},{4,6},{5,7},{6,4},{7,5},{8,10},{9,11},{10,... | collective-permute-start | bytes 245768 | tf_op jit(solution)/shard_map/ppermute | solution.py:176
  21.3 0.7 %collective-permute-start.4 = (bf16[4,40,256]{2,1,0:T(8,128)(2,1)S(1)}, bf16[4,40,256]{2,1,0:T(8,128)(2,1)S(1)}, u32[]{:S(2)}, u32[]{:S(2)}) collective-permute-start(bf16[4,40,256]{2,1,0:T(8,128)(2,1)S(1)} %get-tuple-element.23), channel_id=1, source_target_pairs={{0,6},{1,7},{2,4},{3,5},{4,2},{5,3},{6,0},{7,1},{8,14},{9,15},{10,... | collective-permute-start | bytes 245768 | tf_op jit(solution)/shard_map/ppermute | solution.py:176
  22.0 1.2 %collective-permute-start.3 = (bf16[4,40,256]{2,1,0:T(8,128)(2,1)S(1)}, bf16[4,40,256]{2,1,0:T(8,128)(2,1)S(1)}, u32[]{:S(2)}, u32[]{:S(2)}) collective-permute-start(bf16[4,40,256]{2,1,0:T(8,128)(2,1)S(1)} %get-tuple-element.24), channel_id=1, source_target_pairs={{0,4},{1,5},{2,6},{3,7},{4,0},{5,1},{6,2},{7,3},{8,12},{9,13},{10,... | collective-permute-start | bytes 245768 | tf_op jit(solution)/shard_map/ppermute | solution.py:176
  23.2 3.8 %collective-permute-done.2 = bf16[4,40,256]{2,1,0:T(8,128)(2,1)S(1)} collective-permute-done((bf16[4,40,256]{2,1,0:T(8,128)(2,1)S(1)}, bf16[4,40,256]{2,1,0:T(8,128)(2,1)S(1)}, u32[]{:S(2)}, u32[]{:S(2)}) %collective-permute-start.2) | collective-permute-done | bytes 81952 | tf_op jit(solution)/shard_map/ppermute | solution.py:176
  27.1 8.2 %collective-permute-done.4 = bf16[4,40,256]{2,1,0:T(8,128)(2,1)S(1)} collective-permute-done((bf16[4,40,256]{2,1,0:T(8,128)(2,1)S(1)}, bf16[4,40,256]{2,1,0:T(8,128)(2,1)S(1)}, u32[]{:S(2)}, u32[]{:S(2)}) %collective-permute-start.4) | collective-permute-done | bytes 81952 | tf_op jit(solution)/shard_map/ppermute | solution.py:176
  35.3 1.6 %collective-permute-done.3 = bf16[4,40,256]{2,1,0:T(8,128)(2,1)S(1)} collective-permute-done((bf16[4,40,256]{2,1,0:T(8,128)(2,1)S(1)}, bf16[4,40,256]{2,1,0:T(8,128)(2,1)S(1)}, u32[]{:S(2)}, u32[]{:S(2)}) %collective-permute-start.3) | collective-permute-done | bytes 81952 | tf_op jit(solution)/shard_map/ppermute | solution.py:176
  36.9 1.3 %shard_map.68.early_ref = f32[640,640]{1,0:T(8,128)S(1)} custom-call(bf16[640,256]{1,0:T(8,128)(2,1)S(1)} %bitcast.23), custom_call_target="tpu_custom_call" | custom-call | flops 12999999488 | bytes 655360 | tf_op jit(solution)/shard_map/pallas_call | solution.py:196
  38.2 0.0 copy-start
  38.2 0.0 copy-start.1
  38.2 0.0 all-to-all-done
  38.2 1.9 %shard_map.70 = (f32[16,128]{1,0:T(8,128)S(1)}, f32[1,640,640]{2,1,0:T(8,128)}) custom-call(f32[640,640]{1,0:T(8,128)S(1)} %shard_map.68.early_ref, bf16[640,768]{1,0:T(8,128)(2,1)S(1)} %bitcast.22), custom_call_target="tpu_custom_call" | custom-call | tf_op jit(solution)/shard_map/pallas_call | solution.py:245
  40.2 12.8 %all_to_all.16 = f32[16,1,128]{2,1,0:T(1,128)S(1)} all-to-all(f32[16,1,128]{2,1,0:T(1,128)S(1)} %bitcast.26), channel_id=1, replica_groups=mesh['groups'=2,'clus'=16] {'clus'}, dimensions={0} | all-to-all | bytes 16384 | tf_op jit(solution)/shard_map/all_to_all | solution.py:297
  52.9 0.0 copy-done
  52.9 0.0 copy-done.1
  52.9 0.9 %shard_map.71 = (f32[320]{0:T(512)}, f32[320]{0:T(512)}) custom-call(f32[16,128]{1,0:T(8,128)S(1)} %bitcast.25, s32[1,320]{1,0:T(1,128)S(1)} %bitcast.28, s32[1,320]{1,0:T(1,128)S(1)} %get-tuple-element.18.rank_ref, s32[320]{0:T(512)S(1)} %copy-done), custom_call_target="tpu_custom_call" | custom-call | tf_op jit(solution)/shard_map/pallas_call | solution.py:274
  (3 shorter events, 0.1 us)
Async XLA Ops:
  6.3 11.8 %collective-permute-start = (bf16[1,8,40,256]{3,2,0,1:T(8,128)(2,1)S(1)}, bf16[1,8,40,256]{3,2,0,1:T(8,128)(2,1)S(1)}, u32[]{:S(2)}, u32[]{:S(2)}) collective-permute-start(bf16[1,8,40,256]{3,2,0,1:T(8,128)(2,1)S(1)} %bitcast.29), channel_id=1, source_target_pairs={{0,8},{1,9},{2,10},{3,11},{4,12},{5,13},{6,14},{7,15},{8,0},{9,1},... | collective-permute-start | bytes 491528 | tf_op jit(solution)/shard_map/ppermute | solution.py:169
  12.1 26.2 %all-to-all-start = ((bf16[16,40,768]{2,1,0:T(8,128)(2,1)}), bf16[16,40,768]{2,1,0:T(8,128)(2,1)S(1)}, u32[]{:S(2)}, u32[]{:S(2)}) async-start(bf16[16,40,768]{2,1,0:T(8,128)(2,1)} %bitcast.10), calls=%async_computation | async-start | bytes 1966080 | tf_op jit(solution)/shard_map/all_to_all | solution.py:292
  18.2 1.5 %collective-permute-start.1 = (bf16[2,4,40,256]{3,2,0,1:T(8,128)(2,1)S(1)}, bf16[2,4,40,256]{3,2,0,1:T(8,128)(2,1)S(1)}, u32[]{:S(2)}, u32[]{:S(2)}) collective-permute-start(bf16[2,4,40,256]{3,2,0,1:T(8,128)(2,1)S(1)} %get-tuple-element.26), channel_id=1, source_target_pairs={{0,1},{1,0},{2,3},{3,2},{4,5},{5,4},{6,7},{7,6},{8,9},{9,8},{10,11... | collective-permute-start | bytes 491528 | tf_op jit(solution)/shard_map/ppermute | solution.py:169
  19.7 7.4 %collective-permute-start.2 = (bf16[4,40,256]{2,1,0:T(8,128)(2,1)S(1)}, bf16[4,40,256]{2,1,0:T(8,128)(2,1)S(1)}, u32[]{:S(2)}, u32[]{:S(2)}) collective-permute-start(bf16[4,40,256]{2,1,0:T(8,128)(2,1)S(1)} %get-tuple-element.22), channel_id=1, source_target_pairs={{0,2},{1,3},{2,0},{3,1},{4,6},{5,7},{6,4},{7,5},{8,10},{9,11},{10,... | collective-permute-start | bytes 245768 | tf_op jit(solution)/shard_map/ppermute | solution.py:176
  21.3 14.0 %collective-permute-start.4 = (bf16[4,40,256]{2,1,0:T(8,128)(2,1)S(1)}, bf16[4,40,256]{2,1,0:T(8,128)(2,1)S(1)}, u32[]{:S(2)}, u32[]{:S(2)}) collective-permute-start(bf16[4,40,256]{2,1,0:T(8,128)(2,1)S(1)} %get-tuple-element.23), channel_id=1, source_target_pairs={{0,6},{1,7},{2,4},{3,5},{4,2},{5,3},{6,0},{7,1},{8,14},{9,15},{10,... | collective-permute-start | bytes 245768 | tf_op jit(solution)/shard_map/ppermute | solution.py:176
  22.0 14.8 %collective-permute-start.3 = (bf16[4,40,256]{2,1,0:T(8,128)(2,1)S(1)}, bf16[4,40,256]{2,1,0:T(8,128)(2,1)S(1)}, u32[]{:S(2)}, u32[]{:S(2)}) collective-permute-start(bf16[4,40,256]{2,1,0:T(8,128)(2,1)S(1)} %get-tuple-element.24), channel_id=1, source_target_pairs={{0,4},{1,5},{2,6},{3,7},{4,0},{5,1},{6,2},{7,3},{8,12},{9,13},{10,... | collective-permute-start | bytes 245768 | tf_op jit(solution)/shard_map/ppermute | solution.py:176
  38.2 14.7 %copy-start = (s32[320]{0:T(512)S(1)}, s32[320]{0:T(512)}, u32[]{:S(2)}) copy-start(s32[320]{0:T(512)} %valid_ref.1) | copy-start | bytes 3844
  38.2 14.7 %copy-start.1 = (s32[320,1]{0,1:T(1,128)S(1)}, s32[320,1]{0,1:T(1,128)}, u32[]{:S(2)}) copy-start(s32[320,1]{0,1:T(1,128)} %param.6) | copy-start | bytes 3844

commit v9 on v8

--- a/solution.py
+++ b/solution.py
@@ -53,8 +53,8 @@
 
 
 def embed_kernel(
-    slot_count, bits, tokens_hbm, weight_hbm, label_hbm, valid_hbm, keep_ref, send_ref, slot_ref, late_ref, rank_ref,
-    tokens, weight, total, apart, label_ref, valid_ref, token_sem, weight_sem, small_sem,
+    slot_count, bits, tokens_hbm, weight_hbm, label_hbm, valid_hbm, keep_ref, send_ref, slot_ref, total, scale_ref, rank_ref,
+    tokens, weight, apart, label_ref, valid_ref, token_sem, weight_sem, small_sem,
 ):
     steps = token_sem.shape[0]
     depth = tokens.shape[1]
@@ -105,7 +105,7 @@
     unit = (total[:, :early] * scale).astype(BF16)
     send_ref[...] = jnp.dot(apart[near:, :], unit, preferred_element_type=F32).astype(BF16)
     keep_ref[...] = jnp.dot(apart[:near, :], unit, preferred_element_type=F32).astype(BF16)
-    late_ref[...] = (total[:, early:] * scale).astype(BF16)
+    scale_ref[...] = scale
 
 
 def embed_and_pack(tokens, weight, label_row, valid, owners, slot_count, early):
@@ -120,13 +120,13 @@
             jax.ShapeDtypeStruct((width_all // 2, early), BF16),
             jax.ShapeDtypeStruct((width_all // 2, early), BF16),
             jax.ShapeDtypeStruct((1, rows), jnp.int32),
-            jax.ShapeDtypeStruct((rows, width - early), BF16),
+            jax.ShapeDtypeStruct((rows, width), F32),
+            jax.ShapeDtypeStruct((rows, 1), F32),
             jax.ShapeDtypeStruct((1, rows), jnp.int32),
         ),
         scratch_shapes=[
             pltpu.VMEM((rows, depth), BF16),
             pltpu.VMEM((depth, width), BF16),
-            pltpu.VMEM((rows, width), F32),
             pltpu.VMEM((width_all, rows), BF16),
             pltpu.VMEM((1, rows), jnp.int32),
             pltpu.VMEM((rows,), jnp.int32),
@@ -141,14 +141,17 @@
     )(*(pltpu.with_memory_space_constraint(x, pltpu.HBM) for x in (tokens, weight, label_row, valid)))
 
 
-def pack_kernel(slot_ref, unit_ref, packed_ref):
+def pack_kernel(slot_ref, total_ref, scale_ref, packed_ref):
+    early = total_ref.shape[1] - packed_ref.shape[1]
+    unit = (total_ref[:, early:] * scale_ref[...]).astype(BF16)
     slot = slot_ref[...]
     place = place_rows(slot, slot + 1, packed_ref.shape[0])
-    packed_ref[...] = jnp.dot(place, unit_ref[...], preferred_element_type=F32).astype(BF16)
-
-
-def pack(slot_row, unit, width_all):
-    rows, late = unit.shape
+    packed_ref[...] = jnp.dot(place, unit, preferred_element_type=F32).astype(BF16)
+
+
+def pack(slot_row, total, scale, width_all, early):
+    rows = total.shape[0]
+    late = total.shape[1] - early
     return pl.pallas_call(
         pack_kernel,
         out_shape=jax.ShapeDtypeStruct((width_all, late), BF16),
@@ -156,7 +159,7 @@
         cost_estimate=pl.CostEstimate(
             flops=2 * width_all * rows * late, bytes_accessed=2 * width_all * late, transcendentals=0
         ),
-    )(slot_row, unit)
+    )(slot_row, total, scale)
 
 
 def spread_early(keep, send, owners, slot_count):
@@ -286,11 +289,11 @@
     half = -(-slot_count // 64) * 64
     early = EARLY * proj_weight.shape[1] // 8
     label_row = labels.reshape(1, row_count)
-    keep, send, slot_row, unit, rank_row = embed_and_pack(
+    keep, send, slot_row, total, scale, rank_row = embed_and_pack(
         tokens, proj_weight, label_row, valid_rows, owners, slot_count, early
     )
     arrived = lax.all_to_all(
-        pack(slot_row, unit, width_all).reshape(owners, slot_count, -1), "clus", split_axis=0, concat_axis=0, tiled=True
+        pack(slot_row, total, scale, width_all, early).reshape(owners, slot_count, -1), "clus", split_axis=0, concat_axis=0, tiled=True
     )
     early_gram = order_early(spread_early(keep, send, owners, slot_count), owners, slot_count)
     message, similar = scores(early_gram, arrived.reshape(width_all, -1), owners, slot_count, half)

time: 54 us -> 53.9 us (level)
  transfers between devices with their start and end apart: 6 -> 6, of which waited for: 5 -> 5; matrix products, arithmetic and copies ran while one was open for 0% -> 0% of each run, Pallas kernels for 5% -> 6%
where the time goes in v9:
time: 53.9 us; the launch traced here: 53.7 us
  waiting for transfers between devices  17.2 us (32%)
  blocking collectives  12.6 us (23%)
  starting transfers between devices  11.6 us (22%)
  Pallas kernels  11.5 us (21%)
  between operations  0.7 us (1%)
    ppermute x3, waiting for transfers between devices, spread_early(): lax.ppermute(block, 'clus', [(i, i ^ mask) for i in range(owners)])  13.7 us
    all_to_all x1, blocking collectives, per_device(): lax.all_to_all(message, 'clus', split_axis=0, concat_axis=0, tiled=True)  12.6 us
    pallas_call x1, Pallas kernels, embed_and_pack(): pl.pallas_call(functools.partial(embed_kernel, slot_count, exchange_bits(...  5.71 us
    ppermute x2, starting transfers between devices, spread_early(): lax.ppermute(leaving, 'clus', [(i, i ^ bit) for i in range(owners)])  4.17 us
    all_to_all x1, starting transfers between devices, per_device(): lax.all_to_all(pack(slot_row, total, scale, width_all, early).reshape(own...  3.91 us
    ppermute x3, starting transfers between devices, spread_early(): lax.ppermute(block, 'clus', [(i, i ^ mask) for i in range(owners)])  3.55 us
    ppermute x2, waiting for transfers between devices, spread_early(): lax.ppermute(leaving, 'clus', [(i, i ^ bit) for i in range(owners)])  3.47 us
    pallas_call x1, Pallas kernels, scores(): pl.pallas_call(functools.partial(score_kernel, slot_count, half), out_spe...  1.92 us
  transfers between devices with their start and end apart: 6, of which 5 were waited for; matrix products, arithmetic and copies ran while one was open for 0% of the time, Pallas kernels for 6%

profile of v9, /device:TPU:0, one launch (start us, length us, event | category | flops | bytes accessed | tf_op | source)
XLA Modules:
  0.0 53.7 jit_solution(16194307858151252065)
XLA Ops:
  0.6 5.7 %shard_map.67 = (bf16[320,256]{1,0:T(8,128)(2,1)S(1)}, bf16[320,256]{1,0:T(8,128)(2,1)S(1)}, s32[1,320]{1,0:T(1,128)S(1)}, f32[320,1024]{1,0:T(8,128)S(1)}, f32[320,1]{1,0:T(8,128)S(1)}, /*index=5*/s32[1,320]{1,0:T(1,128)S(1)}) custom-call(bf16[320,4096]{1,0:T(8,128)(2,1)} %tokens_hbm.1, bf16[4096,1024]{1,0:T(8,128)(2,1)} %weight_hbm.1, s32[1,320]{1,0:T(1,128)} %bitcast.27, ...), custom_call_target="tpu_custom_call" | custom-call | flops 2684354560 | bytes 11010048 | tf_op jit(solution)/shard_map/pallas_call | solution.py:116
  6.3 4.1 %collective-permute-start = (bf16[1,8,40,256]{3,2,0,1:T(8,128)(2,1)S(1)}, bf16[1,8,40,256]{3,2,0,1:T(8,128)(2,1)S(1)}, u32[]{:S(2)}, u32[]{:S(2)}) collective-permute-start(bf16[1,8,40,256]{3,2,0,1:T(8,128)(2,1)S(1)} %bitcast.29), channel_id=1, source_target_pairs={{0,8},{1,9},{2,10},{3,11},{4,12},{5,13},{6,14},{7,15},{8,0},{9,1},... | collective-permute-start | bytes 491528 | tf_op jit(solution)/shard_map/ppermute | solution.py:172
  10.4 1.7 %shard_map.69 = bf16[640,768]{1,0:T(8,128)(2,1)} custom-call(s32[1,320]{1,0:T(1,128)S(1)} %get-tuple-element.15.slot_ref, f32[320,1024]{1,0:T(8,128)S(1)} %get-tuple-element.16.total_ref, f32[320,1]{1,0:T(8,128)S(1)} %get-tuple-element.17.scale_ref), custom_call_target="tpu_custom_call" | custom-call | flops 314572800 | bytes 983040 | tf_op jit(solution)/shard_map/pallas_call | solution.py:155
  12.2 3.9 %all-to-all-start = ((bf16[16,40,768]{2,1,0:T(8,128)(2,1)}), bf16[16,40,768]{2,1,0:T(8,128)(2,1)S(1)}, u32[]{:S(2)}, u32[]{:S(2)}) async-start(bf16[16,40,768]{2,1,0:T(8,128)(2,1)} %bitcast.10), calls=%async_computation | async-start | bytes 1966080 | tf_op jit(solution)/shard_map/all_to_all | solution.py:295
  16.1 2.1 %collective-permute-done = bf16[1,8,40,256]{3,2,0,1:T(8,128)(2,1)S(1)} collective-permute-done((bf16[1,8,40,256]{3,2,0,1:T(8,128)(2,1)S(1)}, bf16[1,8,40,256]{3,2,0,1:T(8,128)(2,1)S(1)}, u32[]{:S(2)}, u32[]{:S(2)}) %collective-permute-start) | collective-permute-done | bytes 163872 | tf_op jit(solution)/shard_map/ppermute | solution.py:172
  18.2 0.1 collective-permute-start.1
  18.3 1.4 %collective-permute-done.1 = bf16[2,4,40,256]{3,2,0,1:T(8,128)(2,1)S(1)} collective-permute-done((bf16[2,4,40,256]{3,2,0,1:T(8,128)(2,1)S(1)}, bf16[2,4,40,256]{3,2,0,1:T(8,128)(2,1)S(1)}, u32[]{:S(2)}, u32[]{:S(2)}) %collective-permute-start.1) | collective-permute-done | bytes 163872 | tf_op jit(solution)/shard_map/ppermute | solution.py:172
  19.7 1.6 %collective-permute-start.2 = (bf16[4,40,256]{2,1,0:T(8,128)(2,1)S(1)}, bf16[4,40,256]{2,1,0:T(8,128)(2,1)S(1)}, u32[]{:S(2)}, u32[]{:S(2)}) collective-permute-start(bf16[4,40,256]{2,1,0:T(8,128)(2,1)S(1)} %get-tuple-element.24), channel_id=1, source_target_pairs={{0,2},{1,3},{2,0},{3,1},{4,6},{5,7},{6,4},{7,5},{8,10},{9,11},{10,... | collective-permute-start | bytes 245768 | tf_op jit(solution)/shard_map/ppermute | solution.py:179
  21.3 0.7 %collective-permute-start.4 = (bf16[4,40,256]{2,1,0:T(8,128)(2,1)S(1)}, bf16[4,40,256]{2,1,0:T(8,128)(2,1)S(1)}, u32[]{:S(2)}, u32[]{:S(2)}) collective-permute-start(bf16[4,40,256]{2,1,0:T(8,128)(2,1)S(1)} %get-tuple-element.25), channel_id=1, source_target_pairs={{0,6},{1,7},{2,4},{3,5},{4,2},{5,3},{6,0},{7,1},{8,14},{9,15},{10,... | collective-permute-start | bytes 245768 | tf_op jit(solution)/shard_map/ppermute | solution.py:179
  22.0 1.2 %collective-permute-start.3 = (bf16[4,40,256]{2,1,0:T(8,128)(2,1)S(1)}, bf16[4,40,256]{2,1,0:T(8,128)(2,1)S(1)}, u32[]{:S(2)}, u32[]{:S(2)}) collective-permute-start(bf16[4,40,256]{2,1,0:T(8,128)(2,1)S(1)} %get-tuple-element.26), channel_id=1, source_target_pairs={{0,4},{1,5},{2,6},{3,7},{4,0},{5,1},{6,2},{7,3},{8,12},{9,13},{10,... | collective-permute-start | bytes 245768 | tf_op jit(solution)/shard_map/ppermute | solution.py:179
  23.2 3.9 %collective-permute-done.2 = bf16[4,40,256]{2,1,0:T(8,128)(2,1)S(1)} collective-permute-done((bf16[4,40,256]{2,1,0:T(8,128)(2,1)S(1)}, bf16[4,40,256]{2,1,0:T(8,128)(2,1)S(1)}, u32[]{:S(2)}, u32[]{:S(2)}) %collective-permute-start.2) | collective-permute-done | bytes 81952 | tf_op jit(solution)/shard_map/ppermute | solution.py:179
  27.2 8.2 %collective-permute-done.4 = bf16[4,40,256]{2,1,0:T(8,128)(2,1)S(1)} collective-permute-done((bf16[4,40,256]{2,1,0:T(8,128)(2,1)S(1)}, bf16[4,40,256]{2,1,0:T(8,128)(2,1)S(1)}, u32[]{:S(2)}, u32[]{:S(2)}) %collective-permute-start.4) | collective-permute-done | bytes 81952 | tf_op jit(solution)/shard_map/ppermute | solution.py:179
  35.4 1.6 %collective-permute-done.3 = bf16[4,40,256]{2,1,0:T(8,128)(2,1)S(1)} collective-permute-done((bf16[4,40,256]{2,1,0:T(8,128)(2,1)S(1)}, bf16[4,40,256]{2,1,0:T(8,128)(2,1)S(1)}, u32[]{:S(2)}, u32[]{:S(2)}) %collective-permute-start.3) | collective-permute-done | bytes 81952 | tf_op jit(solution)/shard_map/ppermute | solution.py:179
  37.0 1.3 %shard_map.68.early_ref = f32[640,640]{1,0:T(8,128)S(1)} custom-call(bf16[640,256]{1,0:T(8,128)(2,1)S(1)} %bitcast.23), custom_call_target="tpu_custom_call" | custom-call | flops 12999999488 | bytes 655360 | tf_op jit(solution)/shard_map/pallas_call | solution.py:199
  38.3 0.0 copy-start
  38.3 0.0 copy-start.1
  38.3 0.0 all-to-all-done
  38.3 1.9 %shard_map.70 = (f32[16,128]{1,0:T(8,128)S(1)}, f32[1,640,640]{2,1,0:T(8,128)}) custom-call(f32[640,640]{1,0:T(8,128)S(1)} %shard_map.68.early_ref, bf16[640,768]{1,0:T(8,128)(2,1)S(1)} %bitcast.22), custom_call_target="tpu_custom_call" | custom-call | tf_op jit(solution)/shard_map/pallas_call | solution.py:248
  40.2 12.6 %all_to_all.16 = f32[16,1,128]{2,1,0:T(1,128)S(1)} all-to-all(f32[16,1,128]{2,1,0:T(1,128)S(1)} %bitcast.26), channel_id=1, replica_groups=mesh['groups'=2,'clus'=16] {'clus'}, dimensions={0} | all-to-all | bytes 16384 | tf_op jit(solution)/shard_map/all_to_all | solution.py:300
  52.8 0.0 copy-done
  52.8 0.0 copy-done.1
  52.8 0.9 %shard_map.71 = (f32[320]{0:T(512)}, f32[320]{0:T(512)}) custom-call(f32[16,128]{1,0:T(8,128)S(1)} %bitcast.25, s32[1,320]{1,0:T(1,128)S(1)} %bitcast.28, s32[1,320]{1,0:T(1,128)S(1)} %get-tuple-element.20.rank_ref, s32[320]{0:T(512)S(1)} %copy-done), custom_call_target="tpu_custom_call" | custom-call | tf_op jit(solution)/shard_map/pallas_call | solution.py:277
  (3 shorter events, 0.1 us)
Async XLA Ops:
  6.3 11.8 %collective-permute-start = (bf16[1,8,40,256]{3,2,0,1:T(8,128)(2,1)S(1)}, bf16[1,8,40,256]{3,2,0,1:T(8,128)(2,1)S(1)}, u32[]{:S(2)}, u32[]{:S(2)}) collective-permute-start(bf16[1,8,40,256]{3,2,0,1:T(8,128)(2,1)S(1)} %bitcast.29), channel_id=1, source_target_pairs={{0,8},{1,9},{2,10},{3,11},{4,12},{5,13},{6,14},{7,15},{8,0},{9,1},... | collective-permute-start | bytes 491528 | tf_op jit(solution)/shard_map/ppermute | solution.py:172
  12.2 26.2 %all-to-all-start = ((bf16[16,40,768]{2,1,0:T(8,128)(2,1)}), bf16[16,40,768]{2,1,0:T(8,128)(2,1)S(1)}, u32[]{:S(2)}, u32[]{:S(2)}) async-start(bf16[16,40,768]{2,1,0:T(8,128)(2,1)} %bitcast.10), calls=%async_computation | async-start | bytes 1966080 | tf_op jit(solution)/shard_map/all_to_all | solution.py:295
  18.2 1.5 %collective-permute-start.1 = (bf16[2,4,40,256]{3,2,0,1:T(8,128)(2,1)S(1)}, bf16[2,4,40,256]{3,2,0,1:T(8,128)(2,1)S(1)}, u32[]{:S(2)}, u32[]{:S(2)}) collective-permute-start(bf16[2,4,40,256]{3,2,0,1:T(8,128)(2,1)S(1)} %get-tuple-element.28), channel_id=1, source_target_pairs={{0,1},{1,0},{2,3},{3,2},{4,5},{5,4},{6,7},{7,6},{8,9},{9,8},{10,11... | collective-permute-start | bytes 491528 | tf_op jit(solution)/shard_map/ppermute | solution.py:172
  19.7 7.5 %collective-permute-start.2 = (bf16[4,40,256]{2,1,0:T(8,128)(2,1)S(1)}, bf16[4,40,256]{2,1,0:T(8,128)(2,1)S(1)}, u32[]{:S(2)}, u32[]{:S(2)}) collective-permute-start(bf16[4,40,256]{2,1,0:T(8,128)(2,1)S(1)} %get-tuple-element.24), channel_id=1, source_target_pairs={{0,2},{1,3},{2,0},{3,1},{4,6},{5,7},{6,4},{7,5},{8,10},{9,11},{10,... | collective-permute-start | bytes 245768 | tf_op jit(solution)/shard_map/ppermute | solution.py:179
  21.3 14.1 %collective-permute-start.4 = (bf16[4,40,256]{2,1,0:T(8,128)(2,1)S(1)}, bf16[4,40,256]{2,1,0:T(8,128)(2,1)S(1)}, u32[]{:S(2)}, u32[]{:S(2)}) collective-permute-start(bf16[4,40,256]{2,1,0:T(8,128)(2,1)S(1)} %get-tuple-element.25), channel_id=1, source_target_pairs={{0,6},{1,7},{2,4},{3,5},{4,2},{5,3},{6,0},{7,1},{8,14},{9,15},{10,... | collective-permute-start | bytes 245768 | tf_op jit(solution)/shard_map/ppermute | solution.py:179
  22.0 14.9 %collective-permute-start.3 = (bf16[4,40,256]{2,1,0:T(8,128)(2,1)S(1)}, bf16[4,40,256]{2,1,0:T(8,128)(2,1)S(1)}, u32[]{:S(2)}, u32[]{:S(2)}) collective-permute-start(bf16[4,40,256]{2,1,0:T(8,128)(2,1)S(1)} %get-tuple-element.26), channel_id=1, source_target_pairs={{0,4},{1,5},{2,6},{3,7},{4,0},{5,1},{6,2},{7,3},{8,12},{9,13},{10,... | collective-permute-start | bytes 245768 | tf_op jit(solution)/shard_map/ppermute | solution.py:179
  38.3 14.6 %copy-start = (s32[320]{0:T(512)S(1)}, s32[320]{0:T(512)}, u32[]{:S(2)}) copy-start(s32[320]{0:T(512)} %valid_ref.1) | copy-start | bytes 3844
  38.3 14.5 %copy-start.1 = (s32[320,1]{0,1:T(1,128)S(1)}, s32[320,1]{0,1:T(1,128)}, u32[]{:S(2)}) copy-start(s32[320,1]{0,1:T(1,128)} %param.6) | copy-start | bytes 3844
